TPU v7x, 32 devices: a whole 2x2x4 slice. The times are simulated.
32 devices in a mesh: section: 2 (over x), dp: 4 (over y, core), mp: 4 (over z).
Axes of the slice: x: 2, y: 2, z: 4, core: 2. Of those that a mesh axis runs over, the one named last changes fastest.
Arguments:
- boundary: float32 [2, 3, 4, 1370, 1024], P('section', None, 'dp', None, 'mp'), may hold values from -6 to 6
- ln1_gain: float32 [2, 1024], P('section', 'mp'), may hold values from 0.5 to 1.5
- ln1_bias: float32 [2, 1024], P('section', 'mp'), may hold values from -4 to 4
- w_query: bfloat16 [2, 1024, 1024], P('section', 'dp', 'mp'), may hold values from -0.1875 to 0.1875
- w_key: bfloat16 [2, 1024, 1024], P('section', 'dp', 'mp'), may hold values from -0.1875 to 0.1875
- w_value: bfloat16 [2, 1024, 1024], P('section', 'dp', 'mp'), may hold values from -0.1875 to 0.1875
- b_query: float32 [2, 1024], P('section', 'mp'), may hold values from -6 to 6
- b_value: float32 [2, 1024], P('section', 'mp'), may hold values from -6 to 6
- w_out: bfloat16 [2, 1024, 1024], P('section', 'mp', 'dp'), may hold values from -2 to 2
- b_out: float32 [2, 1024], P('section', 'mp'), may hold values from -4 to 4
- scale_attn: float32 [2, 1024], P('section', 'mp'), may hold values from 0.5 to 1.5
- ln2_gain: float32 [2, 1024], P('section', 'mp'), may hold values from 0.5 to 1.5
- ln2_bias: float32 [2, 1024], P('section', 'mp'), may hold values from -4 to 4
- w_fc1: bfloat16 [2, 1024, 4096], P('section', 'dp', 'mp'), may hold values from -0.1875 to 0.1875
- b_fc1: float32 [2, 4096], P('section', 'mp'), may hold values from -6 to 6
- w_fc2: bfloat16 [2, 4096, 1024], P('section', 'mp', 'dp'), may hold values from -0.09375 to 0.09375
- b_fc2: float32 [2, 1024], P('section', 'mp'), may hold values from -4 to 4
- scale_mlp: float32 [2, 1024], P('section', 'mp'), may hold values from 0.5 to 1.5
Outputs:
- ends_out: float32 [2, 3, 4, 1370, 1024], P('section', None, 'dp', None, 'mp')
- grad_ln1_gain: float32 [2, 1024], P('section', ('mp', 'dp'))
- grad_ln1_bias: float32 [2, 1024], P('section', ('mp', 'dp'))
- grad_w_query: float32 [2, 1024, 1024], P('section', 'dp', 'mp')
- grad_w_key: float32 [2, 1024, 1024], P('section', 'dp', 'mp')
- grad_w_value: float32 [2, 1024, 1024], P('section', 'dp', 'mp')
- grad_b_query: float32 [2, 1024], P('section', ('mp', 'dp'))
- grad_b_value: float32 [2, 1024], P('section', ('mp', 'dp'))
- grad_w_out: float32 [2, 1024, 1024], P('section', 'mp', 'dp')
- grad_b_out: float32 [2, 1024], P('section', ('mp', 'dp'))
- grad_scale_attn: float32 [2, 1024], P('section', ('mp', 'dp'))
- grad_ln2_gain: float32 [2, 1024], P('section', ('mp', 'dp'))
- grad_ln2_bias: float32 [2, 1024], P('section', ('mp', 'dp'))
- grad_w_fc1: float32 [2, 1024, 4096], P('section', 'dp', 'mp')
- grad_b_fc1: float32 [2, 4096], P('section', ('mp', 'dp'))
- grad_w_fc2: float32 [2, 4096, 1024], P('section', 'mp', 'dp')
- grad_b_fc2: float32 [2, 1024], P('section', ('mp', 'dp'))
- grad_scale_mlp: float32 [2, 1024], P('section', ('mp', 'dp'))
All inputs are finite; a program needn't handle non-finite values.
Results may differ from a plain program's by a relative error of at most 0.02.
Values may be sent and summed in bfloat16 or wider, within the bound.
A program may use at most 384 MiB of HBM per device.

v0:
```python
import jax
import jax.numpy as jnp
from jax import lax
from jax.sharding import PartitionSpec as P

HD = 64
QBLOCKS = 2


epsilon = 1e-06
inv_root_two = 0.7071067811865476
inv_root_tau = 0.3989422804014327


def shifted(value, axis, steps):
    count = lax.axis_size(axis)
    leading, last = (max(0, -steps), min(count, count - steps))
    return lax.ppermute(value, axis, [(source, source + steps) for source in range(leading, last)])


def product(left, right):
    return jnp.dot(left, right, preferred_element_type=jnp.float32)


def normalize(rows_in, gain, shift_vec):
    sums = lax.psum((jnp.sum(rows_in, 1), jnp.sum(rows_in * rows_in, 1)), "mp")
    width = rows_in.shape[1] * lax.axis_size("mp")
    row_mean = sums[0] / width
    row_var = sums[1] / width - row_mean * row_mean
    inv_std = lax.rsqrt(row_var + epsilon)
    normed = (rows_in - row_mean[:, None]) * inv_std[:, None]
    whole_rows = lax.all_gather(
        (normed * gain + shift_vec).astype(jnp.bfloat16), "mp", axis=1, tiled=True
    )
    return (normed, inv_std, whole_rows)


def norm_back(grad_rows, normed, inv_std, gain):
    weighted = grad_rows * gain
    sums = lax.psum((jnp.sum(weighted, 1), jnp.sum(weighted * normed, 1)), "mp")
    width = grad_rows.shape[1] * lax.axis_size("mp")
    return inv_std[:, None] * (
        weighted - sums[0][:, None] / width - normed * sums[1][:, None] / width
    )


def branch_total(partial_value):
    return lax.psum_scatter(
        partial_value.astype(jnp.bfloat16), "mp", scatter_dimension=1, tiled=True
    ).astype(jnp.float32)


def branch_spread(grad_low):
    return lax.all_gather(grad_low, "mp", axis=1, tiled=True)


def input_total(partial_value):
    return lax.psum_scatter(
        partial_value.astype(jnp.bfloat16), "mp", scatter_dimension=1, tiled=True
    ).astype(jnp.float32)


def attend(queries, keys, values, images):
    heads_here = queries.shape[1] // HD
    seq_len = queries.shape[0] // images
    span = seq_len // QBLOCKS
    scale = HD ** (-0.5)
    keys_four = keys.reshape(images, seq_len, heads_here, HD)
    values_four = values.reshape(images, seq_len, heads_here, HD)
    blocks = jnp.moveaxis(queries.reshape(images, QBLOCKS, span, heads_here, HD), 1, 0)

    def one_block(part):
        scores = (
            jnp.einsum("ibhd,ikhd->ihbk", part, keys_four, preferred_element_type=jnp.float32)
            * scale
        )
        top_score = jnp.max(scores, -1, keepdims=True)
        expo = jnp.exp(scores - top_score)
        total = jnp.sum(expo, -1, keepdims=True)
        probs = (expo / total).astype(jnp.bfloat16)
        result = jnp.einsum(
            "ihbk,ikhd->ibhd", probs, values_four, preferred_element_type=jnp.float32
        )
        return (result.astype(jnp.bfloat16), top_score[..., 0] + jnp.log(total[..., 0]))

    results, log_sums = lax.map(one_block, blocks)
    return (jnp.moveaxis(results, 0, 1).reshape(queries.shape), log_sums)


def attend_back(queries, keys, values, grad_out, log_sums, images):
    heads_here = queries.shape[1] // HD
    seq_len = queries.shape[0] // images
    span = seq_len // QBLOCKS
    scale = HD ** (-0.5)
    shape_four = (images, seq_len, heads_here, HD)
    keys_four = keys.reshape(shape_four)
    values_four = values.reshape(shape_four)
    query_blocks = jnp.moveaxis(queries.reshape(images, QBLOCKS, span, heads_here, HD), 1, 0)
    grad_blocks = jnp.moveaxis(grad_out.reshape(images, QBLOCKS, span, heads_here, HD), 1, 0)

    def one_block(carry, pieces):
        part, grad_part, level = pieces
        scores = (
            jnp.einsum("ibhd,ikhd->ihbk", part, keys_four, preferred_element_type=jnp.float32)
            * scale
        )
        probs = jnp.exp(scores - level[..., None])
        probs_low = probs.astype(jnp.bfloat16)
        grad_values = carry[1] + jnp.einsum(
            "ihbk,ibhd->ikhd", probs_low, grad_part, preferred_element_type=jnp.float32
        )
        grad_probs = jnp.einsum(
            "ibhd,ikhd->ihbk", grad_part, values_four, preferred_element_type=jnp.float32
        )
        row_dot = jnp.sum(probs * grad_probs, -1, keepdims=True)
        grad_scores = (probs * (grad_probs - row_dot)).astype(jnp.bfloat16)
        grad_query = (
            jnp.einsum(
                "ihbk,ikhd->ibhd", grad_scores, keys_four, preferred_element_type=jnp.float32
            )
            * scale
        )
        grad_keys = (
            carry[0]
            + jnp.einsum("ihbk,ibhd->ikhd", grad_scores, part, preferred_element_type=jnp.float32)
            * scale
        )
        return ((grad_keys, grad_values), grad_query)

    start = (jnp.zeros(shape_four, jnp.float32), jnp.zeros(shape_four, jnp.float32))
    (grad_keys, grad_values), grad_queries = lax.scan(
        one_block, start, (query_blocks, grad_blocks, log_sums)
    )
    grad_queries = jnp.moveaxis(grad_queries, 0, 1).reshape(queries.shape).astype(jnp.bfloat16)
    return (
        grad_queries,
        grad_keys.reshape(queries.shape).astype(jnp.bfloat16),
        grad_values.reshape(queries.shape).astype(jnp.bfloat16),
    )


def layer_forward(rows_in, vectors, matrices, images):
    (
        ln1_gain,
        ln1_bias,
        b_query,
        b_value,
        b_out,
        scale_attn,
        ln2_gain,
        ln2_bias,
        b_fc1,
        b_fc2,
        scale_mlp,
    ) = vectors
    w_query, w_key, w_value, w_out, w_fc1, w_fc2 = matrices
    normed_one, inv_std_one, whole_one = normalize(rows_in, ln1_gain, ln1_bias)
    queries = (product(whole_one, w_query) + b_query).astype(jnp.bfloat16)
    keys = product(whole_one, w_key).astype(jnp.bfloat16)
    values = (product(whole_one, w_value) + b_value).astype(jnp.bfloat16)
    attended, log_sums = attend(queries, keys, values, images)
    branch = branch_total(product(attended, w_out)) + b_out
    middle = rows_in + scale_attn * branch
    normed_two, inv_std_two, whole_two = normalize(middle, ln2_gain, ln2_bias)
    hidden = product(whole_two, w_fc1) + b_fc1
    active = jax.nn.gelu(hidden, approximate=False).astype(jnp.bfloat16)
    branch_two = branch_total(product(active, w_fc2)) + b_fc2
    leaving = middle + scale_mlp * branch_two
    saved_state = (
        normed_one,
        inv_std_one,
        whole_one,
        queries,
        keys,
        values,
        attended,
        log_sums,
        branch,
        normed_two,
        inv_std_two,
        whole_two,
        hidden,
        branch_two,
    )
    return (leaving, saved_state)


def layer_backward(grad_rows, saved_state, vectors, matrices, images):
    (
        ln1_gain,
        ln1_bias,
        b_query,
        b_value,
        b_out,
        scale_attn,
        ln2_gain,
        ln2_bias,
        b_fc1,
        b_fc2,
        scale_mlp,
    ) = vectors
    w_query, w_key, w_value, w_out, w_fc1, w_fc2 = matrices
    (
        normed_one,
        inv_std_one,
        whole_one,
        queries,
        keys,
        values,
        attended,
        log_sums,
        branch,
        normed_two,
        inv_std_two,
        whole_two,
        hidden,
        branch_two,
    ) = saved_state
    grad_scale_mlp = jnp.sum(grad_rows * branch_two, 0)
    grad_mlp_low = (grad_rows * scale_mlp).astype(jnp.bfloat16)
    grad_b_fc2 = jnp.sum(grad_mlp_low.astype(jnp.float32), 0)
    grad_mlp_whole = branch_spread(grad_mlp_low)
    active = jax.nn.gelu(hidden, approximate=False).astype(jnp.bfloat16)
    grad_w_fc2 = jnp.einsum("rf,rd->fd", active, grad_mlp_whole, preferred_element_type=jnp.float32)
    grad_active = jnp.einsum("rd,fd->rf", grad_mlp_whole, w_fc2, preferred_element_type=jnp.float32)
    cdf_part = 0.5 * lax.erfc(-hidden * inv_root_two)
    pdf_part = jnp.exp(-0.5 * hidden * hidden) * inv_root_tau
    grad_hidden = (grad_active * (cdf_part + hidden * pdf_part)).astype(jnp.bfloat16)
    grad_b_fc1 = jnp.sum(grad_hidden.astype(jnp.float32), 0)
    grad_w_fc1 = jnp.einsum("rd,rf->df", whole_two, grad_hidden, preferred_element_type=jnp.float32)
    grad_normed_two = input_total(
        jnp.einsum("rf,df->rd", grad_hidden, w_fc1, preferred_element_type=jnp.float32)
    )
    grad_ln2_gain = jnp.sum(grad_normed_two * normed_two, 0)
    grad_ln2_bias = jnp.sum(grad_normed_two, 0)
    grad_middle = grad_rows + norm_back(grad_normed_two, normed_two, inv_std_two, ln2_gain)
    grad_scale_attn = jnp.sum(grad_middle * branch, 0)
    grad_attn_low = (grad_middle * scale_attn).astype(jnp.bfloat16)
    grad_b_out = jnp.sum(grad_attn_low.astype(jnp.float32), 0)
    grad_attn_whole = branch_spread(grad_attn_low)
    grad_w_out = jnp.einsum(
        "rc,rd->cd", attended, grad_attn_whole, preferred_element_type=jnp.float32
    )
    grad_attended = jnp.einsum(
        "rd,cd->rc", grad_attn_whole, w_out, preferred_element_type=jnp.float32
    ).astype(jnp.bfloat16)
    grad_queries, grad_keys, grad_values = attend_back(
        queries, keys, values, grad_attended, log_sums, images
    )
    grad_b_query = jnp.sum(grad_queries.astype(jnp.float32), 0)
    grad_b_value = jnp.sum(grad_values.astype(jnp.float32), 0)
    grad_w_query = jnp.einsum(
        "rd,rc->dc", whole_one, grad_queries, preferred_element_type=jnp.float32
    )
    grad_w_key = jnp.einsum("rd,rc->dc", whole_one, grad_keys, preferred_element_type=jnp.float32)
    grad_w_value = jnp.einsum(
        "rd,rc->dc", whole_one, grad_values, preferred_element_type=jnp.float32
    )
    partial_value = jnp.einsum(
        "rc,dc->rd", grad_queries, w_query, preferred_element_type=jnp.float32
    )
    partial_value = partial_value + jnp.einsum(
        "rc,dc->rd", grad_keys, w_key, preferred_element_type=jnp.float32
    )
    partial_value = partial_value + jnp.einsum(
        "rc,dc->rd", grad_values, w_value, preferred_element_type=jnp.float32
    )
    grad_normed_one = input_total(partial_value)
    grad_ln1_gain = jnp.sum(grad_normed_one * normed_one, 0)
    grad_ln1_bias = jnp.sum(grad_normed_one, 0)
    grad_input = grad_middle + norm_back(grad_normed_one, normed_one, inv_std_one, ln1_gain)
    grads = (
        grad_ln1_gain,
        grad_ln1_bias,
        grad_w_query,
        grad_w_key,
        grad_w_value,
        grad_b_query,
        grad_b_value,
        grad_w_out,
        grad_b_out,
        grad_scale_attn,
        grad_ln2_gain,
        grad_ln2_bias,
        grad_w_fc1,
        grad_b_fc1,
        grad_w_fc2,
        grad_b_fc2,
        grad_scale_mlp,
    )
    return (grad_input, grads)


def local(
    boundary,
    ln1_gain,
    ln1_bias,
    w_query,
    w_key,
    w_value,
    b_query,
    b_value,
    w_out,
    b_out,
    scale_attn,
    ln2_gain,
    ln2_bias,
    w_fc1,
    b_fc1,
    w_fc2,
    b_fc2,
    scale_mlp,
):
    is_first = lax.axis_index("section") == 0
    boundary_slice = boundary[0]
    micro_count = boundary_slice.shape[0]
    images = boundary_slice.shape[1]
    seq_len = boundary_slice.shape[2]
    local_width = boundary_slice.shape[3]
    row_count = images * seq_len
    vectors = (
        ln1_gain[0],
        ln1_bias[0],
        b_query[0],
        b_value[0],
        b_out[0],
        scale_attn[0],
        ln2_gain[0],
        ln2_bias[0],
        b_fc1[0],
        b_fc2[0],
        scale_mlp[0],
    )
    matrix_shards = (w_query[0], w_key[0], w_value[0], w_out[0], w_fc1[0], w_fc2[0])

    def weights_now():
        return (
            lax.all_gather(matrix_shards[0], "dp", axis=0, tiled=True),
            lax.all_gather(matrix_shards[1], "dp", axis=0, tiled=True),
            lax.all_gather(matrix_shards[2], "dp", axis=0, tiled=True),
            lax.all_gather(matrix_shards[3], "dp", axis=1, tiled=True),
            lax.all_gather(matrix_shards[4], "dp", axis=0, tiled=True),
            lax.all_gather(matrix_shards[5], "dp", axis=1, tiled=True),
        )

    empty_rows = jnp.zeros((row_count, local_width), jnp.float32)
    received = empty_rows
    saved_all = []
    leaving_all = []
    for moment in range(micro_count + 1):
        own_rows = (
            boundary_slice[moment].reshape(row_count, local_width)
            if moment < micro_count
            else empty_rows
        )
        entering = jnp.where(is_first, own_rows, received)
        leaving, saved_state = layer_forward(entering, vectors, weights_now(), images)
        saved_all.append(saved_state)
        leaving_all.append(leaving)
        if moment < micro_count:
            received = shifted(leaving.astype(jnp.bfloat16), "section", 1).astype(jnp.float32)
    back_received = empty_rows
    totals = None
    grads_in_all = []
    for moment in range(micro_count + 1):
        own_cot = (
            boundary_slice[moment].reshape(row_count, local_width)
            if moment < micro_count
            else empty_rows
        )
        arriving = jnp.where(is_first, back_received, own_cot)
        early_state = saved_all[max(moment - 1, 0)]
        late_state = saved_all[min(moment + 1, micro_count)]
        saved_state = jax.tree.map(lambda a, b: jnp.where(is_first, a, b), early_state, late_state)
        grad_input, grads = layer_backward(arriving, saved_state, vectors, weights_now(), images)
        totals = grads if totals is None else tuple((t + g for t, g in zip(totals, grads)))
        grads_in_all.append(grad_input)
        if moment < micro_count:
            back_received = shifted(grad_input.astype(jnp.bfloat16), "section", -1).astype(
                jnp.float32
            )
    ends_block = jnp.where(is_first, jnp.stack(grads_in_all[1:]), jnp.stack(leaving_all[1:]))
    ends_out = ends_block.reshape(1, micro_count, images, seq_len, local_width)
    reduced = (
        lax.psum_scatter(
            totals[0].astype(jnp.bfloat16), "dp", scatter_dimension=0, tiled=True
        ).astype(jnp.float32),
        lax.psum_scatter(
            totals[1].astype(jnp.bfloat16), "dp", scatter_dimension=0, tiled=True
        ).astype(jnp.float32),
        lax.psum_scatter(
            totals[2].astype(jnp.bfloat16), "dp", scatter_dimension=0, tiled=True
        ).astype(jnp.float32),
        lax.psum_scatter(
            totals[3].astype(jnp.bfloat16), "dp", scatter_dimension=0, tiled=True
        ).astype(jnp.float32),
        lax.psum_scatter(
            totals[4].astype(jnp.bfloat16), "dp", scatter_dimension=0, tiled=True
        ).astype(jnp.float32),
        lax.psum_scatter(
            totals[5].astype(jnp.bfloat16), "dp", scatter_dimension=0, tiled=True
        ).astype(jnp.float32),
        lax.psum_scatter(
            totals[6].astype(jnp.bfloat16), "dp", scatter_dimension=0, tiled=True
        ).astype(jnp.float32),
        lax.psum_scatter(
            totals[7].astype(jnp.bfloat16), "dp", scatter_dimension=1, tiled=True
        ).astype(jnp.float32),
        lax.psum_scatter(
            totals[8].astype(jnp.bfloat16), "dp", scatter_dimension=0, tiled=True
        ).astype(jnp.float32),
        lax.psum_scatter(
            totals[9].astype(jnp.bfloat16), "dp", scatter_dimension=0, tiled=True
        ).astype(jnp.float32),
        lax.psum_scatter(
            totals[10].astype(jnp.bfloat16), "dp", scatter_dimension=0, tiled=True
        ).astype(jnp.float32),
        lax.psum_scatter(
            totals[11].astype(jnp.bfloat16), "dp", scatter_dimension=0, tiled=True
        ).astype(jnp.float32),
        lax.psum_scatter(
            totals[12].astype(jnp.bfloat16), "dp", scatter_dimension=0, tiled=True
        ).astype(jnp.float32),
        lax.psum_scatter(
            totals[13].astype(jnp.bfloat16), "dp", scatter_dimension=0, tiled=True
        ).astype(jnp.float32),
        lax.psum_scatter(
            totals[14].astype(jnp.bfloat16), "dp", scatter_dimension=1, tiled=True
        ).astype(jnp.float32),
        lax.psum_scatter(
            totals[15].astype(jnp.bfloat16), "dp", scatter_dimension=0, tiled=True
        ).astype(jnp.float32),
        lax.psum_scatter(
            totals[16].astype(jnp.bfloat16), "dp", scatter_dimension=0, tiled=True
        ).astype(jnp.float32),
    )
    return (
        ends_out,
        reduced[0][None],
        reduced[1][None],
        reduced[2][None],
        reduced[3][None],
        reduced[4][None],
        reduced[5][None],
        reduced[6][None],
        reduced[7][None],
        reduced[8][None],
        reduced[9][None],
        reduced[10][None],
        reduced[11][None],
        reduced[12][None],
        reduced[13][None],
        reduced[14][None],
        reduced[15][None],
        reduced[16][None],
    )


def solution(mesh):
    return jax.shard_map(
        local,
        mesh=mesh,
        in_specs=(
            P("section", None, "dp", None, "mp"),
            P("section", "mp"),
            P("section", "mp"),
            P("section", "dp", "mp"),
            P("section", "dp", "mp"),
            P("section", "dp", "mp"),
            P("section", "mp"),
            P("section", "mp"),
            P("section", "mp", "dp"),
            P("section", "mp"),
            P("section", "mp"),
            P("section", "mp"),
            P("section", "mp"),
            P("section", "dp", "mp"),
            P("section", "mp"),
            P("section", "mp", "dp"),
            P("section", "mp"),
            P("section", "mp"),
        ),
        out_specs=(
            P("section", None, "dp", None, "mp"),
            P("section", ("mp", "dp")),
            P("section", ("mp", "dp")),
            P("section", "dp", "mp"),
            P("section", "dp", "mp"),
            P("section", "dp", "mp"),
            P("section", ("mp", "dp")),
            P("section", ("mp", "dp")),
            P("section", "mp", "dp"),
            P("section", ("mp", "dp")),
            P("section", ("mp", "dp")),
            P("section", ("mp", "dp")),
            P("section", ("mp", "dp")),
            P("section", "dp", "mp"),
            P("section", ("mp", "dp")),
            P("section", "mp", "dp"),
            P("section", ("mp", "dp")),
            P("section", ("mp", "dp")),
        ),
        check_vma=False,
    )
```

profile of v0, /device:TPU:26, one launch (start us, length us, event | category | flops | bytes accessed | tf_op | source)
XLA Modules:
  0.0 2856.6 jit_solution(8563936288044306229)
XLA Ops:
  14.6 15.3 all-reduce.22
  61.7 27.2 all-gather.25.cloned.1.call-done
  103.6 19.2 while.108
  127.4 54.5 %reduce-scatter.23.cloned.1.call-done = bf16[1370,256]{1,0:T(8,128)(2,1)} async-done(((bf16[1370,1024]{1,0:T(8,128)(2,1)}), bf16[1370,256]{1,0:T(8,128)(2,1)}) %reduce-scatter.23.cloned.1.call-update) | async-done | bytes 701456 | tf_op jit(solution)/shard_map/reduce_scatter | solution.py:48
  185.0 15.1 all-reduce.21
  202.9 56.0 %all-gather.27.cloned.1.call-done = bf16[1370,1024]{1,0:T(8,128)(2,1)} async-done(((bf16[1370,256]{1,0:T(8,128)(2,1)}), bf16[1370,1024]{1,0:T(8,128)(2,1)}) %all-gather.27.cloned.1.call-update) | async-done | bytes 2805776 | tf_op jit(solution)/shard_map/all_gather | solution.py:32
  267.0 17.1 all-gather.59.cloned.1.call-done
  284.2 17.3 convolution_convert_fusion.11
  301.6 54.1 %reduce-scatter.25.cloned.1.call-done = bf16[1370,256]{1,0:T(8,128)(2,1)} async-done(((bf16[1370,1024]{1,0:T(8,128)(2,1)}), bf16[1370,256]{1,0:T(8,128)(2,1)}) %reduce-scatter.25.cloned.1.call-update) | async-done | bytes 701456 | tf_op jit(solution)/shard_map/reduce_scatter | solution.py:48
  358.4 18.2 collective-permute-done
  378.4 15.2 all-reduce.20
  396.0 56.4 %all-gather.29.cloned.1.call-done = bf16[1370,1024]{1,0:T(8,128)(2,1)} async-done(((bf16[1370,256]{1,0:T(8,128)(2,1)}), bf16[1370,1024]{1,0:T(8,128)(2,1)}) %all-gather.29.cloned.1.call-update) | async-done | bytes 2805776 | tf_op jit(solution)/shard_map/all_gather | solution.py:32
  469.6 19.2 while.109
  492.8 54.9 %reduce-scatter.27.cloned.1.call-done = bf16[1370,256]{1,0:T(8,128)(2,1)} async-done(((bf16[1370,1024]{1,0:T(8,128)(2,1)}), bf16[1370,256]{1,0:T(8,128)(2,1)}) %reduce-scatter.27.cloned.1.call-update) | async-done | bytes 701456 | tf_op jit(solution)/shard_map/reduce_scatter | solution.py:48
  549.4 15.4 all-reduce.19
  566.8 56.5 %all-gather.33.cloned.1.call-done = bf16[1370,1024]{1,0:T(8,128)(2,1)} async-done(((bf16[1370,256]{1,0:T(8,128)(2,1)}), bf16[1370,1024]{1,0:T(8,128)(2,1)}) %all-gather.33.cloned.1.call-update) | async-done | bytes 2805776 | tf_op jit(solution)/shard_map/all_gather | solution.py:32
  623.3 19.5 fusion.175
  645.3 15.3 convolution_convert_fusion.9
  661.0 26.5 all-gather.31.cloned.1.call-done
  702.5 25.8 reduce-scatter.33.cloned.1.call-done
  728.2 57.1 %reduce-scatter.29.cloned.1.call-done = bf16[1370,256]{1,0:T(8,128)(2,1)} async-done(((bf16[1370,1024]{1,0:T(8,128)(2,1)}), bf16[1370,256]{1,0:T(8,128)(2,1)}) %reduce-scatter.29.cloned.1.call-update) | async-done | bytes 701456 | tf_op jit(solution)/shard_map/reduce_scatter | solution.py:58
  791.6 18.1 collective-permute-done.2
  810.9 16.0 all-reduce.18
  841.6 46.4 %all-gather.35.cloned.1.call-done = bf16[1370,1024]{1,0:T(8,128)(2,1)} async-done(((bf16[1370,256]{1,0:T(8,128)(2,1)}), bf16[1370,1024]{1,0:T(8,128)(2,1)}) %all-gather.35.cloned.1.call-update) | async-done | bytes 2805776 | tf_op jit(solution)/shard_map/all_gather | solution.py:54
  898.3 65.9 %while.112 = (s32[]{:T(128)}, f32[1,1370,4,64]{1,3,2,0:T(8,128)}, f32[1,1370,4,64]{1,3,2,0:T(8,128)S(1)}, bf16[2,1,685,4,64]{2,4,3,1,0:T(8,128)(2,1)}, bf16[2,1,...) while((s32[]{:T(128)}, f32[1,1370,4,64]{1,3,2,0:T(8,128)}, ...), condition=%wide.region_34.35_spmd.clone, body=%wide.region_32.34_spmd.clone.sunk | while | flops 2449403904 | bytes 176487248 | solution.py:131
  974.1 55.0 %reduce-scatter.31.cloned.1.call-done = bf16[1370,256]{1,0:T(8,128)(2,1)} async-done(((bf16[1370,1024]{1,0:T(8,128)(2,1)}), bf16[1370,256]{1,0:T(8,128)(2,1)}) %reduce-scatter.31.cloned.1.call-update) | async-done | bytes 701456 | tf_op jit(solution)/shard_map/reduce_scatter | solution.py:58
  1033.9 56.1 %all-gather.37.cloned.1.call-done = bf16[1370,1024]{1,0:T(8,128)(2,1)} async-done(((bf16[1370,256]{1,0:T(8,128)(2,1)}), bf16[1370,1024]{1,0:T(8,128)(2,1)}) %all-gather.37.cloned.1.call-update) | async-done | bytes 2805776 | tf_op jit(solution)/shard_map/all_gather | solution.py:32
  1106.1 19.2 while.110
  1129.3 55.1 %reduce-scatter.35.cloned.1.call-done = bf16[1370,256]{1,0:T(8,128)(2,1)} async-done(((bf16[1370,1024]{1,0:T(8,128)(2,1)}), bf16[1370,256]{1,0:T(8,128)(2,1)}) %reduce-scatter.35.cloned.1.call-update) | async-done | bytes 701456 | tf_op jit(solution)/shard_map/reduce_scatter | solution.py:48
  1186.6 17.0 all-reduce.17
  1213.1 11.4 collective-permute-done.1
  1226.2 37.5 %all-gather.41.cloned.1.call-done = bf16[1370,1024]{1,0:T(8,128)(2,1)} async-done(((bf16[1370,256]{1,0:T(8,128)(2,1)}), bf16[1370,1024]{1,0:T(8,128)(2,1)}) %all-gather.41.cloned.1.call-update) | async-done | bytes 2805776 | tf_op jit(solution)/shard_map/all_gather | solution.py:32
  1263.8 19.7 fusion.185
  1285.9 16.8 convolution_convert_fusion.7
  1303.2 24.3 all-gather.39.cloned.1.call-done
  1344.6 23.8 reduce-scatter.41.cloned.1.call-done
  1368.4 57.2 %reduce-scatter.37.cloned.1.call-done = bf16[1370,256]{1,0:T(8,128)(2,1)} async-done(((bf16[1370,1024]{1,0:T(8,128)(2,1)}), bf16[1370,256]{1,0:T(8,128)(2,1)}) %reduce-scatter.37.cloned.1.call-update) | async-done | bytes 701456 | tf_op jit(solution)/shard_map/reduce_scatter | solution.py:58
  1431.1 18.2 collective-permute-done.4
  1449.7 16.0 all-reduce.16
  1468.0 56.6 %all-gather.45.cloned.1.call-done = bf16[1370,1024]{1,0:T(8,128)(2,1)} async-done(((bf16[1370,256]{1,0:T(8,128)(2,1)}), bf16[1370,1024]{1,0:T(8,128)(2,1)}) %all-gather.45.cloned.1.call-update) | async-done | bytes 2805776 | tf_op jit(solution)/shard_map/all_gather | solution.py:32
  1544.1 19.2 while.111
  1567.4 54.9 %reduce-scatter.43.cloned.1.call-done = bf16[1370,256]{1,0:T(8,128)(2,1)} async-done(((bf16[1370,1024]{1,0:T(8,128)(2,1)}), bf16[1370,256]{1,0:T(8,128)(2,1)}) %reduce-scatter.43.cloned.1.call-update) | async-done | bytes 701456 | tf_op jit(solution)/shard_map/reduce_scatter | solution.py:48
  1636.8 46.8 %all-gather.43.cloned.1.call-done = bf16[1370,1024]{1,0:T(8,128)(2,1)} async-done(((bf16[1370,256]{1,0:T(8,128)(2,1)}), bf16[1370,1024]{1,0:T(8,128)(2,1)}) %all-gather.43.cloned.1.call-update) | async-done | bytes 2805776 | tf_op jit(solution)/shard_map/all_gather | solution.py:54
  1691.5 66.2 %while.113 = (s32[]{:T(128)}, f32[1,1370,4,64]{1,3,2,0:T(8,128)}, f32[1,1370,4,64]{1,3,2,0:T(8,128)S(1)}, bf16[2,1,685,4,64]{2,4,3,1,0:T(8,128)(2,1)}, bf16[2,1,...) while((s32[]{:T(128)}, f32[1,1370,4,64]{1,3,2,0:T(8,128)}, ...), condition=%wide.region_61.62_spmd.clone, body=%wide.region_59.61_spmd.clone.sunk | while | flops 2449403904 | bytes 176487248 | solution.py:131
  1767.5 54.9 %reduce-scatter.39.cloned.1.call-done = bf16[1370,256]{1,0:T(8,128)(2,1)} async-done(((bf16[1370,1024]{1,0:T(8,128)(2,1)}), bf16[1370,256]{1,0:T(8,128)(2,1)}) %reduce-scatter.39.cloned.1.call-update) | async-done | bytes 701456 | tf_op jit(solution)/shard_map/reduce_scatter | solution.py:58
  1826.1 16.3 all-reduce.15
  1865.7 37.6 %all-gather.49.cloned.1.call-done = bf16[1370,1024]{1,0:T(8,128)(2,1)} async-done(((bf16[1370,256]{1,0:T(8,128)(2,1)}), bf16[1370,1024]{1,0:T(8,128)(2,1)}) %all-gather.49.cloned.1.call-update) | async-done | bytes 2805776 | tf_op jit(solution)/shard_map/all_gather | solution.py:32
  1903.3 31.9 %fusion.202 = (f32[1370,1024]{1,0:T(8,128)}, f32[1370,1024]{1,0:T(8,128)}, f32[1370,1024]{1,0:T(8,128)}, f32[1370,1024]{1,0:T(8,128)}, f32[1370,1024]{1,0:T(8,128)S(1)}) fusion(f32[1370,1024]{1,0:T(8,128)} %copy-done.345, f32[1024]{0:T(1024)S(1)} %bitcast.918, pred[]{:T(512)S(6)} %eq.3, f32[1370,1024]{1,0:T(8,128)} %copy-done.344, ...), kind=kOutput, calls=%fused_computation.234 | convolution fusion | flops 3054069760 | bytes 44187648 | tf_op jit(solution)/shard_map/dot_general | solution.py:22
  1935.3 15.3 convolution_convert_fusion.4
  1977.1 31.4 %reduce-scatter.53.cloned.1.call-done = bf16[1370,256]{1,0:T(8,128)(2,1)} async-done(((bf16[1370,1024]{1,0:T(8,128)(2,1)}), bf16[1370,256]{1,0:T(8,128)(2,1)}) %reduce-scatter.53.cloned.1.call-update) | async-done | bytes 701456 | tf_op jit(solution)/shard_map/reduce_scatter | solution.py:48
  2008.4 57.8 %reduce-scatter.45.cloned.1.call-done = bf16[1370,256]{1,0:T(8,128)(2,1)} async-done(((bf16[1370,1024]{1,0:T(8,128)(2,1)}), bf16[1370,256]{1,0:T(8,128)(2,1)}) %reduce-scatter.45.cloned.1.call-update) | async-done | bytes 701456 | tf_op jit(solution)/shard_map/reduce_scatter | solution.py:58
  2071.1 15.8 all-reduce.14
  2100.9 47.9 %all-gather.51.cloned.1.call-done = bf16[1370,1024]{1,0:T(8,128)(2,1)} async-done(((bf16[1370,256]{1,0:T(8,128)(2,1)}), bf16[1370,1024]{1,0:T(8,128)(2,1)}) %all-gather.51.cloned.1.call-update) | async-done | bytes 2805776 | tf_op jit(solution)/shard_map/all_gather | solution.py:54
  2156.7 65.9 %while.114 = (s32[]{:T(128)}, f32[1,1370,4,64]{1,3,2,0:T(8,128)}, f32[1,1370,4,64]{1,3,2,0:T(8,128)S(1)}, bf16[2,1,685,4,64]{2,4,3,1,0:T(8,128)(2,1)}, bf16[2,1,...) while((s32[]{:T(128)}, f32[1,1370,4,64]{1,3,2,0:T(8,128)}, ...), condition=%wide.region_88.89_spmd.clone, body=%wide.region_86.88_spmd.clone.sunk | while | flops 2449403904 | bytes 176487248 | solution.py:131
  2232.5 55.0 %reduce-scatter.47.cloned.1.call-done = bf16[1370,256]{1,0:T(8,128)(2,1)} async-done(((bf16[1370,1024]{1,0:T(8,128)(2,1)}), bf16[1370,256]{1,0:T(8,128)(2,1)}) %reduce-scatter.47.cloned.1.call-update) | async-done | bytes 701456 | tf_op jit(solution)/shard_map/reduce_scatter | solution.py:58
  2291.2 15.9 all-reduce.13
  2313.3 11.7 collective-permute-done.5
  2329.9 57.4 %all-gather.53.cloned.1.call-done = bf16[1370,1024]{1,0:T(8,128)(2,1)} async-done(((bf16[1370,256]{1,0:T(8,128)(2,1)}), bf16[1370,1024]{1,0:T(8,128)(2,1)}) %all-gather.53.cloned.1.call-update) | async-done | bytes 2805776 | tf_op jit(solution)/shard_map/all_gather | solution.py:54
  2404.2 55.1 %reduce-scatter.49.cloned.1.call-done = bf16[1370,256]{1,0:T(8,128)(2,1)} async-done(((bf16[1370,1024]{1,0:T(8,128)(2,1)}), bf16[1370,256]{1,0:T(8,128)(2,1)}) %reduce-scatter.49.cloned.1.call-update) | async-done | bytes 701456 | tf_op jit(solution)/shard_map/reduce_scatter | solution.py:58
  2463.0 15.1 all-reduce.12
  2597.6 66.3 %while.115 = (s32[]{:T(128)}, f32[1,1370,4,64]{1,3,2,0:T(8,128)}, f32[1,1370,4,64]{1,3,2,0:T(8,128)S(1)}, bf16[2,1,685,4,64]{2,4,3,1,0:T(8,128)(2,1)}, bf16[2,1,...) while((s32[]{:T(128)}, f32[1,1370,4,64]{1,3,2,0:T(8,128)}, ...), condition=%wide.region_101.102_spmd.clone, body=%wide.region_99.101_spmd.clone.sunk | while | flops 2449403904 | bytes 176487248 | solution.py:131
  2720.6 22.3 reduce-scatter.57.cloned.1.call-done
  2744.6 55.3 %reduce-scatter.51.cloned.1.call-done = bf16[1370,256]{1,0:T(8,128)(2,1)} async-done(((bf16[1370,1024]{1,0:T(8,128)(2,1)}), bf16[1370,256]{1,0:T(8,128)(2,1)}) %reduce-scatter.51.cloned.1.call-update) | async-done | bytes 701456 | tf_op jit(solution)/shard_map/reduce_scatter | solution.py:58
  2816.6 15.8 all-reduce.11
  (1200 shorter events, 956.7 us)
Async XLA Ops:
  8.0 81.0 %all-gather.25.cloned.1.call-start = ((), (), s32[]{:S(2)}) async-start(), calls=%async_computation.22 | async-start | bytes 3522560 | tf_op jit(solution)/shard_map/all_gather | solution.py:32
  31.8 150.0 %reduce-scatter.23.cloned.1.call-start = ((), (), s32[]{:S(2)}) async-start(), calls=%async_computation.23 | async-start | bytes 3522560 | tf_op jit(solution)/shard_map/reduce_scatter | solution.py:48
  126.8 76.2 %all-gather.57.cloned.1.call-start = ((), (), s32[]{:S(2)}) async-start(), calls=%async_computation.60 | async-start | bytes 2621440 | tf_op jit(solution)/shard_map/all_gather | solution.py:342
  127.3 131.6 %all-gather.27.cloned.1.call-start = ((), (), s32[]{:S(2)}) async-start(), calls=%async_computation.24 | async-start | bytes 3522560 | tf_op jit(solution)/shard_map/all_gather | solution.py:32
  185.0 170.7 %copy-start.36 = (f32[1370,256]{1,0:T(8,128)}, f32[1370,256]{1,0:T(8,128)S(1)}, u32[]{:S(2)}) copy-start(f32[1370,256]{1,0:T(8,128)S(1)} %get-tuple-element.1032) | copy-start | bytes 4208644
  202.1 82.1 %all-gather.59.cloned.1.call-start = ((), (), s32[]{:S(2)}) async-start(), calls=%async_computation.61 | async-start | bytes 2621440 | tf_op jit(solution)/shard_map/all_gather | solution.py:343
  202.6 153.0 %reduce-scatter.25.cloned.1.call-start = ((), (), s32[]{:S(2)}) async-start(), calls=%async_computation.25 | async-start | bytes 3522560 | tf_op jit(solution)/shard_map/reduce_scatter | solution.py:48
  301.5 150.8 %all-gather.29.cloned.1.call-start = ((), (), s32[]{:S(2)}) async-start(), calls=%async_computation.26 | async-start | bytes 3522560 | tf_op jit(solution)/shard_map/all_gather | solution.py:32
  357.1 19.5 collective-permute-start
  395.5 152.3 %reduce-scatter.27.cloned.1.call-start = ((), (), s32[]{:S(2)}) async-start(), calls=%async_computation.27 | async-start | bytes 3522560 | tf_op jit(solution)/shard_map/reduce_scatter | solution.py:48
  488.8 352.8 %copy-start.180 = (f32[2,1,4,685]{3,2,1,0:T(4,128)}, f32[2,1,4,685]{3,2,1,0:T(4,128)S(1)}, u32[]{:S(2)}) copy-start(f32[2,1,4,685]{3,2,1,0:T(4,128)S(1)} %get-tuple-element.349) | copy-start | bytes 65764
  492.8 130.5 %copy-start.325 = (f32[1,1024]{1,0:T(1,128)S(1)}, f32[1,1024]{1,0:T(1,128)}, u32[]{:S(2)}) copy-start(f32[1,1024]{1,0:T(1,128)} %param.48) | copy-start | bytes 12292
  492.8 130.5 %all-gather.33.cloned.1.call-start = ((), (), s32[]{:S(2)}) async-start(), calls=%async_computation.29 | async-start | bytes 3522560 | tf_op jit(solution)/shard_map/all_gather | solution.py:32
  564.8 220.5 %copy-start.227 = (f32[1370]{0:T(1024)}, f32[1370]{0:T(1024)S(1)}, u32[]{:S(2)}) copy-start(f32[1370]{0:T(1024)S(1)} %get-tuple-element.1059) | copy-start | bytes 16444
  564.8 220.5 %copy-start.229 = (f32[1370]{0:T(1024)}, f32[1370]{0:T(1024)S(1)}, u32[]{:S(2)}) copy-start(f32[1370]{0:T(1024)S(1)} %get-tuple-element.1064) | copy-start | bytes 16444
  566.2 121.2 %all-gather.31.cloned.1.call-start = ((), (), s32[]{:S(2)}) async-start(), calls=%async_computation.28 | async-start | bytes 3522560 | tf_op jit(solution)/shard_map/all_gather | solution.py:54
  566.8 161.4 %reduce-scatter.33.cloned.1.call-start = ((), (), s32[]{:S(2)}) async-start(), calls=%async_computation.33 | async-start | bytes 3522560 | tf_op jit(solution)/shard_map/reduce_scatter | solution.py:48
  660.7 124.6 %reduce-scatter.29.cloned.1.call-start = ((), (), s32[]{:S(2)}) async-start(), calls=%async_computation.30 | async-start | bytes 3522560 | tf_op jit(solution)/shard_map/reduce_scatter | solution.py:58
  702.4 124.5 %copy-start.6 = (f32[1,1,1,1370,256]{4,2,3,1,0:T(1,128)S(1)}, f32[1,1,1,1370,256]{4,2,3,1,0:T(1,128)}, u32[]{:S(2)}) copy-start(f32[1,1,1,1370,256]{4,2,3,1,0:T(1,128)} %copy-done.4) | copy-start | bytes 4208644
  702.4 185.6 %all-gather.35.cloned.1.call-start = ((), (), s32[]{:S(2)}) async-start(), calls=%async_computation.31 | async-start | bytes 3522560 | tf_op jit(solution)/shard_map/all_gather | solution.py:54
  790.1 19.5 collective-permute-start.2
  830.9 198.2 %reduce-scatter.31.cloned.1.call-start = ((), (), s32[]{:S(2)}) async-start(), calls=%async_computation.32 | async-start | bytes 3522560 | tf_op jit(solution)/shard_map/reduce_scatter | solution.py:58
  974.0 116.1 %all-gather.37.cloned.1.call-start = ((), (), s32[]{:S(2)}) async-start(), calls=%async_computation.34 | async-start | bytes 3522560 | tf_op jit(solution)/shard_map/all_gather | solution.py:32
  1033.9 150.5 %reduce-scatter.35.cloned.1.call-start = ((), (), s32[]{:S(2)}) async-start(), calls=%async_computation.35 | async-start | bytes 3522560 | tf_op jit(solution)/shard_map/reduce_scatter | solution.py:48
  1129.3 134.5 %all-gather.41.cloned.1.call-start = ((), (), s32[]{:S(2)}) async-start(), calls=%async_computation.37 | async-start | bytes 3522560 | tf_op jit(solution)/shard_map/all_gather | solution.py:32
  1186.6 238.9 %copy-start.54 = (f32[1370,256]{1,0:T(8,128)}, f32[1370,256]{1,0:T(8,128)S(1)}, u32[]{:S(2)}) copy-start(f32[1370,256]{1,0:T(8,128)S(1)} %get-tuple-element.982) | copy-start | bytes 4208644
  1205.0 220.5 %copy-start.217 = (f32[1370]{0:T(1024)}, f32[1370]{0:T(1024)S(1)}, u32[]{:S(2)}) copy-start(f32[1370]{0:T(1024)S(1)} %get-tuple-element.1055) | copy-start | bytes 16444
  1205.0 220.5 %copy-start.219 = (f32[1370]{0:T(1024)}, f32[1370]{0:T(1024)S(1)}, u32[]{:S(2)}) copy-start(f32[1370]{0:T(1024)S(1)} %get-tuple-element.1062) | copy-start | bytes 16444
  1207.0 120.6 %all-gather.39.cloned.1.call-start = ((), (), s32[]{:S(2)}) async-start(), calls=%async_computation.36 | async-start | bytes 3522560 | tf_op jit(solution)/shard_map/all_gather | solution.py:54
  1210.5 13.9 collective-permute-start.1
  1226.2 142.2 %reduce-scatter.41.cloned.1.call-start = ((), (), s32[]{:S(2)}) async-start(), calls=%async_computation.41 | async-start | bytes 3522560 | tf_op jit(solution)/shard_map/reduce_scatter | solution.py:48
  1302.7 122.8 %reduce-scatter.37.cloned.1.call-start = ((), (), s32[]{:S(2)}) async-start(), calls=%async_computation.38 | async-start | bytes 3522560 | tf_op jit(solution)/shard_map/reduce_scatter | solution.py:58
  1344.4 121.3 %copy-start.256 = (f32[1370]{0:T(1024)S(1)}, f32[1370]{0:T(1024)}, u32[]{:S(2)}) copy-start(f32[1370]{0:T(1024)} %copy-done.254) | copy-start | bytes 16444
  1344.4 121.3 %copy-start.259 = (f32[1370]{0:T(1024)S(1)}, f32[1370]{0:T(1024)}, u32[]{:S(2)}) copy-start(f32[1370]{0:T(1024)} %copy-done.257) | copy-start | bytes 16444
  1344.5 121.3 %copy-start.275 = (f32[1370]{0:T(1024)S(1)}, f32[1370]{0:T(1024)}, u32[]{:S(2)}) copy-start(f32[1370]{0:T(1024)} %copy-done.274) | copy-start | bytes 16444
  1344.5 121.3 %copy-start.277 = (f32[1370]{0:T(1024)S(1)}, f32[1370]{0:T(1024)}, u32[]{:S(2)}) copy-start(f32[1370]{0:T(1024)} %copy-done.276) | copy-start | bytes 16444
  1344.5 121.3 %copy-start.279 = (f32[1370]{0:T(1024)S(1)}, f32[1370]{0:T(1024)}, u32[]{:S(2)}) copy-start(f32[1370]{0:T(1024)} %get-tuple-element.914) | copy-start | bytes 16444
  1344.5 121.3 %copy-start.281 = (f32[1370]{0:T(1024)S(1)}, f32[1370]{0:T(1024)}, u32[]{:S(2)}) copy-start(f32[1370]{0:T(1024)} %get-tuple-element.915) | copy-start | bytes 16444
  1344.5 121.9 %copy-start.291 = (f32[1,256]{1,0:T(1,128)S(1)}, f32[1,256]{1,0:T(1,128)}, u32[]{:S(2)}) copy-start(f32[1,256]{1,0:T(1,128)} %param.36) | copy-start | bytes 3076
  1344.5 180.1 %copy-start.69 = (bf16[1,1024,256]{2,1,0:T(8,128)(2,1)S(1)}, bf16[1,1024,256]{2,1,0:T(8,128)(2,1)}, u32[]{:S(2)}) copy-start(bf16[1,1024,256]{2,1,0:T(8,128)(2,1)} %copy-done.66) | copy-start | bytes 1572868
  1344.5 180.1 %all-gather.45.cloned.1.call-start = ((), (), s32[]{:S(2)}) async-start(), calls=%async_computation.42 | async-start | bytes 3522560 | tf_op jit(solution)/shard_map/all_gather | solution.py:32
  1429.8 19.5 collective-permute-start.4
  1467.7 154.6 %reduce-scatter.43.cloned.1.call-start = ((), (), s32[]{:S(2)}) async-start(), calls=%async_computation.43 | async-start | bytes 3522560 | tf_op jit(solution)/shard_map/reduce_scatter | solution.py:48
  1567.3 116.2 %all-gather.43.cloned.1.call-start = ((), (), s32[]{:S(2)}) async-start(), calls=%async_computation.39 | async-start | bytes 3522560 | tf_op jit(solution)/shard_map/all_gather | solution.py:54
  1627.2 195.3 %reduce-scatter.39.cloned.1.call-start = ((), (), s32[]{:S(2)}) async-start(), calls=%async_computation.40 | async-start | bytes 3522560 | tf_op jit(solution)/shard_map/reduce_scatter | solution.py:58
  1767.5 135.8 %all-gather.49.cloned.1.call-start = ((), (), s32[]{:S(2)}) async-start(), calls=%async_computation.45 | async-start | bytes 3522560 | tf_op jit(solution)/shard_map/all_gather | solution.py:32
  1846.4 115.4 %all-gather.47.cloned.1.call-start = ((), (), s32[]{:S(2)}) async-start(), calls=%async_computation.44 | async-start | bytes 3522560 | tf_op jit(solution)/shard_map/all_gather | solution.py:54
  1850.1 13.8 collective-permute-start.3
  1865.6 142.8 %reduce-scatter.53.cloned.1.call-start = ((), (), s32[]{:S(2)}) async-start(), calls=%async_computation.53 | async-start | bytes 3522560 | tf_op jit(solution)/shard_map/reduce_scatter | solution.py:48
  1950.6 115.6 %reduce-scatter.45.cloned.1.call-start = ((), (), s32[]{:S(2)}) async-start(), calls=%async_computation.46 | async-start | bytes 3522560 | tf_op jit(solution)/shard_map/reduce_scatter | solution.py:58
  1977.0 171.8 %all-gather.51.cloned.1.call-start = ((), (), s32[]{:S(2)}) async-start(), calls=%async_computation.47 | async-start | bytes 3522560 | tf_op jit(solution)/shard_map/all_gather | solution.py:54
  2091.7 195.9 %reduce-scatter.47.cloned.1.call-start = ((), (), s32[]{:S(2)}) async-start(), calls=%async_computation.48 | async-start | bytes 3522560 | tf_op jit(solution)/shard_map/reduce_scatter | solution.py:58
  2232.5 154.8 %all-gather.53.cloned.1.call-start = ((), (), s32[]{:S(2)}) async-start(), calls=%async_computation.49 | async-start | bytes 3522560 | tf_op jit(solution)/shard_map/all_gather | solution.py:54
  2311.0 14.0 collective-permute-start.5
  2329.7 129.6 %reduce-scatter.49.cloned.1.call-start = ((), (), s32[]{:S(2)}) async-start(), calls=%async_computation.50 | async-start | bytes 3522560 | tf_op jit(solution)/shard_map/reduce_scatter | solution.py:58
  2404.2 181.1 %all-gather.55.cloned.1.call-start = ((), (), s32[]{:S(2)}) async-start(), calls=%async_computation.51 | async-start | bytes 3522560 | tf_op jit(solution)/shard_map/all_gather | solution.py:54
  2485.9 210.9 %reduce-scatter.65.cloned.1.call-start = ((), (), s32[]{:S(2)}) async-start(), calls=%async_computation.59 | async-start | bytes 2621440 | tf_op jit(solution)/shard_map/reduce_scatter | solution.py:427
  2520.3 178.5 %reduce-scatter.63.cloned.1.call-start = ((), (), s32[]{:S(2)}) async-start(), calls=%async_computation.58 | async-start | bytes 2621440 | tf_op jit(solution)/shard_map/reduce_scatter | solution.py:421
  2566.0 145.4 %reduce-scatter.61.cloned.1.call-start = ((), (), s32[]{:S(2)}) async-start(), calls=%async_computation.57 | async-start | bytes 655360 | tf_op jit(solution)/shard_map/reduce_scatter | solution.py:406
  2596.6 116.4 %reduce-scatter.55.cloned.1.call-start = ((), (), s32[]{:S(2)}) async-start(), calls=%async_computation.54 | async-start | bytes 655360 | tf_op jit(solution)/shard_map/reduce_scatter | solution.py:391
  2672.3 46.7 %reduce-scatter.59.cloned.1.call-start = ((), (), s32[]{:S(2)}) async-start(), calls=%async_computation.56 | async-start | bytes 655360 | tf_op jit(solution)/shard_map/reduce_scatter | solution.py:397
  2679.8 63.2 %reduce-scatter.57.cloned.1.call-start = ((), (), s32[]{:S(2)}) async-start(), calls=%async_computation.55 | async-start | bytes 655360 | tf_op jit(solution)/shard_map/reduce_scatter | solution.py:394
  2686.3 113.6 %reduce-scatter.51.cloned.1.call-start = ((), (), s32[]{:S(2)}) async-start(), calls=%async_computation.52 | async-start | bytes 3522560 | tf_op jit(solution)/shard_map/reduce_scatter | solution.py:58
  2698.8 133.6 %copy-start.88 = (f32[1370,256]{1,0:T(8,128)S(1)}, f32[1370,256]{1,0:T(8,128)}, u32[]{:S(2)}) copy-start(f32[1370,256]{1,0:T(8,128)} %copy-done.87) | copy-start | bytes 4208644
  (366 other events, 10299.1 us)
Sparse Core Ops, SparseCore 0:
  32.0 56.9 all-gather.24
  126.9 54.9 reduce-scatter.22
  301.7 53.9 reduce-scatter.24
  566.3 56.9 all-gather.32
  625.3 62.0 all-gather.30
  831.1 56.9 all-gather.34
  974.1 54.9 reduce-scatter.30
  1129.4 54.9 reduce-scatter.34
  1302.8 65.4 reduce-scatter.40
  1370.5 54.9 reduce-scatter.36
  1627.3 56.2 all-gather.42
  1846.5 56.7 all-gather.48
  1905.5 56.3 all-gather.46
  2091.8 56.9 all-gather.50
  2232.6 54.9 reduce-scatter.46
  2404.3 54.9 reduce-scatter.48
Sparse Core Ops, SparseCore 1:
  128.8 23.4 all-gather.56
  202.1 56.8 all-gather.26
  260.5 23.7 all-gather.58
  395.6 56.7 all-gather.28
  492.8 54.8 reduce-scatter.26
  660.8 67.4 reduce-scatter.32
  730.4 54.8 reduce-scatter.28
  1034.0 56.1 all-gather.36
  1207.1 56.6 all-gather.40
  1265.4 62.1 all-gather.38
  1467.8 56.7 all-gather.44
  1567.4 54.8 reduce-scatter.42
  1767.6 54.8 reduce-scatter.38
  1950.7 57.7 reduce-scatter.52
  2011.4 54.8 reduce-scatter.44
  2329.7 57.5 all-gather.52
  2485.9 56.8 all-gather.54
  2545.5 32.3 reduce-scatter.64
  2580.3 31.3 reduce-scatter.62
  2614.3 21.6 reduce-scatter.60
  2672.4 22.5 reduce-scatter.54
  2697.4 21.5 reduce-scatter.58
  2721.4 21.6 reduce-scatter.56
  2746.0 53.8 reduce-scatter.50
where the time goes:
time: 2870 us; the launch traced here: 2860 us
  waiting for transfers between devices  1580 us (55%)
  matrix products  601 us (21%)
  other arithmetic  256 us (9%)
  blocking collectives  226 us (8%)
  local copies, waits for them, and re-layouts  154 us (5%)
    reduce_scatter x8, waiting for transfers between devices, input_total(): lax.psum_scatter(partial_value.astype(jnp.bfloat16), 'mp', scatter_dimens...  447 us
    all_gather x8, waiting for transfers between devices, normalize(): lax.all_gather((normed * gain + shift_vec).astype(jnp.bfloat16), 'mp', ax...  384 us
    reduce_scatter x8, waiting for transfers between devices, branch_total(): lax.psum_scatter(partial_value.astype(jnp.bfloat16), 'mp', scatter_dimens...  354 us
    all_gather x8, waiting for transfers between devices, branch_spread(): return lax.all_gather(grad_low, 'mp', axis=1, tiled=True)  261 us
    dot_general x24, matrix products, product(): return jnp.dot(left, right, preferred_element_type=jnp.float32)  195 us
    psum x8, blocking collectives, normalize(): sums = lax.psum((jnp.sum(rows_in, 1), jnp.sum(rows_in * rows_in, 1)), 'mp')  126 us
    ppermute x6, waiting for transfers between devices, shifted(): lax.ppermute(value, axis, [(source, source + steps) for source in range(l...  88.8 us
    convert_element_type x8, other arithmetic, one_block(): grad_scores = (probs * (grad_probs - row_dot)).astype(jnp.bfloat16)  79.8 us
  transfers between devices with their start and end apart: 46, of which 40 were waited for; matrix products, arithmetic and copies ran while one was open for 15% of the time, Pallas kernels for 0%

commit v1 on v0

v1 whole, which is shorter than its diff:
```python
import functools

import jax
import jax.numpy as jnp
from jax import lax
from jax.experimental import pallas as pl
from jax.experimental.pallas import tpu as pltpu
from jax.sharding import PartitionSpec as P


HD = 64
LOW = jnp.bfloat16
WIDE = jnp.float32
HBM = pl.BlockSpec(memory_space=pl.ANY)

epsilon = 1e-06
inv_root_two = 0.7071067811865476
inv_root_tau = 0.3989422804014327


class Place:
    def __init__(self):
        self.S = lax.axis_size("section")
        self.DP = lax.axis_size("dp")
        self.MP = lax.axis_size("mp")
        self.Y = self.DP // 2
        self.H = self.MP // 2
        self.s = lax.axis_index("section")
        self.d = lax.axis_index("dp")
        self.z = lax.axis_index("mp")
        self.y = lax.div(self.d, 2)
        self.c = lax.rem(self.d, 2)

    def other_y(self, r):
        return lax.rem(self.y + r, self.Y)

    def other_z(self, r):
        return lax.rem(self.z + r, self.MP)


class Moves:
    def __init__(self, send_sems, recv_sems, counts):
        self.send_sems, self.recv_sems = send_sems, recv_sems
        self.base, total = {}, 0
        for name, count in counts.items():
            self.base[name] = total
            total += count
        self.total = total
        self.sent = []

    def arrival(self, name, index):
        return self.recv_sems.at[self.base[name] + index]

    def send(self, src, dst, name, index, when=None, **to):
        at = len(self.sent)
        assert at < self.send_sems.shape[0]
        copy = pltpu.make_async_remote_copy(
            src_ref=src,
            dst_ref=dst,
            send_sem=self.send_sems.at[at],
            recv_sem=self.arrival(name, index),
            device_id=to,
        )
        self.sent.append((copy, when))
        if when is None:
            copy.start()
        else:
            pl.when(when)(copy.start)

    def wait(self, ref, name, index):
        pltpu.make_async_copy(ref, ref, self.arrival(name, index)).wait()

    def finish(self):
        for copy, when in self.sent:
            if when is None:
                copy.wait_send()
            else:
                pl.when(when)(copy.wait_send)


def tile(start, size):
    return pl.ds(pl.multiple_of(start * size, size), size)


def holder(place, c, piece):
    image = 2 * (piece // 2) + c
    return lax.div(image, place.MP), piece % 2, lax.rem(image, place.MP)


def gather_counts(S, Y, MP, groups=3):
    return dict(rows=S * MP, vectors=S * MP, piece=groups * S * Y * MP, pair=groups * S * Y * MP)


def gather_kernel(pieces, sent_ref, vec_ref, a_ref, b_ref, c_ref, rows_ref, vecs_ref, A, B, C, send_sems, recv_sems, own_sems):
    place = Place()
    s, y, c, z, d = place.s, place.y, place.c, place.z, place.d
    S, Y, MP, H = place.S, place.Y, place.MP, place.H
    moves = Moves(send_sems, recv_sems, gather_counts(S, Y, MP))
    columns = sent_ref.shape[2]
    shards, wholes = (a_ref, b_ref, c_ref), (A, B, C)

    def spot(g, l, yy, cc, zz):
        dd = yy * 2 + cc
        shard, whole = shards[g], wholes[g]
        at = (tile(dd, shard.shape[-2]), tile(zz, shard.shape[-1]))
        return whole.at[(l, slice(None)) + at] if len(shard.shape) == 3 else whole.at[(l,) + at]

    def mark(g, l, yy, zz):
        return ((g * S + l) * Y + yy) * MP + zz

    def to_pair(g, l, yy, zz, src=None, when=None):
        there = spot(g, l, yy, c, zz)
        moves.send(
            there if src is None else src, there, "pair", mark(g, l, yy, zz), when, section=s, dp=y * 2 + 1 - c, mp=z
        )

    def to_rows(g, l, yy, zz, when=None, src=None):
        there = spot(g, l, yy, c, zz)
        for r in range(1, Y):
            moves.send(
                there if src is None else src, there, "piece", mark(g, l, yy, zz), when,
                section=s, dp=place.other_y(r) * 2 + c, mp=z,
            )

    def to_section(g, l, yy, zz, when=None, src=None):
        there = spot(g, l, yy, c, zz)
        moves.send(there if src is None else src, there, "piece", mark(g, l, yy, zz), when, section=1 - s, dp=d, mp=z)

    def landed(g, l, yy, zz):
        moves.wait(spot(g, l, yy, c, zz), "piece", mark(g, l, yy, zz))

    own_copies = []

    def near(zz):
        return lax.div(zz, H) == lax.div(z, H)

    def along(g, zz, step, when, src=None):
        there = spot(g, s, y, c, zz)
        moves.send(
            there if src is None else src, there, "piece", mark(g, s, y, zz), when,
            section=s, dp=d, mp=jnp.clip(z + step, 0, MP - 1),
        )

    def columns_out(g):
        there = spot(g, s, y, c, z)
        along(g, z, 1, z + 1 < MP, shards[g])
        along(g, z, -1, z >= 1, shards[g])
        to_section(g, s, y, z, src=shards[g])
        to_rows(g, s, y, z, src=shards[g])
        to_pair(g, s, y, z, shards[g])
        copy = pltpu.make_async_copy(shards[g], there, own_sems.at[g])
        copy.start()
        own_copies.append(copy)

    def columns_in(g, far):
        for step, there in ((1, z >= far), (-1, z + far < MP)):
            zz = jnp.clip(z - step * far, 0, MP - 1)

            @pl.when(there)
            def _():
                landed(g, s, y, zz)

            along(g, zz, step, there & ((z + 1 < MP) if step == 1 else (z >= 1)))
            to_section(g, s, y, zz, there)
            to_rows(g, s, y, zz, there & ((s == 0) | near(zz)))
            to_pair(g, s, y, zz, when=there)

    def far_column(k):
        return lax.rem(lax.div(z, H) + 1, 2) * H + k

    def near_column(k):
        return lax.div(z, H) * H + k

    def nearest_first():
        return [z] + [lax.div(z, H) * H + lax.rem(z + r, H) for r in range(1, H)] + [far_column(k) for k in range(H)]

    def section_in(g, which):
        zz = nearest_first()[which]
        landed(g, 1 - s, y, zz)
        to_rows(g, 1 - s, y, zz, None if which >= H else s == 1)
        to_pair(g, 1 - s, y, zz)

    def rows_in(g):
        for r in range(1, Y):
            yy = place.other_y(r)
            for k in range(H):
                zz = jnp.where(s == 1, near_column(k), far_column(k))
                landed(g, 1, yy, zz)
                to_section(g, 1, yy, zz)
                to_pair(g, 1, yy, zz)
            for zz in range(MP):
                landed(g, 0, yy, zz)
                to_pair(g, 0, yy, zz)

    def corner_in(g):
        for r in range(1, Y):
            for k in range(H):
                zz = jnp.where(s == 1, far_column(k), near_column(k))
                landed(g, 1, place.other_y(r), zz)
                to_pair(g, 1, place.other_y(r), zz)

    for piece in range(pieces):
        to_s, to_c, to_z = holder(place, c, piece)
        here = (to_s == s) & (to_c == c) & (to_z == z)
        there = rows_ref.at[s, :, tile(z, columns)]
        moves.send(
            sent_ref.at[piece], there, "rows", s * MP + z, jnp.logical_not(here),
            section=to_s, dp=y * 2 + to_c, mp=to_z,
        )

        @pl.when(here)
        def _():
            pltpu.make_async_copy(sent_ref.at[piece], there, moves.arrival("rows", s * MP + z)).start()

    for q in range(1, S * MP):
        at = lax.rem(s * MP + z + q, S * MP)
        moves.send(vec_ref, vecs_ref.at[s * MP + z], "vectors", s * MP + z, section=lax.div(at, MP), dp=d, mp=lax.rem(at, MP))
    own_vec = pltpu.make_async_copy(vec_ref, vecs_ref.at[s * MP + z], own_sems.at[3])
    own_vec.start()

    for g in range(3):
        columns_out(g)
        own_copies[g].wait()
        for far in range(1, MP):
            columns_in(g, far)
            section_in(g, far - 1)
        section_in(g, MP - 1)
        if g:
            rows_in(g - 1)
            corner_in(g - 1)
    rows_in(2)
    corner_in(2)

    @pl.when(s * MP + z < pieces)
    def _():
        for section in range(S):
            for zz in range(MP):
                moves.wait(rows_ref.at[section, :, tile(zz, columns)], "rows", section * MP + zz)

    for q in range(1, S * MP):
        at = lax.rem(s * MP + z + q, S * MP)
        moves.wait(vecs_ref.at[at], "vectors", at)
    for g in range(3):
        for l in range(S):
            for yy in range(Y):
                for zz in range(MP):
                    moves.wait(spot(g, l, yy, 1 - c, zz), "pair", mark(g, l, yy, zz))
    own_vec.wait()
    moves.finish()


def gather(sent, vec, a, b, c):
    S, DP, MP = (lax.axis_size(name) for name in ("section", "dp", "mp"))
    Y = DP // 2
    pieces, rows, columns = sent.shape
    counts = gather_counts(S, Y, MP)
    sends = pieces + S * MP - 1 + 3 * (2 * MP + (1 + 2 * (MP - 1)) * (1 + Y) + MP * Y + (Y - 1) * (MP + 3 * (MP // 2)))
    return pl.pallas_call(
        functools.partial(gather_kernel, pieces),
        in_specs=[HBM] * 5,
        out_specs=[HBM] * 5,
        out_shape=[
            jax.ShapeDtypeStruct((S, rows, columns * MP), LOW),
            jax.ShapeDtypeStruct((S * MP,) + vec.shape, WIDE),
            jax.ShapeDtypeStruct((S, a.shape[0], a.shape[1] * DP, a.shape[2] * MP), LOW),
            jax.ShapeDtypeStruct((S, b.shape[0] * DP, b.shape[1] * MP), LOW),
            jax.ShapeDtypeStruct((S, c.shape[0] * DP, c.shape[1] * MP), LOW),
        ],
        scratch_shapes=[
            pltpu.SemaphoreType.DMA((sends,)),
            pltpu.SemaphoreType.DMA((sum(counts.values()),)),
            pltpu.SemaphoreType.DMA((4,)),
        ],
        compiler_params=pltpu.CompilerParams(has_side_effects=True),
    )(sent, vec, a, b, c)


def scatter_counts(S, Y, MP, pieces, groups=4):
    H = MP // 2
    return dict(
        back=max(pieces, MP),
        corner_x=groups * (Y - 1) * H,
        corner_y=groups * (Y - 1) * H,
        from_x=groups * MP,
        from_y=groups * (Y - 1) * MP,
        from_z=groups * MP,
        vec_pair=1,
        vec_x=1,
        vec_y=Y - 1,
        vec_z=MP,
    )


ORDER = (3, 2, 1, 0)


def scatter_kernel(
    pieces, table_ref, first_ref, last_ref, *refs
):
    place = Place()
    s, y, c, z, d = place.s, place.y, place.c, place.z, place.d
    S, Y, MP, H = place.S, place.Y, place.MP, place.H
    grads = (refs[0:2], refs[2:4], refs[4:6], refs[6:8])
    ends_ref, sums_ref, outs = refs[8], refs[9], refs[10:14]
    mine, over, across, corner_x, corner_y, from_x, from_y, from_z = (refs[14 + 4 * i : 18 + 4 * i] for i in range(8))
    send_sems, recv_sems, load_sems, vec_here, vec_pair, vec_x, vec_y, vec_z = refs[46:]
    moves = Moves(send_sems, recv_sems, scatter_counts(S, Y, MP, pieces))
    block = first_ref.shape[2]

    def part(g, l, yy, zz):
        ref = grads[g][l]
        piece = outs[g].shape
        at = (yy, slice(None), tile(zz, piece[-1]))
        return ref.at[(slice(None),) + at] if len(piece) == 3 else ref.at[at]

    moves.send(table_ref.at[1 - c], vec_pair, "vec_pair", 0, section=s, dp=y * 2 + 1 - c, mp=z)
    moves.wait(vec_pair, "vec_pair", 0)
    vec_here[...] = table_ref[c] + vec_pair[...]
    moves.send(vec_here.at[1 - s], vec_x, "vec_x", 0, section=1 - s, dp=d, mp=z)
    moves.wait(vec_x, "vec_x", 0)
    vec_here[s] = vec_here[s] + vec_x[...]
    for r in range(1, Y):
        at = Y - r - 1
        moves.send(
            vec_here.at[s, place.other_y(r)], vec_y.at[at], "vec_y", at, section=s, dp=place.other_y(r) * 2 + c, mp=z
        )
    for r in range(1, Y):
        moves.wait(vec_y.at[r - 1], "vec_y", r - 1)
    vec_here[s, y] = vec_here[s, y] + jnp.sum(vec_y[...], 0)
    for r in range(1, MP):
        moves.send(vec_here.at[s, y, place.other_z(r)], vec_z.at[z], "vec_z", z, section=s, dp=d, mp=place.other_z(r))
    vec_total = vec_here[s, y, z]
    for r in range(1, MP):
        moves.wait(vec_z.at[place.other_z(r)], "vec_z", place.other_z(r))
        vec_total = vec_total + vec_z[place.other_z(r)]
    sums_ref[...] = vec_total

    number = s * MP + z
    active = number < pieces
    piece = 2 * lax.div(number, 2) + c
    for section, ref in ((0, first_ref), (1, last_ref)):
        for zz in range(MP):
            to_c = lax.rem(number, 2)
            here = (s == section) & (to_c == c) & (z == zz)
            there = ends_ref.at[piece]
            moves.send(
                ref.at[zz], there, "back", piece, active & jnp.logical_not(here), section=section, dp=y * 2 + to_c, mp=zz
            )

            @pl.when(active & here)
            def _():
                pltpu.make_async_copy(ref.at[zz], there, moves.arrival("back", piece)).start()

    loads = []

    def by_section(g, mine_too, yy, zz, use):
        for layer in range(S):
            pl.when((s == layer) if mine_too else (s != layer))(lambda: use(part(g, layer, yy, zz)))

    def send_part(g, mine_too, yy, zz, dst, name, index, **to):
        at = len(moves.sent)
        sample = part(g, 0, yy, zz)

        def go(ref):
            pltpu.make_async_remote_copy(
                src_ref=ref, dst_ref=dst, send_sem=send_sems.at[at], recv_sem=moves.arrival(name, index), device_id=to
            ).start()

        by_section(g, mine_too, yy, zz, go)
        moves.sent.append(
            (
                pltpu.make_async_remote_copy(
                    src_ref=sample, dst_ref=dst, send_sem=send_sems.at[at], recv_sem=moves.arrival(name, index), device_id=to
                ),
                None,
            )
        )

    def load(g, mine_too, yy, zz, dst):
        at = len(loads)
        by_section(g, mine_too, yy, zz, lambda ref: pltpu.make_async_copy(ref, dst, load_sems.at[at]).start())
        loads.append(pltpu.make_async_copy(dst, dst, load_sems.at[at]))
        return at

    over_at, across_at, mine_at = {}, {}, {}
    for g in ORDER:
        for r in range(1, Y):
            for k in range(H):
                slot = ((r - 1) * H) + k
                send_part(
                    g, False, place.other_y(r), k, corner_x[g].at[slot], "corner_x", g * (Y - 1) * H + slot,
                    section=1 - s, dp=d, mp=z,
                )
                back = (Y - r) % Y
                send_part(
                    g, False, place.other_y(r), H + k, corner_y[g].at[(back - 1) * H + k], "corner_y",
                    g * (Y - 1) * H + (back - 1) * H + k,
                    section=s, dp=place.other_y(r) * 2 + c, mp=z,
                )
        for k in range(H):
            over_at[g, k] = load(g, False, y, H + k, over[g].at[k])
            for r in range(1, Y):
                across_at[g, r, k] = load(g, True, place.other_y(r), k, across[g].at[(r - 1) * H + k])
        for k in range(H):
            send_part(g, False, y, k, from_x[g].at[k], "from_x", g * MP + k, section=1 - s, dp=d, mp=z)
            for r in range(1, Y):
                back = (Y - r) % Y
                slot = (back - 1) * MP + H + k
                send_part(
                    g, True, place.other_y(r), H + k, from_y[g].at[slot], "from_y", g * (Y - 1) * MP + slot,
                    section=s, dp=place.other_y(r) * 2 + c, mp=z,
                )
    for g in ORDER:
        for zz in range(MP):
            mine_at[g, zz] = load(g, True, y, zz, mine[g].at[zz])

    def add_into(dst, *terms):
        total = dst[...].astype(WIDE)
        for term in terms:
            total = total + term[...].astype(WIDE)
        dst[...] = total.astype(LOW)

    for g in ORDER:
        for k in range(H):
            for r in range(1, Y):
                slot = (r - 1) * H + k
                moves.wait(corner_x[g].at[slot], "corner_x", g * (Y - 1) * H + slot)
                loads[across_at[g, r, k]].wait()
                add_into(across[g].at[slot], corner_x[g].at[slot])
                back = (Y - r) % Y
                out = (back - 1) * MP + k
                moves.send(
                    across[g].at[slot], from_y[g].at[out], "from_y", g * (Y - 1) * MP + out,
                    section=s, dp=place.other_y(r) * 2 + c, mp=z,
                )
            for r in range(1, Y):
                slot = (r - 1) * H + k
                moves.wait(corner_y[g].at[slot], "corner_y", g * (Y - 1) * H + slot)
            loads[over_at[g, k]].wait()
            add_into(over[g].at[k], *(corner_y[g].at[(r - 1) * H + k] for r in range(1, Y)))
            moves.send(over[g].at[k], from_x[g].at[H + k], "from_x", g * MP + H + k, section=1 - s, dp=d, mp=z)

    for g in ORDER:
        for zz in list(range(H)) + list(range(H, MP)):
            moves.wait(from_x[g].at[zz], "from_x", g * MP + zz)
            for r in range(1, Y):
                slot = (r - 1) * MP + zz
                moves.wait(from_y[g].at[slot], "from_y", g * (Y - 1) * MP + slot)
            loads[mine_at[g, zz]].wait()
            add_into(mine[g].at[zz], from_x[g].at[zz], *(from_y[g].at[(r - 1) * MP + zz] for r in range(1, Y)))
            moves.send(
                mine[g].at[zz], from_z[g].at[z], "from_z", g * MP + z, z != zz, section=s, dp=d, mp=zz
            )

    for g in ORDER:
        total = mine[g][z].astype(WIDE)
        for r in range(1, MP):
            zz = place.other_z(r)
            moves.wait(from_z[g].at[zz], "from_z", g * MP + zz)
            total = total + from_z[g][zz].astype(WIDE)
        outs[g][...] = total

    for p in range(pieces):
        moves.wait(ends_ref.at[p], "back", p)
    moves.finish()


def scatter(table, first, last, grads, shapes):
    S, DP, MP = (lax.axis_size(name) for name in ("section", "dp", "mp"))
    Y, H = DP // 2, MP // 2
    _, rows, block = first.shape
    pieces = grads["pieces"]
    flat = [grads[name][layer] for name in ("qkv", "out", "fc1", "fc2") for layer in range(S)]
    counts = scatter_counts(S, Y, MP, pieces)
    vmem = pl.BlockSpec(memory_space=pltpu.VMEM)

    def room(count):
        return [pltpu.VMEM((count,) + shape, LOW) for shape in shapes]

    sends = 2 + Y - 1 + MP - 1 + S * MP + 4 * ((Y - 1) * H * 2 + H * Y + H * Y + MP)
    return pl.pallas_call(
        functools.partial(scatter_kernel, pieces),
        in_specs=[vmem] + [HBM] * (2 + len(flat)),
        out_specs=[HBM] + [vmem] * 5,
        out_shape=[jax.ShapeDtypeStruct((pieces, rows, block), LOW), jax.ShapeDtypeStruct(table.shape[4:], WIDE)]
        + [jax.ShapeDtypeStruct(shape, WIDE) for shape in shapes],
        scratch_shapes=room(MP)
        + room(H)
        + room((Y - 1) * H)
        + room((Y - 1) * H)
        + room((Y - 1) * H)
        + room(MP)
        + room((Y - 1) * MP)
        + room(MP)
        + [
            pltpu.SemaphoreType.DMA((sends,)),
            pltpu.SemaphoreType.DMA((sum(counts.values()),)),
            pltpu.SemaphoreType.DMA((4 * (H * Y + MP),)),
            pltpu.VMEM(table.shape[1:], WIDE),
            pltpu.VMEM(table.shape[1:], WIDE),
            pltpu.VMEM(table.shape[2:], WIDE),
            pltpu.VMEM((Y - 1,) + table.shape[3:], WIDE),
            pltpu.VMEM(table.shape[3:], WIDE),
        ],
        compiler_params=pltpu.CompilerParams(has_side_effects=True, vmem_limit_bytes=60 << 20),
    )(table, first, last, *flat)


def nn(left, right):
    return lax.dot_general(left, right, (((1,), (0,)), ((), ())), preferred_element_type=WIDE)


def nt(left, right):
    return lax.dot_general(left, right, (((1,), (1,)), ((), ())), preferred_element_type=WIDE)


def tn(left, right):
    return lax.dot_general(left, right, (((0,), (0,)), ((), ())), preferred_element_type=WIDE)


def row_mean(value):
    return jnp.mean(value, 1, keepdims=True)


def column_sum(value):
    return jnp.sum(value.astype(WIDE), 0, keepdims=True)


def centre(rows_in):
    mean = row_mean(rows_in)
    inv_std = lax.rsqrt(row_mean(rows_in * rows_in) - mean * mean + epsilon)
    return (rows_in - mean) * inv_std, inv_std


def norm_back(grad, rows_in, gain):
    xhat, inv_std = centre(rows_in)
    weighted = grad * gain
    d_rows = inv_std * (weighted - row_mean(weighted) - xhat * row_mean(weighted * xhat))
    return d_rows, column_sum(grad * xhat), column_sum(grad)


def full(shape):
    return pl.BlockSpec(shape, lambda i: (0,) * len(shape))


def compute_call(kernel, steps, ins, outs, scratch, flops, args):
    return pl.pallas_call(
        kernel,
        grid=(steps,),
        in_specs=ins,
        out_specs=[spec for spec, _ in outs],
        out_shape=[shape for _, shape in outs],
        scratch_shapes=scratch,
        compiler_params=pltpu.CompilerParams(vmem_limit_bytes=58 << 20),
        cost_estimate=pl.CostEstimate(flops=flops, bytes_accessed=40 << 20, transcendentals=0),
    )(*args)


LN1_GAIN, LN1_BIAS, B_QUERY, B_VALUE, B_OUT, SCALE_ATTN, LN2_GAIN, LN2_BIAS, B_FC2, SCALE_MLP = range(10)


def project_kernel(x_ref, vec_ref, w_ref, n_ref, kv_ref, q_ref, held):
    step = pl.program_id(0)

    @pl.when(step == 0)
    def _():
        xhat, _ = centre(x_ref[...])
        low = (xhat * vec_ref[LN1_GAIN][None] + vec_ref[LN1_BIAS][None]).astype(LOW)
        held[...] = low
        n_ref[...] = low

    value = nn(held[...], w_ref[...])

    @pl.when(step == 0)
    def _():
        kv_ref[0] = value.astype(LOW)

    @pl.when(step == 1)
    def _():
        kv_ref[1] = (value + vec_ref[B_VALUE][None]).astype(LOW)

    @pl.when(step == 2)
    def _():
        q_ref[...] = (value + vec_ref[B_QUERY][None]).astype(LOW)


def project(rows_in, vec, attn, layer):
    rows, width = rows_in.shape
    low = jax.ShapeDtypeStruct((rows, width), LOW)
    return compute_call(
        project_kernel,
        3,
        [
            full(rows_in.shape),
            full(vec.shape),
            pl.BlockSpec((None, None, width, width), lambda i: (layer, lax.rem(i + 1, 3), 0, 0)),
        ],
        [
            (full(rows_in.shape), low),
            (full((2, rows, width)), jax.ShapeDtypeStruct((2, rows, width), LOW)),
            (full(rows_in.shape), low),
        ],
        [pltpu.VMEM((rows, width), LOW)],
        6 * rows * width * width,
        (rows_in, vec, attn),
    )


def attend_kernel(q_ref, k0, k1, v0, v1, mask_ref, o_ref, wide_ref, p_ref):
    bias0, bias1 = mask_ref[:, 0:1], mask_ref[:, 1:2]
    outs = []
    for head in range(q_ref.shape[1] // HD):
        at = slice(head * HD, head * HD + HD)
        q = (q_ref[:, at].astype(WIDE) * (HD**-0.5)).astype(LOW)
        s0 = nt(k0[:, at], q) + bias0
        s1 = nt(k1[:, at], q) + bias1
        top = jnp.maximum(jnp.max(s0, 0, keepdims=True), jnp.max(s1, 0, keepdims=True))
        e0 = jnp.exp(s0 - top)
        e1 = jnp.exp(s1 - top)
        scale = 1.0 / (jnp.sum(e0, 0, keepdims=True) + jnp.sum(e1, 0, keepdims=True))
        p0 = (e0 * scale).astype(LOW)
        p1 = (e1 * scale).astype(LOW)
        p_ref[head, 0] = p0
        p_ref[head, 1] = p1
        outs.append(tn(v0[:, at], p0) + tn(v1[:, at], p1))
    out = jnp.concatenate(outs, 0).T
    wide_ref[...] = out
    o_ref[...] = out.astype(LOW)


def attend(q, kv0, kv1, mask):
    rows, width = q.shape
    steps, heads = width // 128, width // HD
    one = pl.BlockSpec((rows, 128), lambda i: (0, i))
    key = pl.BlockSpec((None, rows, 128), lambda i: (0, 0, i))
    value = pl.BlockSpec((None, rows, 128), lambda i: (1, 0, i))
    return compute_call(
        attend_kernel,
        steps,
        [one, key, key, value, value, full(mask.shape)],
        [
            (one, jax.ShapeDtypeStruct((rows, width), LOW)),
            (one, jax.ShapeDtypeStruct((rows, width), WIDE)),
            (
                pl.BlockSpec((2, 2, rows, rows), lambda i: (i, 0, 0, 0)),
                jax.ShapeDtypeStruct((heads, 2, rows, rows), LOW),
            ),
        ],
        [],
        32 * heads * rows * rows * HD,
        (q, kv0, kv1, kv0, kv1, mask),
    )


def mlp_kernel(x_ref, o_ref, vec_ref, bias_ref, wo_ref, w1_ref, w2_ref, y_ref, branch_ref, middle_ref, n_ref, act_ref, slope_ref, two_ref, total):
    step = pl.program_id(0)

    @pl.when(step == 0)
    def _():
        branch = nt(o_ref[...], wo_ref[...]) + vec_ref[B_OUT][None]
        branch_ref[...] = branch.astype(LOW)
        middle = x_ref[...] + vec_ref[SCALE_ATTN][None] * branch
        middle_ref[...] = middle
        xhat, _ = centre(middle)
        n_ref[...] = (xhat * vec_ref[LN2_GAIN][None] + vec_ref[LN2_BIAS][None]).astype(LOW)
        total[...] = jnp.zeros_like(total)

    hidden = nn(n_ref[...], w1_ref[...]) + bias_ref[0:1]
    cdf = 0.5 + 0.5 * lax.erf(hidden * inv_root_two)
    active = (hidden * cdf).astype(LOW)
    act_ref[...] = active
    slope_ref[...] = (cdf + hidden * jnp.exp(-0.5 * hidden * hidden) * inv_root_tau).astype(LOW)
    total[...] += nt(active, w2_ref[...])

    @pl.when(step == pl.num_programs(0) - 1)
    def _():
        two = total[...] + vec_ref[B_FC2][None]
        two_ref[...] = two.astype(LOW)
        y_ref[...] = middle_ref[...] + vec_ref[SCALE_MLP][None] * two


CHUNK = 512


def mlp(rows_in, out, vec, bias, weights, layer):
    attn, fc1, fc2 = weights
    rows, width = rows_in.shape
    hidden = fc1.shape[2]
    low = (full(rows_in.shape), jax.ShapeDtypeStruct((rows, width), LOW))
    wide = (full(rows_in.shape), jax.ShapeDtypeStruct((rows, width), WIDE))
    units = (pl.BlockSpec((rows, CHUNK), lambda i: (0, i)), jax.ShapeDtypeStruct((rows, hidden), LOW))
    weight = pl.BlockSpec((None, width, CHUNK), lambda i: (layer, 0, i))
    return compute_call(
        mlp_kernel,
        hidden // CHUNK,
        [
            full(rows_in.shape),
            full(rows_in.shape),
            full(vec.shape),
            pl.BlockSpec((8, CHUNK), lambda i: (0, i)),
            pl.BlockSpec((None, None, width, width), lambda i: (layer, 3, 0, 0)),
            weight,
            weight,
        ],
        [wide, low, wide, low, units, units, low],
        [pltpu.VMEM((rows, width), WIDE)],
        4 * rows * width * hidden,
        (rows_in, out, vec, bias, attn, fc1, fc2),
    )


def store_halves(value, even_first, own_ref, there_ref, lead=()):
    count = own_ref.shape[len(lead)]
    size = own_ref.shape[len(lead) + 1]
    for d in range(2 * count):
        part = value[d * size : (d + 1) * size].astype(LOW)

        def put(ref, part=part, d=d):
            ref[lead + (d // 2,)] = part

        if d % 2 == 0:
            pl.when(even_first)(lambda: put(own_ref))
            pl.when(jnp.logical_not(even_first))(lambda: put(there_ref))
        else:
            pl.when(even_first)(lambda: put(there_ref))
            pl.when(jnp.logical_not(even_first))(lambda: put(own_ref))


def mlp_back_kernel(
    c_ref, dy_ref, vec_ref, two_ref, act_ref, slope_ref, n_ref, middle_ref, branch_ref, o_ref, wo_ref, w1_ref, w2_ref,
    grad_ref, do_ref, own1, there1, own2, there2, own_o, there_o, sums_ref, units_ref, dm, total,
):
    step = pl.program_id(0)
    even = c_ref[0] == 0

    @pl.when(step == 0)
    def _():
        low = (dy_ref[...] * vec_ref[SCALE_MLP][None]).astype(LOW)
        dm[...] = low
        sums_ref[0:1] = column_sum(dy_ref[...] * two_ref[...].astype(WIDE))
        sums_ref[1:2] = column_sum(low)
        total[...] = jnp.zeros_like(total)

    df = (nn(dm[...], w2_ref[...]) * slope_ref[...].astype(WIDE)).astype(LOW)
    units_ref[...] = jnp.broadcast_to(column_sum(df), units_ref.shape)
    store_halves(tn(dm[...], act_ref[...]), even, own2, there2)
    store_halves(tn(n_ref[...], df), even, own1, there1)
    total[...] += nt(df, w1_ref[...])

    @pl.when(step == pl.num_programs(0) - 1)
    def _():
        d_rows, d_gain, d_bias = norm_back(total[...], middle_ref[...], vec_ref[LN2_GAIN][None])
        sums_ref[2:3] = d_gain
        sums_ref[3:4] = d_bias
        grad = dy_ref[...] + d_rows
        grad_ref[...] = grad
        sums_ref[4:5] = column_sum(grad * branch_ref[...].astype(WIDE))
        da = (grad * vec_ref[SCALE_ATTN][None]).astype(LOW)
        sums_ref[5:6] = column_sum(da)
        sums_ref[6:8] = jnp.zeros((2, sums_ref.shape[1]), WIDE)
        do_ref[...] = nn(da, wo_ref[...]).astype(LOW)
        store_halves(tn(da, o_ref[...]), even, own_o, there_o)


def mlp_back(half, dy, vec, saved, weights, layer, count):
    attn, fc1, fc2 = weights
    rows, width = dy.shape
    hidden = fc1.shape[2]
    block = width // (2 * count)
    whole = full(dy.shape)
    low = (whole, jax.ShapeDtypeStruct((rows, width), LOW))
    wide = (whole, jax.ShapeDtypeStruct((rows, width), WIDE))
    units = pl.BlockSpec((rows, CHUNK), lambda i: (0, i))
    weight = pl.BlockSpec((None, width, CHUNK), lambda i: (layer, 0, i))
    grad = (
        pl.BlockSpec((count, block, CHUNK), lambda i: (0, 0, i)),
        jax.ShapeDtypeStruct((count, block, hidden), LOW),
    )
    grad_o = (full((count, block, width)), jax.ShapeDtypeStruct((count, block, width), LOW))
    return compute_call(
        mlp_back_kernel,
        hidden // CHUNK,
        [
            pl.BlockSpec(memory_space=pltpu.SMEM),
            whole,
            full(vec.shape),
            whole,
            units,
            units,
            whole,
            whole,
            whole,
            whole,
            pl.BlockSpec((None, None, width, width), lambda i: (layer, 3, 0, 0)),
            weight,
            weight,
        ],
        [
            wide,
            low,
            grad,
            grad,
            grad,
            grad,
            grad_o,
            grad_o,
            (full((8, width)), jax.ShapeDtypeStruct((8, width), WIDE)),
            (pl.BlockSpec((8, CHUNK), lambda i: (0, i)), jax.ShapeDtypeStruct((8, hidden), WIDE)),
        ],
        [pltpu.VMEM((rows, width), LOW), pltpu.VMEM((rows, width), WIDE)],
        8 * rows * width * hidden,
        (
            half,
            dy,
            vec,
            saved["two"],
            saved["active"],
            saved["slope"],
            saved["n_two"],
            saved["middle"],
            saved["branch"],
            saved["out"],
            attn,
            fc1,
            fc2,
        ),
    )


def attend_back_kernel(q_ref, k0, k1, v0, v1, p_ref, g_ref, o_ref, d0_ref, d1_ref):
    outs = []
    for head in range(q_ref.shape[1] // HD):
        at = slice(head * HD, head * HD + HD)
        q = q_ref[:, at]
        g = g_ref[:, at]
        prod = g.astype(WIDE) * o_ref[:, at]
        dot = jnp.sum(prod.T, 0, keepdims=True)
        dq = None
        for half, (k, v, out, first) in enumerate(((k0, v0, d0_ref, 1), (k1, v1, d1_ref, 0))):
            p = p_ref[head, half]
            out[first + 1, :, at] = nn(p, g).astype(LOW)
            ds = (p.astype(WIDE) * (nt(v[:, at], g) - dot)).astype(LOW)
            part = tn(k[:, at], ds)
            dq = part if dq is None else dq + part
            out[first, :, at] = (nn(ds, q) * (HD**-0.5)).astype(LOW)
        outs.append(dq * (HD**-0.5))
    d0_ref[0] = jnp.concatenate(outs, 0).T.astype(LOW)


def attend_back(q, kv0, kv1, probs, grad, out):
    rows, width = q.shape
    steps, heads = width // 128, width // HD
    one = pl.BlockSpec((rows, 128), lambda i: (0, i))
    key = pl.BlockSpec((None, rows, 128), lambda i: (0, 0, i))
    value = pl.BlockSpec((None, rows, 128), lambda i: (1, 0, i))

    def several(count):
        return (
            pl.BlockSpec((count, rows, 128), lambda i: (0, 0, i)),
            jax.ShapeDtypeStruct((count, rows, width), LOW),
        )

    return compute_call(
        attend_back_kernel,
        steps,
        [one, key, key, value, value, pl.BlockSpec((2, 2, rows, rows), lambda i: (i, 0, 0, 0)), one, one],
        [several(3), several(2)],
        [],
        40 * heads * rows * rows * HD,
        (q, kv0, kv1, kv0, kv1, probs, grad, out),
    )


def project_back_kernel(
    c_ref, d0_ref, d1_ref, n_ref, x_ref, grad_ref, vec_ref, w_ref, dx_ref, own, there, sums_ref, total
):
    step = pl.program_id(0)
    even = c_ref[0] == 0

    @pl.when(step == 0)
    def _():
        total[...] = jnp.zeros_like(total)

    theirs = jnp.where(step == 0, 0.0, d1_ref[...].astype(WIDE))
    grad = (d0_ref[...].astype(WIDE) + theirs).astype(LOW)
    store_halves(tn(n_ref[...], grad), even, own, there)
    total[...] += nt(grad, w_ref[...])
    sums = column_sum(grad)

    @pl.when(step == 0)
    def _():
        sums_ref[0:1] = sums

    @pl.when(step == 2)
    def _():
        sums_ref[1:2] = sums
        d_rows, d_gain, d_bias = norm_back(total[...], x_ref[...], vec_ref[LN1_GAIN][None])
        sums_ref[2:3] = d_gain
        sums_ref[3:4] = d_bias
        sums_ref[4:8] = jnp.zeros((4, sums_ref.shape[1]), WIDE)
        dx_ref[...] = grad_ref[...] + d_rows


def project_back(half, d0, d1, saved, grad, vec, attn, layer, count):
    rows, width = grad.shape
    block = width // (2 * count)
    whole = full(grad.shape)
    out = (
        pl.BlockSpec((None, count, block, width), lambda i: (i, 0, 0, 0)),
        jax.ShapeDtypeStruct((3, count, block, width), LOW),
    )
    return compute_call(
        project_back_kernel,
        3,
        [
            pl.BlockSpec(memory_space=pltpu.SMEM),
            pl.BlockSpec((None, rows, width), lambda i: (i, 0, 0)),
            pl.BlockSpec((None, rows, width), lambda i: (jnp.maximum(i - 1, 0), 0, 0)),
            whole,
            whole,
            whole,
            full(vec.shape),
            pl.BlockSpec((None, None, width, width), lambda i: (layer, i, 0, 0)),
        ],
        [
            (whole, jax.ShapeDtypeStruct((rows, width), WIDE)),
            out,
            out,
            (full((8, width)), jax.ShapeDtypeStruct((8, width), WIDE)),
        ],
        [pltpu.VMEM((rows, width), WIDE)],
        12 * rows * width * width,
        (half, d0, d1, saved["n_one"], saved["rows_in"], grad, vec, attn),
    )


def pick(stack, index, axis=0):
    return lax.dynamic_index_in_dim(stack, index, axis, keepdims=False)


def layer_forward(rows_in, vec, bias, weights, layer, mask, from_pair):
    n_one, kv0, q = project(rows_in, vec, weights[0], layer)
    kv1 = from_pair(kv0)
    out, out_wide, probs = attend(q, kv0, kv1, mask)
    leaving, branch, middle, n_two, active, slope, two = mlp(rows_in, out, vec, bias, weights, layer)
    saved = dict(
        rows_in=rows_in,
        n_one=n_one,
        q=q,
        kv0=kv0,
        kv1=kv1,
        out=out,
        out_wide=out_wide,
        probs=probs,
        branch=branch,
        middle=middle,
        n_two=n_two,
        active=active,
        slope=slope,
        two=two,
    )
    return (leaving, saved)


def layer_backward(grad_rows, saved, vec, weights, layer, half, from_pair):
    count = lax.axis_size("dp") // 2
    grad_middle, d_out, own1, there1, own2, there2, own_o, there_o, sums, units = mlp_back(
        half, grad_rows, vec, saved, weights, layer, count
    )

    def joined(own, there):
        return (own.astype(WIDE) + from_pair(there).astype(WIDE)).astype(LOW)

    g_fc2, g_fc1, g_out = joined(own2, there2), joined(own1, there1), joined(own_o, there_o)
    d0, d1 = attend_back(saved["q"], saved["kv0"], saved["kv1"], saved["probs"], d_out, saved["out_wide"])
    grad_in, own, there, sums_one = project_back(
        half, d0, from_pair(d1), saved, grad_middle, vec, weights[0], layer, count
    )
    g_qkv = joined(own, there)
    vectors = dict(
        ln1_gain=sums_one[2],
        ln1_bias=sums_one[3],
        b_query=sums_one[0],
        b_value=sums_one[1],
        b_out=sums[5],
        scale_attn=sums[4],
        ln2_gain=sums[2],
        ln2_bias=sums[3],
        b_fc1=units[0],
        b_fc2=sums[1],
        scale_mlp=sums[0],
    )
    return (grad_in, dict(qkv=g_qkv, out=g_out, fc1=g_fc1, fc2=g_fc2), vectors)


NARROW = ("ln1_gain", "ln1_bias", "b_query", "b_value", "b_out", "scale_attn", "ln2_gain", "ln2_bias", "b_fc2", "scale_mlp")


def local(
    boundary,
    ln1_gain,
    ln1_bias,
    w_query,
    w_key,
    w_value,
    b_query,
    b_value,
    w_out,
    b_out,
    scale_attn,
    ln2_gain,
    ln2_bias,
    w_fc1,
    b_fc1,
    w_fc2,
    b_fc2,
    scale_mlp,
):
    place = Place()
    _, micros, images, seq_len, columns = boundary.shape
    S, DP, MP = place.S, place.DP, place.MP
    width = columns * MP
    rows = -(-seq_len // 32) * 16
    pieces = 2 * micros
    number = place.s * MP + place.z
    active = number < pieces

    def from_pair(value):
        return lax.ppermute(value, "dp", [(i, i + 1 - 2 * (i % 2)) for i in range(DP)])

    images_low = boundary.reshape(micros, seq_len, columns).astype(LOW)
    sent = jnp.pad(images_low, ((0, 0), (0, 2 * rows - seq_len), (0, 0))).reshape(pieces, rows, columns)
    keys = jnp.arange(rows)[:, None] + rows * jnp.stack([place.c, 1 - place.c])[None]
    mask = jnp.where(keys < seq_len, 0.0, -1e30).astype(WIDE)
    mask = jnp.pad(mask, ((0, 0), (0, 126)))
    half = place.c.reshape(1)
    narrow = (ln1_gain, ln1_bias, b_query, b_value, b_out, scale_attn, ln2_gain, ln2_bias, b_fc2, scale_mlp)
    packed = jnp.concatenate([v[0] for v in narrow] + [b_fc1[0]])
    lines = -(-packed.shape[0] // 1024) * 8
    packed = jnp.pad(packed, (0, lines * 128 - packed.shape[0])).reshape(lines, 128)
    attn_shard = jnp.stack([w_query[0], w_key[0], w_value[0], w_out[0].T])
    arrived, vecs, *weights = gather(sent, packed, attn_shard, w_fc1[0], w_fc2[0].T)
    arrived = jnp.where(active, arrived.astype(WIDE), 0.0)
    vecs = vecs.reshape(S, MP, -1)
    vectors, biases = [], []
    for layer in range(S):
        start = len(NARROW) * columns
        table = vecs[layer, :, :start].reshape(MP, len(NARROW), columns)
        table = jnp.moveaxis(table, 0, 1).reshape(len(NARROW), width)
        vectors.append(jnp.pad(table, ((0, 16 - len(NARROW)), (0, 0))))
        bias = vecs[layer, :, start : start + b_fc1.shape[1]].reshape(1, -1)
        biases.append(jnp.pad(bias, ((0, 7), (0, 0))))

    saved = []
    rows_now = arrived[0]
    for layer in range(S):
        rows_now, kept = layer_forward(rows_now, vectors[layer], biases[layer], weights, layer, mask, from_pair)
        saved.append(kept)
        if layer + 1 < S:
            rows_now = rows_now.astype(LOW).astype(WIDE)
    end_rows = rows_now

    grad_now = arrived[1]
    matrix_grads, vector_grads = [None] * S, [None] * S
    for layer in reversed(range(S)):
        grad_now, matrix_grads[layer], vector_grads[layer] = layer_backward(
            grad_now, saved[layer], vectors[layer], weights, layer, half, from_pair
        )
        if layer:
            grad_now = grad_now.astype(LOW).astype(WIDE)

    def by_column(value):
        return jnp.stack([value[:, i * columns : (i + 1) * columns].astype(LOW) for i in range(MP)])

    grads = {name: [matrix_grads[layer][name] for layer in range(S)] for name in ("qkv", "out", "fc1", "fc2")}
    grads["pieces"] = pieces
    shapes = [(3,) + w_query.shape[1:], w_query.shape[1:], w_fc1.shape[1:], (w_fc2.shape[2], w_fc2.shape[1])]
    names = NARROW + ("b_fc1",)
    table = jnp.stack(
        [
            jnp.concatenate([vector_grads[layer][name].reshape(MP, DP, -1) for name in names], 2)
            for layer in range(S)
        ]
    )
    lines = -(-table.shape[3] // 1024) * 8
    table = jnp.pad(table, ((0, 0), (0, 0), (0, 0), (0, lines * 128 - table.shape[3])))
    table = table.reshape(S, MP, DP // 2, 2, lines, 128).transpose(3, 0, 2, 1, 4, 5)
    ends, summed, g_qkv, g_out, g_fc1, g_fc2 = scatter(table, by_column(grad_now), by_column(end_rows), grads, shapes)
    ends_out = ends.reshape(micros, 2 * rows, columns)[:, :seq_len].astype(WIDE).reshape(boundary.shape)
    summed = summed.reshape(-1)
    v, start = {}, 0
    for name in names:
        size = (b_fc1.shape[1] if name == "b_fc1" else columns) // DP
        v[name] = summed[start : start + size][None]
        start += size

    return (
        ends_out,
        v["ln1_gain"],
        v["ln1_bias"],
        g_qkv[0][None],
        g_qkv[1][None],
        g_qkv[2][None],
        v["b_query"],
        v["b_value"],
        g_out.T[None],
        v["b_out"],
        v["scale_attn"],
        v["ln2_gain"],
        v["ln2_bias"],
        g_fc1[None],
        v["b_fc1"],
        g_fc2.T[None],
        v["b_fc2"],
        v["scale_mlp"],
    )


def solution(mesh):
    return jax.shard_map(
        local,
        mesh=mesh,
        in_specs=(
            P("section", None, "dp", None, "mp"),
            P("section", "mp"),
            P("section", "mp"),
            P("section", "dp", "mp"),
            P("section", "dp", "mp"),
            P("section", "dp", "mp"),
            P("section", "mp"),
            P("section", "mp"),
            P("section", "mp", "dp"),
            P("section", "mp"),
            P("section", "mp"),
            P("section", "mp"),
            P("section", "mp"),
            P("section", "dp", "mp"),
            P("section", "mp"),
            P("section", "mp", "dp"),
            P("section", "mp"),
            P("section", "mp"),
        ),
        out_specs=(
            P("section", None, "dp", None, "mp"),
            P("section", ("mp", "dp")),
            P("section", ("mp", "dp")),
            P("section", "dp", "mp"),
            P("section", "dp", "mp"),
            P("section", "dp", "mp"),
            P("section", ("mp", "dp")),
            P("section", ("mp", "dp")),
            P("section", "mp", "dp"),
            P("section", ("mp", "dp")),
            P("section", ("mp", "dp")),
            P("section", ("mp", "dp")),
            P("section", ("mp", "dp")),
            P("section", "dp", "mp"),
            P("section", ("mp", "dp")),
            P("section", "mp", "dp"),
            P("section", ("mp", "dp")),
            P("section", ("mp", "dp")),
        ),
        check_vma=False,
    )
```

time: 2870 us -> 1150 us (0.40)
  waiting for transfers between devices: 1580 us -> 7.13 us
  Pallas kernels: 0 us -> 999 us
  matrix products: 601 us -> 0 us
  blocking collectives: 226 us -> 0 us
  other arithmetic: 256 us -> 60.6 us
  local copies, waits for them, and re-layouts: 154 us -> 70.9 us
    pallas_call x0 -> x14, Pallas kernels: none -> 999 us  [the longest x12 376 us: compute_call(): pl.pallas_call(kernel, grid=(steps,), in_specs=ins, out_specs=[spec for s...]
    reduce_scatter x22 -> x0, waiting for transfers between devices: 828 us -> none  [the longest x8 447 us: input_total(): lax.psum_scatter(partial_value.astype(jnp.bfloat16), 'mp', scatter_dimens...]
    all_gather x18 -> x0, waiting for transfers between devices: 662 us -> none  [the longest x8 384 us: normalize(): lax.all_gather((normed * gain + shift_vec).astype(jnp.bfloat16), 'mp', ax...]
    dot_general x128 -> x0, matrix products: 601 us -> none  [the longest x24 195 us: product(): return jnp.dot(left, right, preferred_element_type=jnp.float32)]
    psum x12 -> x0, blocking collectives: 189 us -> none  [the longest x8 126 us: normalize(): sums = lax.psum((jnp.sum(rows_in, 1), jnp.sum(rows_in * rows_in, 1)), 'mp')]
    reduce_sum x36 -> x0, other arithmetic: 97.3 us -> none  [the longest x8 25.1 us: one_block(): total = jnp.sum(expo, -1, keepdims=True)]
    ppermute x6 -> x12, waiting for transfers between devices: 88.8 us -> 7.13 us  [from_pair(): lax.ppermute(value, 'dp', [(i, i + 1 - 2 * (i % 2)) for i in range(DP)])]
    convert_element_type x31 -> x11, other arithmetic: 114 us -> 50.6 us  [the longest x8 37 us: joined(): return (own.astype(WIDE) + from_pair(there).astype(WIDE)).astype(LOW)]
  transfers between devices with their start and end apart: 46 -> 12, of which waited for: 40 -> 2; matrix products, arithmetic and copies ran while one was open for 15% -> 7% of each run, Pallas kernels for 0% -> 12%
where the time goes in v1:
time: 1150 us; the launch traced here: 1140 us
  Pallas kernels  999 us (87%)
  local copies, waits for them, and re-layouts  70.9 us (6%)
  other arithmetic  60.6 us (5%)
    pallas_call x12, Pallas kernels, compute_call(): pl.pallas_call(kernel, grid=(steps,), in_specs=ins, out_specs=[spec for s...  376 us
    pallas_call x1, Pallas kernels, scatter(): pl.pallas_call(functools.partial(scatter_kernel, pieces), in_specs=[vmem]...  344 us
    pallas_call x1, Pallas kernels, gather(): pl.pallas_call(functools.partial(gather_kernel, pieces), in_specs=[HBM] *...  279 us
    convert_element_type x8, other arithmetic, joined(): return (own.astype(WIDE) + from_pair(there).astype(WIDE)).astype(LOW)  37 us
  transfers between devices with their start and end apart: 12, of which 2 were waited for; matrix products, arithmetic and copies ran while one was open for 7% of the time, Pallas kernels for 12%

profile of v1, /device:TPU:26, one launch (start us, length us, event | category | flops | bytes accessed | tf_op | source)
XLA Modules:
  0.0 1142.6 jit_solution(10510378901673209704)
XLA Ops:
  4.1 0.7 constant_dynamic-update-slice_fusion.5
  4.8 0.7 constant_dynamic-update-slice_fusion.4
  5.5 0.7 constant_dynamic-update-slice_fusion.3
  6.8 0.7 constant_dynamic-update-slice_fusion.1
  7.5 0.7 constant_dynamic-update-slice_fusion
  8.8 1.0 copy.40
  9.8 2.0 copy.41
  11.9 6.2 convert_element_type.116
  18.5 1.5 pad.30
  20.0 0.9 pad_maximum_fusion.2.a_ref
  20.8 279.2 %shard_map.313 = (bf16[2,688,1024]{2,1,0:T(8,128)(2,1)}, f32[8,32,128]{2,1,0:T(8,128)}, bf16[2,4,1024,1024]{3,2,1,0:T(8,128)(2,1)}, bf16[2,1024,4096]{2,1,0:T(8,128)(2,1)}, bf16[2,1024,4096]{2,1,0:T(8,128)(2,1)}) custom-call(bf16[6,688,256]{2,1,0:T(8,128)(2,1)} %bitcast.101, f32[32,128]{1,0:T(8,128)} %pad_bitcast_fusion.vec_ref, ...), custom_call_target="tpu_custom_call" | custom-call | tf_op jit(solution)/shard_map/pallas_call | solution.py:258
  300.1 0.9 reshape.94
  301.7 2.6 convert_select_fusion
  304.3 3.1 slice_bitcast_fusion
  307.4 11.9 %shard_map.314 = (bf16[688,1024]{1,0:T(8,128)(2,1)}, bf16[2,688,1024]{2,1,0:T(8,128)(2,1)}, bf16[688,1024]{1,0:T(8,128)(2,1)}) custom-call(f32[688,1024]{1,0:T(8,128)} %get-tuple-element.213.x_ref, f32[16,1024]{1,0:T(8,128)} %pad.32.vec_ref, bf16[2,4,1024,1024]{3,2,1,0:T(8,128)(2,1)} %get-tuple-element.89.w_ref.wo_ref), custom_call_target="tpu_custom_call" | custom-call | flops 4328521728 | bytes 41943040 | tf_op jit(solution)/shard_map/pallas_call | solution.py:547
  320.0 0.8 pad.33.mask_ref
  322.2 2.8 collective-permute-done.k1.v1
  324.9 1.5 copy-done.19
  326.4 36.8 %shard_map.315 = (bf16[688,1024]{1,0:T(8,128)(2,1)}, f32[688,1024]{1,0:T(8,128)}, bf16[16,2,688,688]{3,2,1,0:T(8,128)(2,1)}) custom-call(bf16[688,1024]{1,0:T(8,128)(2,1)} %get-tuple-element.90.q_ref, bf16[2,688,1024]{2,1,0:T(8,128)(2,1)} %get-tuple-element.91.k0.v0, bf16[2,688,1024]{2,1,0:T(8,128)(2,1)} %copy-done.19, ...), custom_call_target="tpu_custom_call" | custom-call | flops 15510536192 | bytes 41943040 | tf_op jit(solution)/shard_map/pallas_call | solution.py:547
  363.3 27.4 %shard_map.316 = (f32[688,1024]{1,0:T(8,128)}, bf16[688,1024]{1,0:T(8,128)(2,1)}, f32[688,1024]{1,0:T(8,128)}, bf16[688,1024]{1,0:T(8,128)(2,1)}, bf16[688,4096]...) custom-call(f32[688,1024]{1,0:T(8,128)} %get-tuple-element.213.x_ref, ...), custom_call_target="tpu_custom_call" | custom-call | flops 11542724608 | bytes 41943040 | tf_op jit(solution)/shard_map/pallas_call | solution.py:547
  390.7 3.7 convert_convert_fusion.1.x_ref
  394.4 11.3 shard_map.317
  406.8 4.3 collective-permute-done.1.k1.v1
  411.1 1.5 copy-done.20
  412.6 36.9 %shard_map.318 = (bf16[688,1024]{1,0:T(8,128)(2,1)}, f32[688,1024]{1,0:T(8,128)}, bf16[16,2,688,688]{3,2,1,0:T(8,128)(2,1)}) custom-call(bf16[688,1024]{1,0:T(8,128)(2,1)} %get-tuple-element.97.q_ref, bf16[2,688,1024]{2,1,0:T(8,128)(2,1)} %get-tuple-element.98.k0.v0, bf16[2,688,1024]{2,1,0:T(8,128)(2,1)} %copy-done.20, ...), custom_call_target="tpu_custom_call" | custom-call | flops 15510536192 | bytes 41943040 | tf_op jit(solution)/shard_map/pallas_call | solution.py:547
  449.5 27.4 %shard_map.319 = (f32[688,1024]{1,0:T(8,128)}, bf16[688,1024]{1,0:T(8,128)(2,1)}, f32[688,1024]{1,0:T(8,128)}, bf16[688,1024]{1,0:T(8,128)(2,1)}, bf16[688,4096]...) custom-call(f32[688,1024]{1,0:T(8,128)} %convert_convert_fusion.1.x_ref, ...), custom_call_target="tpu_custom_call" | custom-call | flops 11542724608 | bytes 41943040 | tf_op jit(solution)/shard_map/pallas_call | solution.py:547
  476.9 48.5 %shard_map.320 = (f32[688,1024]{1,0:T(8,128)}, bf16[688,1024]{1,0:T(8,128)(2,1)}, bf16[2,256,4096]{2,1,0:T(8,128)(2,1)}, bf16[2,256,4096]{2,1,0:T(8,128)(2,1)}, ...) custom-call(s32[1]{0:T(128)} %bitcast.c_ref, ...), custom_call_target="tpu_custom_call" | custom-call | flops 23085449216 | bytes 41943040 | tf_op jit(solution)/shard_map/pallas_call | solution.py:547
  525.4 43.0 %shard_map.321 = (bf16[3,688,1024]{2,1,0:T(8,128)(2,1)}, bf16[2,688,1024]{2,1,0:T(8,128)(2,1)}) custom-call(bf16[688,1024]{1,0:T(8,128)(2,1)} %get-tuple-element.97.q_ref, bf16[2,688,1024]{2,1,0:T(8,128)(2,1)} %get-tuple-element.98.k0.v0, bf16[2,688,1024]{2,1,0:T(8,128)(2,1)} %copy-done.20, bf16[2,688,1024]{2,1,0:T(8,128)(2,1)} %get-tuple-element.98.k0.v0, ...), custom_call_target="tpu_custom_call" | custom-call | flops 19388170240 | bytes 41943040 | tf_op jit(solution)/shard_map/pallas_call | solution.py:547
  568.9 0.9 slice_reduce_fusion
  575.4 1.1 slice_bitcast_fusion.5
  576.5 2.6 add_convert_fusion.6.refs_3_
  579.1 20.8 %shard_map.322 = (f32[688,1024]{1,0:T(8,128)}, bf16[3,2,256,1024]{3,2,1,0:T(8,128)(2,1)}, bf16[3,2,256,1024]{3,2,1,0:T(8,128)(2,1)}, f32[8,1024]{1,0:T(8,128)}) custom-call(s32[1]{0:T(128)} %bitcast.c_ref, bf16[3,688,1024]{2,1,0:T(8,128)(2,1)} %get-tuple-element.109.d0_ref, bf16[2,688,1024]{2,1,0:T(8,128)(2,1)} %collective-permute-done.2.d1_ref, ...), custom_call_target="tpu_custom_call" | custom-call | flops 8657043456 | bytes 41943040 | tf_op jit(solution)/shard_map/pallas_call | solution.py:547
  599.9 3.7 convert_convert_fusion.dy_ref
  603.6 48.4 %shard_map.323 = (f32[688,1024]{1,0:T(8,128)}, bf16[688,1024]{1,0:T(8,128)(2,1)}, bf16[2,256,4096]{2,1,0:T(8,128)(2,1)}, bf16[2,256,4096]{2,1,0:T(8,128)(2,1)}, ...) custom-call(s32[1]{0:T(128)} %bitcast.c_ref, ...), custom_call_target="tpu_custom_call" | custom-call | flops 23085449216 | bytes 41943040 | tf_op jit(solution)/shard_map/pallas_call | solution.py:547
  652.0 0.9 slice_reduce_fusion.1
  656.5 42.5 %shard_map.324 = (bf16[3,688,1024]{2,1,0:T(8,128)(2,1)}, bf16[2,688,1024]{2,1,0:T(8,128)(2,1)}) custom-call(bf16[688,1024]{1,0:T(8,128)(2,1)} %get-tuple-element.90.q_ref, bf16[2,688,1024]{2,1,0:T(8,128)(2,1)} %get-tuple-element.91.k0.v0, bf16[2,688,1024]{2,1,0:T(8,128)(2,1)} %copy-done.19, bf16[2,688,1024]{2,1,0:T(8,128)(2,1)} %get-tuple-element.91.k0.v0, ...), custom_call_target="tpu_custom_call" | custom-call | flops 19388170240 | bytes 41943040 | tf_op jit(solution)/shard_map/pallas_call | solution.py:547
  703.7 1.0 concatenate.15
  705.0 2.9 add_convert_fusion.7.refs_2_
  708.2 7.3 add_convert_fusion.2.refs_5_
  715.6 5.8 add_convert_fusion.refs_7_
  721.3 21.0 %shard_map.325 = (f32[688,1024]{1,0:T(8,128)}, bf16[3,2,256,1024]{3,2,1,0:T(8,128)(2,1)}, bf16[3,2,256,1024]{3,2,1,0:T(8,128)(2,1)}, f32[8,1024]{1,0:T(8,128)}) custom-call(s32[1]{0:T(128)} %bitcast.c_ref, bf16[3,688,1024]{2,1,0:T(8,128)(2,1)} %get-tuple-element.122.d0_ref, bf16[2,688,1024]{2,1,0:T(8,128)(2,1)} %collective-permute-done.3.d1_ref, ...), custom_call_target="tpu_custom_call" | custom-call | flops 8657043456 | bytes 41943040 | tf_op jit(solution)/shard_map/pallas_call | solution.py:547
  742.3 1.5 slice_reduce_fusion.18
  743.9 1.4 reshape_squeeze.85
  745.3 1.4 reshape_squeeze.84
  746.6 1.3 reshape_squeeze.83
  748.0 1.3 reshape_squeeze.82
  749.3 1.6 concatenate.14
  750.9 1.5 select_maximum_fusion
  752.4 1.6 reshape.97
  754.0 1.7 copy.53
  755.7 2.1 convert.13
  758.3 2.2 pad_maximum_fusion
  761.2 3.3 add_convert_fusion.4.refs_1_
  764.5 5.9 add_convert_fusion.3.refs_4_
  770.4 5.8 add_convert_fusion.1.refs_6_
  776.2 3.4 add_convert_fusion.5.refs_0_
  779.6 343.8 %shard_map.326 = (bf16[6,688,256]{2,1,0:T(8,128)(2,1)}, f32[8,128]{1,0:T(8,128)}, f32[3,256,256]{2,1,0:T(8,128)}, f32[256,256]{1,0:T(8,128)}, f32[256,1024]{1,0:T(8,128)}, /*index=5*/f32[256,1024]{1,0:T(8,128)}) custom-call(f32[2,2,2,4,8,128]{5,4,3,2,1,0:T(8,128)} %bitcast.107, bf16[4,688,256]{2,1,0:T(8,128)(2,1)} %get-tuple-element.239.first_ref, ...), custom_call_target="tpu_custom_call" | custom-call | tf_op jit(solution)/shard_map/pallas_call | solution.py:481
  1123.4 1.4 slice.210
  1124.8 1.6 slice_bitcast_fusion.12
  1126.5 1.8 copy.43
  1128.2 2.0 fusion.1
  1130.2 2.5 copy.44
  1133.1 8.3 reshape.103
  1141.4 1.0 copy.66
  (109 shorter events, 25.2 us)
Async XLA Ops:
  18.5 1.5 copy-start.12
  18.5 1.5 copy-start.13
  18.5 1.5 copy-start.14
  319.3 5.6 collective-permute-start
  324.9 1.5 copy-start.19
  405.7 5.4 collective-permute-start.1
  411.1 1.5 copy-start.20
  525.4 45.1 %copy-start.16 = (f32[8,1024]{1,0:T(8,128)S(1)}, f32[8,1024]{1,0:T(8,128)}, u32[]{:S(2)}) copy-start(f32[8,1024]{1,0:T(8,128)} %get-tuple-element.130) | copy-start | bytes 98308
  525.4 49.2 %copy-start.5 = (f32[688,1024]{1,0:T(8,128)S(1)}, f32[688,1024]{1,0:T(8,128)}, u32[]{:S(2)}) copy-start(f32[688,1024]{1,0:T(8,128)} %get-tuple-element.133) | copy-start | bytes 8454148
  568.4 10.7 collective-permute-start.2
  568.8 7.7 collective-permute-start.7
  574.6 1.9 copy-start.10
  574.8 133.1 %collective-permute-start.9 = (bf16[2,256,4096]{2,1,0:T(8,128)(2,1)}, bf16[2,256,4096]{2,1,0:T(8,128)(2,1)}, u32[]{:S(2)}, u32[]{:S(2)}) collective-permute-start(bf16[2,256,4096]{2,1,0:T(8,128)(2,1)} %get-tuple-element.145), channel_id=1, source_target_pairs={{0,4},{4,0},{8,12},{12,8},{1,5},{5,1},{9,13},{13,9},{2,6},{6,2},{1... | collective-permute-start | bytes 12582920 | tf_op jit(solution)/shard_map/ppermute | solution.py:1029
  575.2 140.3 %collective-permute-start.11 = (bf16[2,256,4096]{2,1,0:T(8,128)(2,1)}, bf16[2,256,4096]{2,1,0:T(8,128)(2,1)}, u32[]{:S(2)}, u32[]{:S(2)}) collective-permute-start(bf16[2,256,4096]{2,1,0:T(8,128)(2,1)} %get-tuple-element.149), channel_id=1, source_target_pairs={{0,4},{4,0},{8,12},{12,8},{1,5},{5,1},{9,13},{13,9},{2,6},{6,2},{1... | collective-permute-start | bytes 12582920 | tf_op jit(solution)/shard_map/ppermute | solution.py:1029
  603.6 50.0 %copy-start.17 = (f32[8,1024]{1,0:T(8,128)S(1)}, f32[8,1024]{1,0:T(8,128)}, u32[]{:S(2)}) copy-start(f32[8,1024]{1,0:T(8,128)} %get-tuple-element.129) | copy-start | bytes 98308
  656.3 48.4 %collective-permute-start.6 = (bf16[2,256,1024]{2,1,0:T(8,128)(2,1)}, bf16[2,256,1024]{2,1,0:T(8,128)(2,1)}, u32[]{:S(2)}, u32[]{:S(2)}) collective-permute-start(bf16[2,256,1024]{2,1,0:T(8,128)(2,1)} %get-tuple-element.139), channel_id=1, source_target_pairs={{0,4},{4,0},{8,12},{12,8},{1,5},{5,1},{9,13},{13,9},{2,6},{6,2},{1... | collective-permute-start | bytes 3145736 | tf_op jit(solution)/shard_map/ppermute | solution.py:1029
  656.5 42.8 %copy-start.15 = (f32[8,1024]{1,0:T(8,128)S(1)}, f32[8,1024]{1,0:T(8,128)}, u32[]{:S(2)}) copy-start(f32[8,1024]{1,0:T(8,128)} %get-tuple-element.127) | copy-start | bytes 98308
  699.0 22.3 %collective-permute-start.3 = (bf16[2,688,1024]{2,1,0:T(8,128)(2,1)}, bf16[2,688,1024]{2,1,0:T(8,128)(2,1)}, u32[]{:S(2)}, u32[]{:S(2)}) collective-permute-start(bf16[2,688,1024]{2,1,0:T(8,128)(2,1)} %get-tuple-element.123), channel_id=1, source_target_pairs={{0,4},{4,0},{8,12},{12,8},{1,5},{5,1},{9,13},{13,9},{2,6},{6,2},{1... | collective-permute-start | bytes 8454152 | tf_op jit(solution)/shard_map/ppermute | solution.py:1029
  703.5 57.1 %collective-permute-start.5 = (bf16[3,2,256,1024]{3,2,1,0:T(8,128)(2,1)}, bf16[3,2,256,1024]{3,2,1,0:T(8,128)(2,1)S(1)}, u32[]{:S(2)}, u32[]{:S(2)}) collective-permute-start(bf16[3,2,256,1024]{3,2,1,0:T(8,128)(2,1)} %get-tuple-element.137), channel_id=1, source_target_pairs={{0,4},{4,0},{8,12},{12,8},{1,5},{5,1},{9,13},{13,9},{2,6},{6,2},{1... | collective-permute-start | bytes 9437192 | tf_op jit(solution)/shard_map/ppermute | solution.py:1029
  704.7 59.8 %collective-permute-start.8 = (bf16[2,256,4096]{2,1,0:T(8,128)(2,1)}, bf16[2,256,4096]{2,1,0:T(8,128)(2,1)}, u32[]{:S(2)}, u32[]{:S(2)}) collective-permute-start(bf16[2,256,4096]{2,1,0:T(8,128)(2,1)} %get-tuple-element.143), channel_id=1, source_target_pairs={{0,4},{4,0},{8,12},{12,8},{1,5},{5,1},{9,13},{13,9},{2,6},{6,2},{1... | collective-permute-start | bytes 12582920 | tf_op jit(solution)/shard_map/ppermute | solution.py:1029
  707.9 62.4 %collective-permute-start.10 = (bf16[2,256,4096]{2,1,0:T(8,128)(2,1)}, bf16[2,256,4096]{2,1,0:T(8,128)(2,1)}, u32[]{:S(2)}, u32[]{:S(2)}) collective-permute-start(bf16[2,256,4096]{2,1,0:T(8,128)(2,1)} %get-tuple-element.147), channel_id=1, source_target_pairs={{0,4},{4,0},{8,12},{12,8},{1,5},{5,1},{9,13},{13,9},{2,6},{6,2},{1... | collective-permute-start | bytes 12582920 | tf_op jit(solution)/shard_map/ppermute | solution.py:1029
  708.2 7.4 copy-start
  754.0 3.8 copy-start.18
  755.7 2.5 copy-start.7
  755.7 2.5 copy-start.8
  755.7 2.5 copy-start.9
  757.9 18.3 %collective-permute-start.4 = (bf16[3,2,256,1024]{3,2,1,0:T(8,128)(2,1)S(1)}, bf16[3,2,256,1024]{3,2,1,0:T(8,128)(2,1)S(1)}, u32[]{:S(2)}, u32[]{:S(2)}) collective-permute-start(bf16[3,2,256,1024]{3,2,1,0:T(8,128)(2,1)S(1)} %copy-done.18), channel_id=1, source_target_pairs={{0,4},{4,0},{8,12},{12,8},{1,5},{5,1},{9,13},{13,9},{2,6},{6,2},{1... | collective-permute-start | bytes 9437192 | tf_op jit(solution)/shard_map/ppermute | solution.py:1029
  758.3 2.9 copy-start.3
  761.2 3.3 copy-start.2
  764.5 5.9 copy-start.1
  770.4 5.8 copy-start.4
  1123.4 9.4 copy-start.6
  1133.1 8.3 copy-start.11

commit v2 on v1

--- a/solution.py
+++ b/solution.py
@@ -30,6 +30,7 @@
         self.z = lax.axis_index("mp")
         self.y = lax.div(self.d, 2)
         self.c = lax.rem(self.d, 2)
+        self.nearest = sorted(range(self.MP), key=lambda r: min(r, self.MP - r))
 
     def other_y(self, r):
         return lax.rem(self.y + r, self.Y)
@@ -67,6 +68,20 @@
         else:
             pl.when(when)(copy.start)
 
+    def send_one_of(self, options, name, when, **to):
+        at = len(self.sent)
+        assert at < self.send_sems.shape[0]
+        for cond, src, dst, index in options:
+            copy = pltpu.make_async_remote_copy(
+                src_ref=src,
+                dst_ref=dst,
+                send_sem=self.send_sems.at[at],
+                recv_sem=self.arrival(name, index),
+                device_id=to,
+            )
+            pl.when(cond)(copy.start)
+        self.sent.append((copy, when))
+
     def wait(self, ref, name, index):
         pltpu.make_async_copy(ref, ref, self.arrival(name, index)).wait()
 
@@ -88,68 +103,75 @@
 
 
 def gather_counts(S, Y, MP, groups=3):
-    return dict(rows=S * MP, vectors=S * MP, piece=groups * S * Y * MP, pair=groups * S * Y * MP)
-
-
-def gather_kernel(pieces, sent_ref, vec_ref, a_ref, b_ref, c_ref, rows_ref, vecs_ref, A, B, C, send_sems, recv_sems, own_sems):
+    return dict(rows=MP, vectors=S * MP, piece=groups * S * Y * MP, pair=groups * S * Y * MP)
+
+
+def gather_kernel(pieces, sent_ref, vec_ref, a_ref, b_ref, c_ref, rows_ref, vecs_ref, *refs):
     place = Place()
     s, y, c, z, d = place.s, place.y, place.c, place.z, place.d
     S, Y, MP, H = place.S, place.Y, place.MP, place.H
+    shards = (a_ref, b_ref, c_ref)
+    wholes = (refs[0:S], refs[S : 2 * S], refs[2 * S : 3 * S])
+    send_sems, recv_sems, own_sems = refs[3 * S :]
     moves = Moves(send_sems, recv_sems, gather_counts(S, Y, MP))
     columns = sent_ref.shape[2]
-    shards, wholes = (a_ref, b_ref, c_ref), (A, B, C)
 
     def spot(g, l, yy, cc, zz):
         dd = yy * 2 + cc
-        shard, whole = shards[g], wholes[g]
+        shard, whole = shards[g], wholes[g][l]
         at = (tile(dd, shard.shape[-2]), tile(zz, shard.shape[-1]))
-        return whole.at[(l, slice(None)) + at] if len(shard.shape) == 3 else whole.at[(l,) + at]
+        return whole.at[(slice(None),) + at] if len(shard.shape) == 3 else whole.at[at]
 
     def mark(g, l, yy, zz):
         return ((g * S + l) * Y + yy) * MP + zz
 
-    def to_pair(g, l, yy, zz, src=None, when=None):
-        there = spot(g, l, yy, c, zz)
-        moves.send(
-            there if src is None else src, there, "pair", mark(g, l, yy, zz), when, section=s, dp=y * 2 + 1 - c, mp=z
+    def each(mine):
+        return [(layer, (s == layer) if mine else (s != layer)) for layer in range(S)]
+
+    def hand(g, mine, yy, zz, name, when, src, **to):
+        moves.send_one_of(
+            [
+                (
+                    cond if when is None else cond & when,
+                    spot(g, layer, yy, c, zz) if src is None else src,
+                    spot(g, layer, yy, c, zz),
+                    mark(g, layer, yy, zz),
+                )
+                for layer, cond in each(mine)
+            ],
+            name,
+            when,
+            **to,
         )
 
-    def to_rows(g, l, yy, zz, when=None, src=None):
-        there = spot(g, l, yy, c, zz)
+    def to_pair(g, mine, zz, src=None, when=None):
+        hand(g, mine, y, zz, "pair", when, src, section=s, dp=y * 2 + 1 - c, mp=z)
+
+    def to_section(g, zz, when=None, src=None):
+        hand(g, True, y, zz, "piece", when, src, section=1 - s, dp=d, mp=z)
+
+    def along(g, zz, step, when, src=None):
+        hand(g, True, y, zz, "piece", when, src, section=s, dp=d, mp=jnp.clip(z + step, 0, MP - 1))
+
+    def rows_if(g, mine, zz, first_layer, there, src=None):
+        when = first_layer | (zz < H) if g == 1 else first_layer
         for r in range(1, Y):
-            moves.send(
-                there if src is None else src, there, "piece", mark(g, l, yy, zz), when,
-                section=s, dp=place.other_y(r) * 2 + c, mp=z,
-            )
-
-    def to_section(g, l, yy, zz, when=None, src=None):
-        there = spot(g, l, yy, c, zz)
-        moves.send(there if src is None else src, there, "piece", mark(g, l, yy, zz), when, section=1 - s, dp=d, mp=z)
+            hand(g, mine, y, zz, "piece", when & there, src, section=s, dp=place.other_y(r) * 2 + c, mp=z)
 
     def landed(g, l, yy, zz):
-        moves.wait(spot(g, l, yy, c, zz), "piece", mark(g, l, yy, zz))
+        moves.wait(spot(g, 0, yy, c, zz), "piece", mark(g, l, yy, zz))
 
     own_copies = []
 
-    def near(zz):
-        return lax.div(zz, H) == lax.div(z, H)
-
-    def along(g, zz, step, when, src=None):
-        there = spot(g, s, y, c, zz)
-        moves.send(
-            there if src is None else src, there, "piece", mark(g, s, y, zz), when,
-            section=s, dp=d, mp=jnp.clip(z + step, 0, MP - 1),
-        )
-
     def columns_out(g):
-        there = spot(g, s, y, c, z)
         along(g, z, 1, z + 1 < MP, shards[g])
         along(g, z, -1, z >= 1, shards[g])
-        to_section(g, s, y, z, src=shards[g])
-        to_rows(g, s, y, z, src=shards[g])
-        to_pair(g, s, y, z, shards[g])
-        copy = pltpu.make_async_copy(shards[g], there, own_sems.at[g])
-        copy.start()
+        to_section(g, z, src=shards[g])
+        rows_if(g, True, z, s == 0, z >= 0, shards[g])
+        to_pair(g, True, z, shards[g])
+        for layer, cond in each(True):
+            copy = pltpu.make_async_copy(shards[g], spot(g, layer, y, c, z), own_sems.at[g])
+            pl.when(cond)(copy.start)
         own_copies.append(copy)
 
     def columns_in(g, far):
@@ -161,56 +183,28 @@
                 landed(g, s, y, zz)
 
             along(g, zz, step, there & ((z + 1 < MP) if step == 1 else (z >= 1)))
-            to_section(g, s, y, zz, there)
-            to_rows(g, s, y, zz, there & ((s == 0) | near(zz)))
-            to_pair(g, s, y, zz, when=there)
-
-    def far_column(k):
-        return lax.rem(lax.div(z, H) + 1, 2) * H + k
-
-    def near_column(k):
-        return lax.div(z, H) * H + k
-
-    def nearest_first():
-        return [z] + [lax.div(z, H) * H + lax.rem(z + r, H) for r in range(1, H)] + [far_column(k) for k in range(H)]
-
-    def section_in(g, which):
-        zz = nearest_first()[which]
-        landed(g, 1 - s, y, zz)
-        to_rows(g, 1 - s, y, zz, None if which >= H else s == 1)
-        to_pair(g, 1 - s, y, zz)
+            to_section(g, zz, there)
+            rows_if(g, True, zz, s == 0, there)
+            to_pair(g, True, zz, when=there)
+
+    def section_in(g, far):
+        for step, there in ((1, z >= far), (-1, z + far < MP))[: 2 if far else 1]:
+            zz = jnp.clip(z - step * far, 0, MP - 1)
+
+            @pl.when(there)
+            def _():
+                landed(g, 1 - s, y, zz)
+
+            rows_if(g, False, zz, s == 1, there)
+            to_pair(g, False, zz, when=there)
 
     def rows_in(g):
         for r in range(1, Y):
             yy = place.other_y(r)
-            for k in range(H):
-                zz = jnp.where(s == 1, near_column(k), far_column(k))
-                landed(g, 1, yy, zz)
-                to_section(g, 1, yy, zz)
-                to_pair(g, 1, yy, zz)
-            for zz in range(MP):
-                landed(g, 0, yy, zz)
-                to_pair(g, 0, yy, zz)
-
-    def corner_in(g):
-        for r in range(1, Y):
-            for k in range(H):
-                zz = jnp.where(s == 1, far_column(k), near_column(k))
-                landed(g, 1, place.other_y(r), zz)
-                to_pair(g, 1, place.other_y(r), zz)
-
-    for piece in range(pieces):
-        to_s, to_c, to_z = holder(place, c, piece)
-        here = (to_s == s) & (to_c == c) & (to_z == z)
-        there = rows_ref.at[s, :, tile(z, columns)]
-        moves.send(
-            sent_ref.at[piece], there, "rows", s * MP + z, jnp.logical_not(here),
-            section=to_s, dp=y * 2 + to_c, mp=to_z,
-        )
-
-        @pl.when(here)
-        def _():
-            pltpu.make_async_copy(sent_ref.at[piece], there, moves.arrival("rows", s * MP + z)).start()
+            for layer, zz in [(0, zz) for zz in range(MP)] + ([(1, zz) for zz in range(H)] if g == 1 else []):
+                landed(g, layer, yy, zz)
+                there = spot(g, layer, yy, c, zz)
+                moves.send(there, there, "pair", mark(g, layer, yy, zz), section=s, dp=y * 2 + 1 - c, mp=z)
 
     for q in range(1, S * MP):
         at = lax.rem(s * MP + z + q, S * MP)
@@ -220,32 +214,48 @@
 
     for g in range(3):
         columns_out(g)
-        own_copies[g].wait()
-        for far in range(1, MP):
+    for piece in range(pieces):
+        to_s, to_c, to_z = holder(place, c, piece)
+        here = (to_s == s) & (to_c == c) & (to_z == z)
+        there = rows_ref.at[:, tile(z, columns)]
+        moves.send(
+            sent_ref.at[piece], there, "rows", z, (s == 0) & jnp.logical_not(here),
+            section=to_s, dp=y * 2 + to_c, mp=to_z,
+        )
+
+        @pl.when((s == 0) & here)
+        def _():
+            pltpu.make_async_copy(sent_ref.at[piece], there, moves.arrival("rows", z)).start()
+
+    for far in range(1, MP):
+        for g in range(3):
             columns_in(g, far)
             section_in(g, far - 1)
+    for g in range(3):
         section_in(g, MP - 1)
-        if g:
-            rows_in(g - 1)
-            corner_in(g - 1)
-    rows_in(2)
-    corner_in(2)
+    for g in range(3):
+        rows_in(g)
 
     @pl.when(s * MP + z < pieces)
     def _():
-        for section in range(S):
-            for zz in range(MP):
-                moves.wait(rows_ref.at[section, :, tile(zz, columns)], "rows", section * MP + zz)
+        for zz in range(MP):
+            moves.wait(rows_ref.at[:, tile(zz, columns)], "rows", zz)
 
     for q in range(1, S * MP):
         at = lax.rem(s * MP + z + q, S * MP)
         moves.wait(vecs_ref.at[at], "vectors", at)
     for g in range(3):
-        for l in range(S):
-            for yy in range(Y):
-                for zz in range(MP):
-                    moves.wait(spot(g, l, yy, 1 - c, zz), "pair", mark(g, l, yy, zz))
+        for zz in range(MP):
+            for r in range(Y):
+                yy = place.other_y(r)
+                moves.wait(spot(g, 0, yy, 1 - c, zz), "pair", mark(g, 0, yy, zz))
+                if g == 1 and zz < H and r:
+                    moves.wait(spot(g, 1, yy, 1 - c, zz), "pair", mark(g, 1, yy, zz))
+            for layer in range(1, S):
+                moves.wait(spot(g, 0, y, 1 - c, zz), "pair", mark(g, layer, y, zz))
     own_vec.wait()
+    for copy in own_copies:
+        copy.wait()
     moves.finish()
 
 
@@ -254,18 +264,19 @@
     Y = DP // 2
     pieces, rows, columns = sent.shape
     counts = gather_counts(S, Y, MP)
-    sends = pieces + S * MP - 1 + 3 * (2 * MP + (1 + 2 * (MP - 1)) * (1 + Y) + MP * Y + (Y - 1) * (MP + 3 * (MP // 2)))
-    return pl.pallas_call(
+    sends = pieces + S * MP - 1 + 3 * (2 * MP + (2 * MP - 1) * (1 + 2 * Y) + (Y - 1) * MP) + (Y - 1) * (MP // 2)
+    whole = [
+        jax.ShapeDtypeStruct(shard.shape[:-2] + (shard.shape[-2] * DP, shard.shape[-1] * MP), LOW) for shard in (a, b, c)
+    ]
+    got = pl.pallas_call(
         functools.partial(gather_kernel, pieces),
         in_specs=[HBM] * 5,
-        out_specs=[HBM] * 5,
+        out_specs=[HBM] * (2 + 3 * S),
         out_shape=[
-            jax.ShapeDtypeStruct((S, rows, columns * MP), LOW),
+            jax.ShapeDtypeStruct((rows, columns * MP), LOW),
             jax.ShapeDtypeStruct((S * MP,) + vec.shape, WIDE),
-            jax.ShapeDtypeStruct((S, a.shape[0], a.shape[1] * DP, a.shape[2] * MP), LOW),
-            jax.ShapeDtypeStruct((S, b.shape[0] * DP, b.shape[1] * MP), LOW),
-            jax.ShapeDtypeStruct((S, c.shape[0] * DP, c.shape[1] * MP), LOW),
-        ],
+        ]
+        + [shape for shape in whole for _ in range(S)],
         scratch_shapes=[
             pltpu.SemaphoreType.DMA((sends,)),
             pltpu.SemaphoreType.DMA((sum(counts.values()),)),
@@ -273,14 +284,13 @@
         ],
         compiler_params=pltpu.CompilerParams(has_side_effects=True),
     )(sent, vec, a, b, c)
+    return got[0], got[1], [[got[2 + g * S + layer] for g in range(3)] for layer in range(S)]
 
 
 def scatter_counts(S, Y, MP, pieces, groups=4):
-    H = MP // 2
     return dict(
         back=max(pieces, MP),
-        corner_x=groups * (Y - 1) * H,
-        corner_y=groups * (Y - 1) * H,
+        pair=groups * Y * MP,
         from_x=groups * MP,
         from_y=groups * (Y - 1) * MP,
         from_z=groups * MP,
@@ -291,32 +301,55 @@
     )
 
 
-ORDER = (3, 2, 1, 0)
-
-
-def scatter_kernel(
-    pieces, table_ref, first_ref, last_ref, *refs
-):
+ORDER = (3, 2, 0, 1)
+
+
+def scatter_kernel(pieces, table_ref, first_ref, last_ref, *refs):
     place = Place()
     s, y, c, z, d = place.s, place.y, place.c, place.z, place.d
-    S, Y, MP, H = place.S, place.Y, place.MP, place.H
-    grads = (refs[0:2], refs[2:4], refs[4:6], refs[6:8])
-    ends_ref, sums_ref, outs = refs[8], refs[9], refs[10:14]
-    mine, over, across, corner_x, corner_y, from_x, from_y, from_z = (refs[14 + 4 * i : 18 + 4 * i] for i in range(8))
-    send_sems, recv_sems, load_sems, vec_here, vec_pair, vec_x, vec_y, vec_z = refs[46:]
+    S, Y, MP = place.S, place.Y, place.MP
+    own, there, above = refs[0:4], refs[4:8], refs[8:12]
+    ends_ref, sums_ref, outs = refs[12], refs[13], refs[14:18]
+    held, paired, mine, from_x, from_y, from_z = (refs[18 + 4 * i : 22 + 4 * i] for i in range(6))
+    send_sems, recv_sems, load_sems, vec_here, vec_pair, vec_x, vec_y, vec_z, landing = refs[42:]
     moves = Moves(send_sems, recv_sems, scatter_counts(S, Y, MP, pieces))
-    block = first_ref.shape[2]
-
-    def part(g, l, yy, zz):
-        ref = grads[g][l]
-        piece = outs[g].shape
-        at = (yy, slice(None), tile(zz, piece[-1]))
-        return ref.at[(slice(None),) + at] if len(piece) == 3 else ref.at[at]
+
+    def part(ref, g, zz, yy=None):
+        at = (slice(None), tile(zz, outs[g].shape[-1]))
+        if yy is not None:
+            at = (yy,) + at
+        if len(outs[g].shape) == 3:
+            at = (slice(None),) + at
+        return ref.at[at]
 
     moves.send(table_ref.at[1 - c], vec_pair, "vec_pair", 0, section=s, dp=y * 2 + 1 - c, mp=z)
     moves.wait(vec_pair, "vec_pair", 0)
     vec_here[...] = table_ref[c] + vec_pair[...]
     moves.send(vec_here.at[1 - s], vec_x, "vec_x", 0, section=1 - s, dp=d, mp=z)
+
+    loads = {}
+
+    def load(src, dst, when, key):
+        at = len(loads)
+        copy = pltpu.make_async_copy(src, dst, load_sems.at[at])
+        if when is None:
+            copy.start()
+        else:
+            pl.when(when)(copy.start)
+        loads[key] = (copy, when)
+
+    steps = [(g, k) for g in ORDER for k in place.nearest[::-1]]
+    for g, k in steps:
+        zz = place.other_z(k)
+        for r in list(range(1, Y)) + [0]:
+            slot = place.other_y(r) * MP + zz
+            moves.send(
+                part(there[g], g, zz, place.other_y(r)), paired[g].at[slot], "pair", g * Y * MP + slot,
+                section=s, dp=y * 2 + 1 - c, mp=z,
+            )
+            load(part(own[g], g, zz, place.other_y(r)), held[g].at[slot], None, ("own", g, k, r))
+        load(part(above[g], g, zz), mine[g].at[zz], s == 1, ("above", g, k))
+
     moves.wait(vec_x, "vec_x", 0)
     vec_here[s] = vec_here[s] + vec_x[...]
     for r in range(1, Y):
@@ -329,11 +362,6 @@
     vec_here[s, y] = vec_here[s, y] + jnp.sum(vec_y[...], 0)
     for r in range(1, MP):
         moves.send(vec_here.at[s, y, place.other_z(r)], vec_z.at[z], "vec_z", z, section=s, dp=d, mp=place.other_z(r))
-    vec_total = vec_here[s, y, z]
-    for r in range(1, MP):
-        moves.wait(vec_z.at[place.other_z(r)], "vec_z", place.other_z(r))
-        vec_total = vec_total + vec_z[place.other_z(r)]
-    sums_ref[...] = vec_total
 
     number = s * MP + z
     active = number < pieces
@@ -342,77 +370,25 @@
         for zz in range(MP):
             to_c = lax.rem(number, 2)
             here = (s == section) & (to_c == c) & (z == zz)
-            there = ends_ref.at[piece]
+            dst = landing.at[piece]
             moves.send(
-                ref.at[zz], there, "back", piece, active & jnp.logical_not(here), section=section, dp=y * 2 + to_c, mp=zz
+                ref.at[zz], dst, "back", piece, active & jnp.logical_not(here), section=section, dp=y * 2 + to_c, mp=zz
             )
 
             @pl.when(active & here)
             def _():
-                pltpu.make_async_copy(ref.at[zz], there, moves.arrival("back", piece)).start()
-
-    loads = []
-
-    def by_section(g, mine_too, yy, zz, use):
-        for layer in range(S):
-            pl.when((s == layer) if mine_too else (s != layer))(lambda: use(part(g, layer, yy, zz)))
-
-    def send_part(g, mine_too, yy, zz, dst, name, index, **to):
-        at = len(moves.sent)
-        sample = part(g, 0, yy, zz)
-
-        def go(ref):
-            pltpu.make_async_remote_copy(
-                src_ref=ref, dst_ref=dst, send_sem=send_sems.at[at], recv_sem=moves.arrival(name, index), device_id=to
-            ).start()
-
-        by_section(g, mine_too, yy, zz, go)
-        moves.sent.append(
-            (
-                pltpu.make_async_remote_copy(
-                    src_ref=sample, dst_ref=dst, send_sem=send_sems.at[at], recv_sem=moves.arrival(name, index), device_id=to
-                ),
-                None,
-            )
-        )
-
-    def load(g, mine_too, yy, zz, dst):
-        at = len(loads)
-        by_section(g, mine_too, yy, zz, lambda ref: pltpu.make_async_copy(ref, dst, load_sems.at[at]).start())
-        loads.append(pltpu.make_async_copy(dst, dst, load_sems.at[at]))
-        return at
-
-    over_at, across_at, mine_at = {}, {}, {}
-    for g in ORDER:
-        for r in range(1, Y):
-            for k in range(H):
-                slot = ((r - 1) * H) + k
-                send_part(
-                    g, False, place.other_y(r), k, corner_x[g].at[slot], "corner_x", g * (Y - 1) * H + slot,
-                    section=1 - s, dp=d, mp=z,
-                )
-                back = (Y - r) % Y
-                send_part(
-                    g, False, place.other_y(r), H + k, corner_y[g].at[(back - 1) * H + k], "corner_y",
-                    g * (Y - 1) * H + (back - 1) * H + k,
-                    section=s, dp=place.other_y(r) * 2 + c, mp=z,
-                )
-        for k in range(H):
-            over_at[g, k] = load(g, False, y, H + k, over[g].at[k])
-            for r in range(1, Y):
-                across_at[g, r, k] = load(g, True, place.other_y(r), k, across[g].at[(r - 1) * H + k])
-        for k in range(H):
-            send_part(g, False, y, k, from_x[g].at[k], "from_x", g * MP + k, section=1 - s, dp=d, mp=z)
-            for r in range(1, Y):
-                back = (Y - r) % Y
-                slot = (back - 1) * MP + H + k
-                send_part(
-                    g, True, place.other_y(r), H + k, from_y[g].at[slot], "from_y", g * (Y - 1) * MP + slot,
-                    section=s, dp=place.other_y(r) * 2 + c, mp=z,
-                )
-    for g in ORDER:
-        for zz in range(MP):
-            mine_at[g, zz] = load(g, True, y, zz, mine[g].at[zz])
+                pltpu.make_async_copy(ref.at[zz], dst, moves.arrival("back", piece)).start()
+
+    for g, k in steps:
+        zz = place.other_z(k)
+        moves.send(part(above[g], g, zz), from_x[g].at[zz], "from_x", g * MP + zz, s == 0, section=1 - s, dp=d, mp=z)
+
+    def loaded(key):
+        copy, when = loads[key]
+        if when is None:
+            copy.wait()
+        else:
+            pl.when(when)(copy.wait)
 
     def add_into(dst, *terms):
         total = dst[...].astype(WIDE)
@@ -420,89 +396,121 @@
             total = total + term[...].astype(WIDE)
         dst[...] = total.astype(LOW)
 
-    for g in ORDER:
-        for k in range(H):
-            for r in range(1, Y):
-                slot = (r - 1) * H + k
-                moves.wait(corner_x[g].at[slot], "corner_x", g * (Y - 1) * H + slot)
-                loads[across_at[g, r, k]].wait()
-                add_into(across[g].at[slot], corner_x[g].at[slot])
-                back = (Y - r) % Y
-                out = (back - 1) * MP + k
+    def pair_step(g, k):
+        zz = place.other_z(k)
+        for r in list(range(1, Y)) + [0]:
+            slot = place.other_y(r) * MP + zz
+            moves.wait(paired[g].at[slot], "pair", g * Y * MP + slot)
+            loaded(("own", g, k, r))
+            if r:
+                add_into(held[g].at[slot], paired[g].at[slot])
+                out = (Y - r - 1) * MP + zz
                 moves.send(
-                    across[g].at[slot], from_y[g].at[out], "from_y", g * (Y - 1) * MP + out,
+                    held[g].at[slot], from_y[g].at[out], "from_y", g * (Y - 1) * MP + out,
                     section=s, dp=place.other_y(r) * 2 + c, mp=z,
                 )
-            for r in range(1, Y):
-                slot = (r - 1) * H + k
-                moves.wait(corner_y[g].at[slot], "corner_y", g * (Y - 1) * H + slot)
-            loads[over_at[g, k]].wait()
-            add_into(over[g].at[k], *(corner_y[g].at[(r - 1) * H + k] for r in range(1, Y)))
-            moves.send(over[g].at[k], from_x[g].at[H + k], "from_x", g * MP + H + k, section=1 - s, dp=d, mp=z)
-
-    for g in ORDER:
-        for zz in list(range(H)) + list(range(H, MP)):
-            moves.wait(from_x[g].at[zz], "from_x", g * MP + zz)
-            for r in range(1, Y):
-                slot = (r - 1) * MP + zz
-                moves.wait(from_y[g].at[slot], "from_y", g * (Y - 1) * MP + slot)
-            loads[mine_at[g, zz]].wait()
-            add_into(mine[g].at[zz], from_x[g].at[zz], *(from_y[g].at[(r - 1) * MP + zz] for r in range(1, Y)))
-            moves.send(
-                mine[g].at[zz], from_z[g].at[z], "from_z", g * MP + z, z != zz, section=s, dp=d, mp=zz
-            )
-
-    for g in ORDER:
+
+    def rows_step(g, k):
+        zz = place.other_z(k)
+        slot = y * MP + zz
+        slots = [(r - 1) * MP + zz for r in range(1, Y)]
+        for at in slots:
+            moves.wait(from_y[g].at[at], "from_y", g * (Y - 1) * MP + at)
+        add_into(held[g].at[slot], paired[g].at[slot], *(from_y[g].at[at] for at in slots))
+        moves.send(held[g].at[slot], from_x[g].at[zz], "from_x", g * MP + zz, s == 1, section=1 - s, dp=d, mp=z)
+
+    def section_step(g, k):
+        zz = place.other_z(k)
+        moves.wait(from_x[g].at[zz], "from_x", g * MP + zz)
+        loaded(("above", g, k))
+
+        @pl.when(s == 0)
+        def _():
+            total = held[g][y * MP + zz].astype(WIDE) + from_x[g][zz].astype(WIDE)
+            mine[g][zz] = total.astype(LOW)
+
+        @pl.when(s == 1)
+        def _():
+            add_into(mine[g].at[zz], from_x[g].at[zz])
+
+        if k:
+            moves.send(mine[g].at[zz], from_z[g].at[z], "from_z", g * MP + z, section=s, dp=d, mp=zz)
+
+    def columns_step(g):
         total = mine[g][z].astype(WIDE)
-        for r in range(1, MP):
-            zz = place.other_z(r)
+        for k in range(1, MP):
+            zz = place.other_z(k)
             moves.wait(from_z[g].at[zz], "from_z", g * MP + zz)
             total = total + from_z[g][zz].astype(WIDE)
         outs[g][...] = total
 
+    early, lag = 4, 2
+    for at in range(-early, len(steps) + lag):
+        if at + early < len(steps):
+            pair_step(*steps[at + early])
+        if 0 <= at < len(steps):
+            rows_step(*steps[at])
+        if at >= lag:
+            section_step(*steps[at - lag])
+        if at == 1:
+            total = vec_here[s, y, z]
+            for r in range(1, MP):
+                moves.wait(vec_z.at[place.other_z(r)], "vec_z", place.other_z(r))
+                total = total + vec_z[place.other_z(r)]
+            sums_ref[...] = total
+
+    rows = landing.shape[1]
+    rest = ends_ref.shape[1] - rows
     for p in range(pieces):
-        moves.wait(ends_ref.at[p], "back", p)
+        moves.wait(landing.at[p], "back", p)
+        if p % 2 == 0:
+            ends_ref[p // 2, 0:rows] = landing[p]
+        else:
+            ends_ref[p // 2, rows:] = landing[p][:rest]
+
+    for g in ORDER:
+        columns_step(g)
     moves.finish()
 
 
-def scatter(table, first, last, grads, shapes):
+def scatter(table, first, last, grads, shapes, ends_shape):
     S, DP, MP = (lax.axis_size(name) for name in ("section", "dp", "mp"))
-    Y, H = DP // 2, MP // 2
+    Y = DP // 2
     _, rows, block = first.shape
     pieces = grads["pieces"]
-    flat = [grads[name][layer] for name in ("qkv", "out", "fc1", "fc2") for layer in range(S)]
+    names = ("qkv", "out", "fc1", "fc2")
+    flat = [grads["own"][n] for n in names] + [grads["there"][n] for n in names] + [grads["above"][n] for n in names]
     counts = scatter_counts(S, Y, MP, pieces)
     vmem = pl.BlockSpec(memory_space=pltpu.VMEM)
 
     def room(count):
         return [pltpu.VMEM((count,) + shape, LOW) for shape in shapes]
 
-    sends = 2 + Y - 1 + MP - 1 + S * MP + 4 * ((Y - 1) * H * 2 + H * Y + H * Y + MP)
+    sends = 2 + Y - 1 + MP - 1 + S * MP + 4 * (Y * MP + (Y - 1) * MP + 2 * MP + MP - 1)
     return pl.pallas_call(
         functools.partial(scatter_kernel, pieces),
         in_specs=[vmem] + [HBM] * (2 + len(flat)),
-        out_specs=[HBM] + [vmem] * 5,
-        out_shape=[jax.ShapeDtypeStruct((pieces, rows, block), LOW), jax.ShapeDtypeStruct(table.shape[4:], WIDE)]
+        out_specs=[vmem] * 6,
+        out_shape=[jax.ShapeDtypeStruct(ends_shape, LOW), jax.ShapeDtypeStruct(table.shape[4:], WIDE)]
         + [jax.ShapeDtypeStruct(shape, WIDE) for shape in shapes],
-        scratch_shapes=room(MP)
-        + room(H)
-        + room((Y - 1) * H)
-        + room((Y - 1) * H)
-        + room((Y - 1) * H)
+        scratch_shapes=room(Y * MP)
+        + room(Y * MP)
+        + room(MP)
         + room(MP)
         + room((Y - 1) * MP)
         + room(MP)
         + [
             pltpu.SemaphoreType.DMA((sends,)),
             pltpu.SemaphoreType.DMA((sum(counts.values()),)),
-            pltpu.SemaphoreType.DMA((4 * (H * Y + MP),)),
+            pltpu.SemaphoreType.DMA((4 * (Y + 1) * MP,)),
             pltpu.VMEM(table.shape[1:], WIDE),
             pltpu.VMEM(table.shape[1:], WIDE),
             pltpu.VMEM(table.shape[2:], WIDE),
             pltpu.VMEM((Y - 1,) + table.shape[3:], WIDE),
             pltpu.VMEM(table.shape[3:], WIDE),
+            pltpu.VMEM((pieces, rows, block), LOW),
         ],
-        compiler_params=pltpu.CompilerParams(has_side_effects=True, vmem_limit_bytes=60 << 20),
+        compiler_params=pltpu.CompilerParams(has_side_effects=True, vmem_limit_bytes=63 << 20),
     )(table, first, last, *flat)
 
 
@@ -552,7 +560,7 @@
         out_shape=[shape for _, shape in outs],
         scratch_shapes=scratch,
         compiler_params=pltpu.CompilerParams(vmem_limit_bytes=58 << 20),
-        cost_estimate=pl.CostEstimate(flops=flops, bytes_accessed=40 << 20, transcendentals=0),
+        cost_estimate=pl.CostEstimate(flops=1000, bytes_accessed=1000, transcendentals=0),
     )(*args)
 
 
@@ -584,7 +592,7 @@
         q_ref[...] = (value + vec_ref[B_QUERY][None]).astype(LOW)
 
 
-def project(rows_in, vec, attn, layer):
+def project(rows_in, vec, attn):
     rows, width = rows_in.shape
     low = jax.ShapeDtypeStruct((rows, width), LOW)
     return compute_call(
@@ -593,7 +601,7 @@
         [
             full(rows_in.shape),
             full(vec.shape),
-            pl.BlockSpec((None, None, width, width), lambda i: (layer, lax.rem(i + 1, 3), 0, 0)),
+            pl.BlockSpec((None, width, width), lambda i: (lax.rem(i + 1, 3), 0, 0)),
         ],
         [
             (full(rows_in.shape), low),
@@ -682,14 +690,14 @@
 CHUNK = 512
 
 
-def mlp(rows_in, out, vec, bias, weights, layer):
+def mlp(rows_in, out, vec, bias, weights):
     attn, fc1, fc2 = weights
     rows, width = rows_in.shape
-    hidden = fc1.shape[2]
+    hidden = fc1.shape[1]
     low = (full(rows_in.shape), jax.ShapeDtypeStruct((rows, width), LOW))
     wide = (full(rows_in.shape), jax.ShapeDtypeStruct((rows, width), WIDE))
     units = (pl.BlockSpec((rows, CHUNK), lambda i: (0, i)), jax.ShapeDtypeStruct((rows, hidden), LOW))
-    weight = pl.BlockSpec((None, width, CHUNK), lambda i: (layer, 0, i))
+    weight = pl.BlockSpec((width, CHUNK), lambda i: (0, i))
     return compute_call(
         mlp_kernel,
         hidden // CHUNK,
@@ -698,7 +706,7 @@
             full(rows_in.shape),
             full(vec.shape),
             pl.BlockSpec((8, CHUNK), lambda i: (0, i)),
-            pl.BlockSpec((None, None, width, width), lambda i: (layer, 3, 0, 0)),
+            pl.BlockSpec((None, width, width), lambda i: (3, 0, 0)),
             weight,
             weight,
         ],
@@ -728,7 +736,7 @@
 
 def mlp_back_kernel(
     c_ref, dy_ref, vec_ref, two_ref, act_ref, slope_ref, n_ref, middle_ref, branch_ref, o_ref, wo_ref, w1_ref, w2_ref,
-    grad_ref, do_ref, own1, there1, own2, there2, own_o, there_o, sums_ref, units_ref, dm, total,
+    grad_ref, do_ref, own1, there1, own2, there2, own_o, there_o, sums_ref, units_ref, dm, dm_t, n_t, total,
 ):
     step = pl.program_id(0)
     even = c_ref[0] == 0
@@ -737,14 +745,16 @@
     def _():
         low = (dy_ref[...] * vec_ref[SCALE_MLP][None]).astype(LOW)
         dm[...] = low
+        dm_t[...] = low.T
+        n_t[...] = n_ref[...].T
         sums_ref[0:1] = column_sum(dy_ref[...] * two_ref[...].astype(WIDE))
         sums_ref[1:2] = column_sum(low)
         total[...] = jnp.zeros_like(total)
 
     df = (nn(dm[...], w2_ref[...]) * slope_ref[...].astype(WIDE)).astype(LOW)
     units_ref[...] = jnp.broadcast_to(column_sum(df), units_ref.shape)
-    store_halves(tn(dm[...], act_ref[...]), even, own2, there2)
-    store_halves(tn(n_ref[...], df), even, own1, there1)
+    store_halves(nn(dm_t[...], act_ref[...]), even, own2, there2)
+    store_halves(nn(n_t[...], df), even, own1, there1)
     total[...] += nt(df, w1_ref[...])
 
     @pl.when(step == pl.num_programs(0) - 1)
@@ -762,16 +772,16 @@
         store_halves(tn(da, o_ref[...]), even, own_o, there_o)
 
 
-def mlp_back(half, dy, vec, saved, weights, layer, count):
+def mlp_back(half, dy, vec, saved, weights, count):
     attn, fc1, fc2 = weights
     rows, width = dy.shape
-    hidden = fc1.shape[2]
+    hidden = fc1.shape[1]
     block = width // (2 * count)
     whole = full(dy.shape)
     low = (whole, jax.ShapeDtypeStruct((rows, width), LOW))
     wide = (whole, jax.ShapeDtypeStruct((rows, width), WIDE))
     units = pl.BlockSpec((rows, CHUNK), lambda i: (0, i))
-    weight = pl.BlockSpec((None, width, CHUNK), lambda i: (layer, 0, i))
+    weight = pl.BlockSpec((width, CHUNK), lambda i: (0, i))
     grad = (
         pl.BlockSpec((count, block, CHUNK), lambda i: (0, 0, i)),
         jax.ShapeDtypeStruct((count, block, hidden), LOW),
@@ -791,7 +801,7 @@
             whole,
             whole,
             whole,
-            pl.BlockSpec((None, None, width, width), lambda i: (layer, 3, 0, 0)),
+            pl.BlockSpec((None, width, width), lambda i: (3, 0, 0)),
             weight,
             weight,
         ],
@@ -807,7 +817,12 @@
             (full((8, width)), jax.ShapeDtypeStruct((8, width), WIDE)),
             (pl.BlockSpec((8, CHUNK), lambda i: (0, i)), jax.ShapeDtypeStruct((8, hidden), WIDE)),
         ],
-        [pltpu.VMEM((rows, width), LOW), pltpu.VMEM((rows, width), WIDE)],
+        [
+            pltpu.VMEM((rows, width), LOW),
+            pltpu.VMEM((width, rows), LOW),
+            pltpu.VMEM((width, rows), LOW),
+            pltpu.VMEM((rows, width), WIDE),
+        ],
         8 * rows * width * hidden,
         (
             half,
@@ -872,7 +887,7 @@
 
 
 def project_back_kernel(
-    c_ref, d0_ref, d1_ref, n_ref, x_ref, grad_ref, vec_ref, w_ref, dx_ref, own, there, sums_ref, total
+    c_ref, d0_ref, d1_ref, n_ref, x_ref, grad_ref, vec_ref, w_ref, dx_ref, own, there, sums_ref, n_t, total
 ):
     step = pl.program_id(0)
     even = c_ref[0] == 0
@@ -880,10 +895,11 @@
     @pl.when(step == 0)
     def _():
         total[...] = jnp.zeros_like(total)
+        n_t[...] = n_ref[...].T
 
     theirs = jnp.where(step == 0, 0.0, d1_ref[...].astype(WIDE))
     grad = (d0_ref[...].astype(WIDE) + theirs).astype(LOW)
-    store_halves(tn(n_ref[...], grad), even, own, there)
+    store_halves(nn(n_t[...], grad), even, own, there)
     total[...] += nt(grad, w_ref[...])
     sums = column_sum(grad)
 
@@ -901,7 +917,7 @@
         dx_ref[...] = grad_ref[...] + d_rows
 
 
-def project_back(half, d0, d1, saved, grad, vec, attn, layer, count):
+def project_back(half, d0, d1, saved, grad, vec, attn, count):
     rows, width = grad.shape
     block = width // (2 * count)
     whole = full(grad.shape)
@@ -920,7 +936,7 @@
             whole,
             whole,
             full(vec.shape),
-            pl.BlockSpec((None, None, width, width), lambda i: (layer, i, 0, 0)),
+            pl.BlockSpec((None, width, width), lambda i: (i, 0, 0)),
         ],
         [
             (whole, jax.ShapeDtypeStruct((rows, width), WIDE)),
@@ -928,7 +944,7 @@
             out,
             (full((8, width)), jax.ShapeDtypeStruct((8, width), WIDE)),
         ],
-        [pltpu.VMEM((rows, width), WIDE)],
+        [pltpu.VMEM((width, rows), LOW), pltpu.VMEM((rows, width), WIDE)],
         12 * rows * width * width,
         (half, d0, d1, saved["n_one"], saved["rows_in"], grad, vec, attn),
     )
@@ -938,11 +954,17 @@
     return lax.dynamic_index_in_dim(stack, index, axis, keepdims=False)
 
 
-def layer_forward(rows_in, vec, bias, weights, layer, mask, from_pair):
-    n_one, kv0, q = project(rows_in, vec, weights[0], layer)
+def after(value, *others):
+    return lax.optimization_barrier((value,) + others)[0]
+
+
+def layer_forward(rows_in, vec, bias, weights, mask, from_pair, meanwhile):
+    n_one, kv0, q = project(rows_in, vec, weights[0])
     kv1 = from_pair(kv0)
     out, out_wide, probs = attend(q, kv0, kv1, mask)
-    leaving, branch, middle, n_two, active, slope, two = mlp(rows_in, out, vec, bias, weights, layer)
+    out = meanwhile(0, q, out)
+    leaving, branch, middle, n_two, active, slope, two = mlp(rows_in, out, vec, bias, weights)
+    leaving = meanwhile(1, out, leaving)
     saved = dict(
         rows_in=rows_in,
         n_one=n_one,
@@ -962,21 +984,23 @@
     return (leaving, saved)
 
 
-def layer_backward(grad_rows, saved, vec, weights, layer, half, from_pair):
+def layer_backward(grad_rows, saved, vec, weights, half, from_pair, sums_over, meanwhile):
     count = lax.axis_size("dp") // 2
     grad_middle, d_out, own1, there1, own2, there2, own_o, there_o, sums, units = mlp_back(
-        half, grad_rows, vec, saved, weights, layer, count
-    )
-
-    def joined(own, there):
-        return (own.astype(WIDE) + from_pair(there).astype(WIDE)).astype(LOW)
-
-    g_fc2, g_fc1, g_out = joined(own2, there2), joined(own1, there1), joined(own_o, there_o)
+        half, grad_rows, vec, saved, weights, count
+    )
+    d_out = meanwhile("fc2", grad_rows, d_out)
     d0, d1 = attend_back(saved["q"], saved["kv0"], saved["kv1"], saved["probs"], d_out, saved["out_wide"])
-    grad_in, own, there, sums_one = project_back(
-        half, d0, from_pair(d1), saved, grad_middle, vec, weights[0], layer, count
-    )
-    g_qkv = joined(own, there)
+    own, there = dict(out=own_o, fc1=own1, fc2=own2), dict(out=there_o, fc1=there1, fc2=there2)
+    d0 = meanwhile("fc1", d_out, d0)
+    d1 = from_pair(d1)
+    d0 = sums_over(own, there, d0)
+    grad_in, own["qkv"], there["qkv"], sums_one = project_back(
+        half, d0, d1, saved, grad_middle, vec, weights[0], count
+    )
+    grad_in = sums_over(dict(qkv=own["qkv"]), dict(qkv=there["qkv"]), grad_in)
+    grad_in = meanwhile("out", d0, grad_in)
+    grad_in = meanwhile("qkv", d0, grad_in)
     vectors = dict(
         ln1_gain=sums_one[2],
         ln1_bias=sums_one[3],
@@ -990,7 +1014,7 @@
         b_fc2=sums[1],
         scale_mlp=sums[0],
     )
-    return (grad_in, dict(qkv=g_qkv, out=g_out, fc1=g_fc1, fc2=g_fc2), vectors)
+    return (grad_in, own, there, vectors)
 
 
 NARROW = ("ln1_gain", "ln1_bias", "b_query", "b_value", "b_out", "scale_attn", "ln2_gain", "ln2_bias", "b_fc2", "scale_mlp")
@@ -1028,6 +1052,91 @@
     def from_pair(value):
         return lax.ppermute(value, "dp", [(i, i + 1 - 2 * (i % 2)) for i in range(DP)])
 
+    def from_row(value, r):
+        return lax.ppermute(value, "dp", [(i, (i - 2 * r) % DP) for i in range(DP)])
+
+    turns = max(pieces, MP)
+    spots = [(i, j, k) for i in range(S) for j in range(DP) for k in range(MP)]
+
+    def move(value, target):
+        number_of = {spot: i for i, spot in enumerate(spots)}
+        pairs = [(number_of[spot], number_of[target(*spot)]) for spot in spots if target(*spot) is not None]
+        return lax.ppermute(value, ("section", "dp", "mp"), pairs)
+
+    def bring(blocks, which, began):
+        got = []
+        for turn in which:
+
+            def target(i, j, k, turn=turn):
+                piece = (turn + k) % turns
+                image = 2 * (piece // 2) + j % 2
+                if i != 1 or piece >= pieces:
+                    return None
+                return (image // MP, j // 2 * 2 + piece % 2, image % MP)
+
+            piece = jnp.minimum(lax.rem(place.z + turn, turns), pieces - 1)
+            got.append(move(after(pick(blocks, piece), began), target))
+        return got
+
+    def brought(got):
+        here = 2 * lax.div(number, 2) + place.c
+        stack = jnp.stack(got)
+        return jnp.concatenate([pick(stack, lax.rem(here + turns - zz % turns, turns)) for zz in range(MP)], 1)
+
+    def by_column(value):
+        return jnp.stack([value[:, i * columns : (i + 1) * columns].astype(LOW) for i in range(MP)])
+
+    waiting, above = {}, {}
+
+    def sums_over(own, there, before):
+        parts = []
+        for name in own:
+            axis = own[name].ndim - 3
+            got = from_pair(there[name])
+
+            def row(r, value=own[name], got=got, axis=axis):
+                at = lax.rem(place.y + r, DP // 2)
+                return pick(value, at, axis).astype(WIDE) + pick(got, at, axis).astype(WIDE)
+
+            others = [row(r).astype(LOW) for r in range(1, DP // 2)]
+            parts += others
+            waiting[name] = (row, others)
+        return after(before, *parts)
+
+    def rows_meanwhile(name, before, done):
+        row, others = waiting[name]
+        got = [from_row(after(part, before), DP // 2 - r) for r, part in enumerate(others, 1)]
+        got, done = lax.optimization_barrier((got, done))
+        above[name] = (row, got)
+        return done
+
+    def sums_done(name):
+        row, got = above[name]
+        total = row(0)
+        for other in got:
+            total = total + other.astype(WIDE)
+        return total.astype(LOW)
+
+    def first_unit(at, weight):
+        return weight.shape[-1] // 2 if at == 1 else 0
+
+    def own_block(at, weight):
+        axis, block = weight.ndim - 2, weight.shape[-2] // DP
+        weight = weight[..., first_unit(at, weight) :]
+        return lax.dynamic_slice_in_dim(weight, place.d * block, block, axis)
+
+    def fill_rows(layer, at, weight, began, done):
+        axis, block = weight.ndim - 2, weight.shape[-2] // DP
+        value = after(sliced[layer][at], began)
+        for r in range(1, DP // 2):
+            got, done = lax.optimization_barrier((from_row(value, r), done))
+            row = lax.rem(place.y + r, DP // 2) * 2
+            for rows_of, part in ((row + place.c, got), (row + 1 - place.c, from_pair(got))):
+                start = [jnp.int32(0)] * weight.ndim
+                start[axis], start[-1] = rows_of * block, jnp.int32(first_unit(at, weight))
+                weight = lax.dynamic_update_slice(weight, part, start)
+        return weight, done
+
     images_low = boundary.reshape(micros, seq_len, columns).astype(LOW)
     sent = jnp.pad(images_low, ((0, 0), (0, 2 * rows - seq_len), (0, 0))).reshape(pieces, rows, columns)
     keys = jnp.arange(rows)[:, None] + rows * jnp.stack([place.c, 1 - place.c])[None]
@@ -1039,7 +1148,9 @@
     lines = -(-packed.shape[0] // 1024) * 8
     packed = jnp.pad(packed, (0, lines * 128 - packed.shape[0])).reshape(lines, 128)
     attn_shard = jnp.stack([w_query[0], w_key[0], w_value[0], w_out[0].T])
-    arrived, vecs, *weights = gather(sent, packed, attn_shard, w_fc1[0], w_fc2[0].T)
+    arrived, vecs, weights = gather(sent, packed, attn_shard, w_fc1[0], w_fc2[0].T)
+    sliced = {layer: [own_block(at, w) for at, w in enumerate(weights[layer])] for layer in range(1, S)}
+    arrived = after(arrived, *(w for layer in sliced for w in sliced[layer]))
     arrived = jnp.where(active, arrived.astype(WIDE), 0.0)
     vecs = vecs.reshape(S, MP, -1)
     vectors, biases = [], []
@@ -1051,29 +1162,41 @@
         bias = vecs[layer, :, start : start + b_fc1.shape[1]].reshape(1, -1)
         biases.append(jnp.pad(bias, ((0, 7), (0, 0))))
 
-    saved = []
-    rows_now = arrived[0]
+    saved, cotangent = [], []
+    split = [range(turns)[i * turns // 3 : (i + 1) * turns // 3] for i in range(3)]
+    rows_now = arrived
     for layer in range(S):
-        rows_now, kept = layer_forward(rows_now, vectors[layer], biases[layer], weights, layer, mask, from_pair)
+        def meanwhile(stage, before, done, layer=layer):
+            at = 2 * layer + stage
+            if at > 2:
+                return done
+            few, done = lax.optimization_barrier((bring(sent, split[at], before), done))
+            cotangent.extend(few)
+            weights[1][at], done = fill_rows(1, at, weights[1][at], before, done)
+            return done
+
+        rows_now, kept = layer_forward(
+            rows_now, vectors[layer], biases[layer], weights[layer], mask, from_pair, meanwhile
+        )
         saved.append(kept)
         if layer + 1 < S:
             rows_now = rows_now.astype(LOW).astype(WIDE)
     end_rows = rows_now
 
-    grad_now = arrived[1]
-    matrix_grads, vector_grads = [None] * S, [None] * S
+    grad_now = jnp.where(active, brought(cotangent).astype(WIDE), 0.0)
+    vector_grads = [None] * S
+
     for layer in reversed(range(S)):
-        grad_now, matrix_grads[layer], vector_grads[layer] = layer_backward(
-            grad_now, saved[layer], vectors[layer], weights, layer, half, from_pair
+        grad_now, own, there, vector_grads[layer] = layer_backward(
+            grad_now, saved[layer], vectors[layer], weights[layer], half, from_pair,
+            sums_over if layer else (lambda own, there, before: before),
+            (lambda name, before, done: done) if layer else rows_meanwhile,
         )
         if layer:
             grad_now = grad_now.astype(LOW).astype(WIDE)
 
-    def by_column(value):
-        return jnp.stack([value[:, i * columns : (i + 1) * columns].astype(LOW) for i in range(MP)])
-
-    grads = {name: [matrix_grads[layer][name] for layer in range(S)] for name in ("qkv", "out", "fc1", "fc2")}
-    grads["pieces"] = pieces
+    above = {name: sums_done(name) for name in ("fc2", "fc1", "out", "qkv")}
+    grads = dict(own=own, there=there, above=above, pieces=pieces)
     shapes = [(3,) + w_query.shape[1:], w_query.shape[1:], w_fc1.shape[1:], (w_fc2.shape[2], w_fc2.shape[1])]
     names = NARROW + ("b_fc1",)
     table = jnp.stack(
@@ -1085,8 +1208,10 @@
     lines = -(-table.shape[3] // 1024) * 8
     table = jnp.pad(table, ((0, 0), (0, 0), (0, 0), (0, lines * 128 - table.shape[3])))
     table = table.reshape(S, MP, DP // 2, 2, lines, 128).transpose(3, 0, 2, 1, 4, 5)
-    ends, summed, g_qkv, g_out, g_fc1, g_fc2 = scatter(table, by_column(grad_now), by_column(end_rows), grads, shapes)
-    ends_out = ends.reshape(micros, 2 * rows, columns)[:, :seq_len].astype(WIDE).reshape(boundary.shape)
+    ends, summed, g_qkv, g_out, g_fc1, g_fc2 = scatter(
+        table, by_column(grad_now), by_column(end_rows), grads, shapes, (micros, seq_len, columns)
+    )
+    ends_out = ends.astype(WIDE).reshape(boundary.shape)
     summed = summed.reshape(-1)
     v, start = {}, 0
     for name in names:

time: 1150 us -> 975 us (0.85)
  Pallas kernels: 999 us -> 774 us
  starting transfers between devices: 3.82 us -> 26.1 us
  waiting for transfers between devices: 7.13 us -> 25.4 us
  local copies, waits for them, and re-layouts: 70.9 us -> 83.6 us
    pallas_call x1, Pallas kernels: 344 us -> 212 us  [scatter(): pl.pallas_call(functools.partial(scatter_kernel, pieces), in_specs=[vmem]...]
    pallas_call x1, Pallas kernels: 279 us -> 187 us  [gather(): pl.pallas_call(functools.partial(gather_kernel, pieces), in_specs=[HBM] *...]
    ppermute x0 -> x13, starting transfers between devices: none -> 23.7 us  [the longest x6 16.3 us: move(): return lax.ppermute(value, ('section', 'dp', 'mp'), pairs)]
    unnamed x65 -> x73, local copies, waits for them, and re-layouts: 19.4 us -> 37.3 us
    another operation x22, local copies, waits for them, and re-layouts: 17.4 us -> 1.55 us  [local(): vector_grads[layer][name].reshape(MP, DP, -1)]
    dynamic_update_slice x0 -> x6, local copies, waits for them, and re-layouts: none -> 14.2 us  [fill_rows(): weight = lax.dynamic_update_slice(weight, part, start)]
    ppermute x0 -> x13, waiting for transfers between devices: none -> 13.3 us  [the longest x7 13.3 us: from_row(): return lax.ppermute(value, 'dp', [(i, (i - 2 * r) % DP) for i in range(DP)])]
    convert_element_type x8 -> x7, other arithmetic: 37 us -> 28 us  [the longest x3 15.4 us: sums_done(): return total.astype(LOW)]
  transfers between devices with their start and end apart: 12 -> 24, of which waited for: 2 -> 4; matrix products, arithmetic and copies ran while one was open for 7% -> 6% of each run, Pallas kernels for 12% -> 27%
where the time goes in v2:
time: 975 us; the launch traced here: 961 us
  Pallas kernels  774 us (79%)
  local copies, waits for them, and re-layouts  83.6 us (9%)
  other arithmetic  49.8 us (5%)
  starting transfers between devices  26.1 us (3%)
  waiting for transfers between devices  25.4 us (3%)
    pallas_call x12, Pallas kernels, compute_call(): pl.pallas_call(kernel, grid=(steps,), in_specs=ins, out_specs=[spec for s...  375 us
    pallas_call x1, Pallas kernels, scatter(): pl.pallas_call(functools.partial(scatter_kernel, pieces), in_specs=[vmem]...  212 us
    pallas_call x1, Pallas kernels, gather(): pl.pallas_call(functools.partial(gather_kernel, pieces), in_specs=[HBM] *...  187 us
    unnamed x73, local copies, waits for them, and re-layouts  37.3 us
  transfers between devices with their start and end apart: 24, of which 4 were waited for; matrix products, arithmetic and copies ran while one was open for 6% of the time, Pallas kernels for 27%

profile of v2, /device:TPU:26, one launch (start us, length us, event | category | flops | bytes accessed | tf_op | source)
XLA Modules:
  0.0 961.0 jit_solution(11151679449845913836)
XLA Ops:
  9.8 2.0 copy.45
  11.9 6.2 convert_element_type.159
  18.5 1.5 pad.30
  20.8 187.2 %shard_map.313 = (bf16[688,1024]{1,0:T(8,128)(2,1)}, f32[8,32,128]{2,1,0:T(8,128)}, bf16[4,1024,1024]{2,1,0:T(8,128)(2,1)}, bf16[4,1024,1024]{2,1,0:T(8,128)(2,1...) custom-call(bf16[6,688,256]{2,1,0:T(8,128)(2,1)} %bitcast.155, ...), custom_call_target="tpu_custom_call" | custom-call | tf_op jit(solution)/shard_map/pallas_call | solution.py:271
  209.7 3.2 constant_dynamic-slice_fusion.2
  212.9 3.7 constant_dynamic-slice_fusion
  218.9 1.9 convert_select_fusion.1.x_ref
  220.9 11.2 %shard_map.314 = (bf16[688,1024]{1,0:T(8,128)(2,1)}, bf16[2,688,1024]{2,1,0:T(8,128)(2,1)}, bf16[688,1024]{1,0:T(8,128)(2,1)}) custom-call(f32[688,1024]{1,0:T(8,128)} %convert_select_fusion.1.x_ref, f32[16,1024]{1,0:T(8,128)} %pad.32.vec_ref, bf16[4,1024,1024]{2,1,0:T(8,128)(2,1)} %get-tuple-element.135.w_ref.wo_ref), custom_call_target="tpu_custom_call" | custom-call | flops 1000 | bytes 1000 | tf_op jit(solution)/shard_map/pallas_call | solution.py:555
  233.3 2.9 dynamic-slice_bitcast_fusion.4
  236.2 2.0 collective-permute-start
  238.2 7.2 collective-permute-start.1
  246.3 1.6 copy-done.1
  247.9 36.8 %shard_map.315 = (bf16[688,1024]{1,0:T(8,128)(2,1)}, f32[688,1024]{1,0:T(8,128)}, bf16[16,2,688,688]{3,2,1,0:T(8,128)(2,1)}) custom-call(bf16[688,1024]{1,0:T(8,128)(2,1)} %get-tuple-element.136.q_ref, bf16[2,688,1024]{2,1,0:T(8,128)(2,1)} %get-tuple-element.139.k0.v0, bf16[2,688,1024]{2,1,0:T(8,128)(2,1)} %copy-done.1, ...), custom_call_target="tpu_custom_call" | custom-call | flops 1000 | bytes 1000 | tf_op jit(solution)/shard_map/pallas_call | solution.py:555
  284.9 1.5 collective-permute-start.6
  286.4 2.0 collective-permute-start.4
  288.4 2.1 collective-permute-start.5
  291.8 27.4 %shard_map.316 = (f32[688,1024]{1,0:T(8,128)}, bf16[688,1024]{1,0:T(8,128)(2,1)}, f32[688,1024]{1,0:T(8,128)}, bf16[688,1024]{1,0:T(8,128)(2,1)}, bf16[688,4096]...) custom-call(f32[688,1024]{1,0:T(8,128)} %convert_select_fusion.1.x_ref, ...), custom_call_target="tpu_custom_call" | custom-call | flops 1000 | bytes 1000 | tf_op jit(solution)/shard_map/pallas_call | solution.py:555
  319.2 3.2 constant_dynamic-update-slice_fusion.4
  322.5 2.0 convert_convert_fusion.1.x_ref
  324.5 1.6 constant_dynamic-update-slice_fusion.3.w_ref.wo_ref
  326.0 11.2 %shard_map.317 = (bf16[688,1024]{1,0:T(8,128)(2,1)}, bf16[2,688,1024]{2,1,0:T(8,128)(2,1)}, bf16[688,1024]{1,0:T(8,128)(2,1)}) custom-call(f32[688,1024]{1,0:T(8,128)} %convert_convert_fusion.1.x_ref, f32[16,1024]{1,0:T(8,128)} %pad.35.vec_ref, bf16[4,1024,1024]{2,1,0:T(8,128)(2,1)} %constant_dynamic-update-slice_fusion.3.w_ref.wo_ref), custom_call_target="tpu_custom_call" | custom-call | flops 1000 | bytes 1000 | tf_op jit(solution)/shard_map/pallas_call | solution.py:555
  339.2 1.3 collective-permute-start.8
  340.5 1.7 collective-permute-start.9
  344.3 1.6 copy-done.2
  345.9 36.8 %shard_map.318 = (bf16[688,1024]{1,0:T(8,128)(2,1)}, f32[688,1024]{1,0:T(8,128)}, bf16[16,2,688,688]{3,2,1,0:T(8,128)(2,1)}) custom-call(bf16[688,1024]{1,0:T(8,128)(2,1)} %get-tuple-element.157.q_ref, bf16[2,688,1024]{2,1,0:T(8,128)(2,1)} %get-tuple-element.160.k0.v0, bf16[2,688,1024]{2,1,0:T(8,128)(2,1)} %copy-done.2, ...), custom_call_target="tpu_custom_call" | custom-call | flops 1000 | bytes 1000 | tf_op jit(solution)/shard_map/pallas_call | solution.py:555
  382.7 2.8 collective-permute-done.11
  387.6 2.3 constant_dynamic-update-slice_fusion.16
  389.9 2.4 constant_dynamic-update-slice_fusion.15.w1_ref
  392.5 1.9 convert_select_fusion.dy_ref
  394.4 3.2 constant_dynamic-update-slice_fusion.2
  397.6 1.5 constant_dynamic-update-slice_fusion.1.w2_ref
  399.1 27.4 %shard_map.319 = (f32[688,1024]{1,0:T(8,128)}, bf16[688,1024]{1,0:T(8,128)(2,1)}, f32[688,1024]{1,0:T(8,128)}, bf16[688,1024]{1,0:T(8,128)(2,1)}, bf16[688,4096]...) custom-call(f32[688,1024]{1,0:T(8,128)} %convert_convert_fusion.1.x_ref, ...), custom_call_target="tpu_custom_call" | custom-call | flops 1000 | bytes 1000 | tf_op jit(solution)/shard_map/pallas_call | solution.py:555
  426.6 48.3 %shard_map.320 = (f32[688,1024]{1,0:T(8,128)}, bf16[688,1024]{1,0:T(8,128)(2,1)}, bf16[2,256,4096]{2,1,0:T(8,128)(2,1)}, bf16[2,256,4096]{2,1,0:T(8,128)(2,1)}, ...) custom-call(s32[1]{0:T(128)} %bitcast.c_ref, ...), custom_call_target="tpu_custom_call" | custom-call | flops 1000 | bytes 1000 | tf_op jit(solution)/shard_map/pallas_call | solution.py:555
  475.5 42.5 %shard_map.321 = (bf16[3,688,1024]{2,1,0:T(8,128)(2,1)}, bf16[2,688,1024]{2,1,0:T(8,128)(2,1)}) custom-call(bf16[688,1024]{1,0:T(8,128)(2,1)} %get-tuple-element.157.q_ref, bf16[2,688,1024]{2,1,0:T(8,128)(2,1)} %get-tuple-element.160.k0.v0, bf16[2,688,1024]{2,1,0:T(8,128)(2,1)} %copy-done.2, bf16[2,688,1024]{2,1,0:T(8,128)(2,1)} %get-tuple-element.160.k0.v0, ...), custom_call_target="tpu_custom_call" | custom-call | flops 1000 | bytes 1000 | tf_op jit(solution)/shard_map/pallas_call | solution.py:555
  518.5 6.5 collective-permute-done.16
  525.0 2.2 fusion.7
  527.2 4.5 fusion.3
  531.7 3.7 fusion.4
  535.4 1.6 copy-done.7
  537.0 21.3 %shard_map.322 = (f32[688,1024]{1,0:T(8,128)}, bf16[3,2,256,1024]{3,2,1,0:T(8,128)(2,1)}, bf16[3,2,256,1024]{3,2,1,0:T(8,128)(2,1)}, f32[8,1024]{1,0:T(8,128)}) custom-call(s32[1]{0:T(128)} %bitcast.c_ref, bf16[3,688,1024]{2,1,0:T(8,128)(2,1)} %get-tuple-element.185.d0_ref, bf16[2,688,1024]{2,1,0:T(8,128)(2,1)} %copy-done.7, ...), custom_call_target="tpu_custom_call" | custom-call | flops 1000 | bytes 1000 | tf_op jit(solution)/shard_map/pallas_call | solution.py:555
  558.3 2.6 copy.47
  561.1 5.5 collective-permute-done.18
  566.7 2.1 fusion.5
  568.8 1.8 convert_convert_fusion.dy_ref
  571.5 48.5 %shard_map.323 = (f32[688,1024]{1,0:T(8,128)}, bf16[688,1024]{1,0:T(8,128)(2,1)}, bf16[2,256,4096]{2,1,0:T(8,128)(2,1)}, bf16[2,256,4096]{2,1,0:T(8,128)(2,1)}, ...) custom-call(s32[1]{0:T(128)} %bitcast.c_ref, ...), custom_call_target="tpu_custom_call" | custom-call | flops 1000 | bytes 1000 | tf_op jit(solution)/shard_map/pallas_call | solution.py:555
  620.0 1.3 collective-permute-start.20
  621.3 42.4 %shard_map.324 = (bf16[3,688,1024]{2,1,0:T(8,128)(2,1)}, bf16[2,688,1024]{2,1,0:T(8,128)(2,1)}) custom-call(bf16[688,1024]{1,0:T(8,128)(2,1)} %get-tuple-element.136.q_ref, bf16[2,688,1024]{2,1,0:T(8,128)(2,1)} %get-tuple-element.139.k0.v0, bf16[2,688,1024]{2,1,0:T(8,128)(2,1)} %copy-done.1, bf16[2,688,1024]{2,1,0:T(8,128)(2,1)} %get-tuple-element.139.k0.v0, ...), custom_call_target="tpu_custom_call" | custom-call | flops 1000 | bytes 1000 | tf_op jit(solution)/shard_map/pallas_call | solution.py:555
  665.4 2.0 convert.14
  667.5 1.3 pad_maximum_fusion.1.last_ref
  671.1 1.2 collective-permute-start.22
  672.3 9.4 fusion
  681.7 21.4 %shard_map.325 = (f32[688,1024]{1,0:T(8,128)}, bf16[3,2,256,1024]{3,2,1,0:T(8,128)(2,1)}, bf16[3,2,256,1024]{3,2,1,0:T(8,128)(2,1)}, f32[8,1024]{1,0:T(8,128)}) custom-call(s32[1]{0:T(128)} %bitcast.c_ref, bf16[3,688,1024]{2,1,0:T(8,128)(2,1)} %get-tuple-element.206.d0_ref, bf16[2,688,1024]{2,1,0:T(8,128)(2,1)} %collective-permute-done.21.d1_ref, ...), custom_call_target="tpu_custom_call" | custom-call | flops 1000 | bytes 1000 | tf_op jit(solution)/shard_map/pallas_call | solution.py:555
  705.8 2.4 fusion.6.refs_9_
  708.2 10.4 %collective-permute-done.22 = bf16[3,256,1024]{2,1,0:T(8,128)(2,1)} collective-permute-done((bf16[3,256,1024]{2,1,0:T(8,128)(2,1)}, bf16[3,256,1024]{2,1,0:T(8,128)(2,1)}, u32[]{:S(2)}, u32[]{:S(2)}) %collective-permute-start.22) | collective-permute-done | bytes 1572896 | tf_op jit(solution)/shard_map/ppermute | solution.py:1056
  718.6 2.0 convert.13
  720.7 1.3 pad_maximum_fusion.first_ref
  723.0 3.6 fusion.2.refs_8_
  726.7 212.0 %shard_map.326 = (bf16[3,1370,256]{2,1,0:T(8,128)(2,1)}, f32[8,128]{1,0:T(8,128)}, f32[3,256,256]{2,1,0:T(8,128)}, f32[256,256]{1,0:T(8,128)}, f32[256,1024]{1,0:T(8,128)}, /*index=5*/f32[256,1024]{1,0:T(8,128)}) custom-call(f32[2,2,2,4,8,128]{5,4,3,2,1,0:T(8,128)} %bitcast.161, bf16[4,688,256]{2,1,0:T(8,128)(2,1)} %pad_maximum_fusion.first_ref, ...), custom_call_target="tpu_custom_call" | custom-call | tf_op jit(solution)/shard_map/pallas_call | solution.py:490
  938.7 1.4 slice.202
  940.1 1.6 slice_bitcast_fusion.10
  941.8 1.8 copy.51
  943.6 2.0 fusion.9
  945.6 2.5 copy.52
  948.5 11.1 %copy.50 = f32[1,3,1,1370,256]{4,2,3,1,0:T(1,128)} copy(f32[1,3,1,1370,256]{4,3,1,2,0:T(8,128)S(1)} %bitcast_convert_fusion) | data formatting | bytes 8417280
  (153 shorter events, 35.5 us)
Async XLA Ops:
  18.5 1.5 copy-start.16
  18.5 1.5 copy-start.17
  18.5 1.5 copy-start.18
  209.7 6.9 copy-start
  217.2 1.7 copy-start.12
  232.0 14.3 %collective-permute-start.2 = (bf16[2,688,1024]{2,1,0:T(8,128)(2,1)}, bf16[2,688,1024]{2,1,0:T(8,128)(2,1)S(1)}, u32[]{:S(2)}, u32[]{:S(2)}) collective-permute-start(bf16[2,688,1024]{2,1,0:T(8,128)(2,1)} %get-tuple-element.139.k0.v0), channel_id=1, source_target_pairs={{0,4},{4,0},{8,12},{12,8},{1,5},{5,1},{9,13},{13,9},{2,6},{6,2},{1... | collective-permute-start | bytes 8454152 | tf_op jit(solution)/shard_map/ppermute | solution.py:1053
  232.7 52.1 %collective-permute-start.3 = (bf16[4,256,1024]{2,1,0:T(8,128)(2,1)}, bf16[4,256,1024]{2,1,0:T(8,128)(2,1)}, u32[]{:S(2)}, u32[]{:S(2)}) collective-permute-start(bf16[4,256,1024]{2,1,0:T(8,128)(2,1)} %constant_dynamic-slice_fusion.2), channel_id=1, source_target_pairs={{0,8},{4,12},{8,0},{12,4},{1,9},{5,13},{9,1},{13,5},{2,10},{6,14},... | collective-permute-start | bytes 6291464 | tf_op jit(solution)/shard_map/ppermute | solution.py:1056
  236.2 48.6 %collective-permute-start = (bf16[688,256]{1,0:T(8,128)(2,1)}, bf16[688,256]{1,0:T(8,128)(2,1)}, u32[]{:S(2)}, u32[]{:S(2)}) collective-permute-start(bf16[688,256]{1,0:T(8,128)(2,1)} %get-tuple-element.137), channel_id=1, source_target_pairs={{16,0},{17,4},{18,2},{19,6},{20,1},{21,5},{22,3},{23,7},{24,8},{25... | collective-permute-start | bytes 1056776 | tf_op jit(solution)/shard_map/ppermute | solution.py:1064
  238.2 46.5 %collective-permute-start.1 = (bf16[688,256]{1,0:T(8,128)(2,1)}, bf16[688,256]{1,0:T(8,128)(2,1)}, u32[]{:S(2)}, u32[]{:S(2)}) collective-permute-start(bf16[688,256]{1,0:T(8,128)(2,1)} %get-tuple-element.138), channel_id=1, source_target_pairs={{16,4},{17,2},{18,6},{19,16},{20,5},{21,3},{22,7},{23,17},{24,12},... | collective-permute-start | bytes 1056776 | tf_op jit(solution)/shard_map/ppermute | solution.py:1064
  246.3 1.6 copy-start.1
  284.8 39.7 %collective-permute-start.7 = (bf16[4,256,1024]{2,1,0:T(8,128)(2,1)}, bf16[4,256,1024]{2,1,0:T(8,128)(2,1)S(1)}, u32[]{:S(2)}, u32[]{:S(2)}) collective-permute-start(bf16[4,256,1024]{2,1,0:T(8,128)(2,1)} %collective-permute-done.3), channel_id=1, source_target_pairs={{0,4},{4,0},{8,12},{12,8},{1,5},{5,1},{9,13},{13,9},{2,6},{6,2},{1... | collective-permute-start | bytes 6291464 | tf_op jit(solution)/shard_map/ppermute | solution.py:1053
  284.9 37.6 %collective-permute-start.6 = (bf16[256,2048]{1,0:T(8,128)(2,1)}, bf16[256,2048]{1,0:T(8,128)(2,1)S(1)}, u32[]{:S(2)}, u32[]{:S(2)}) collective-permute-start(bf16[256,2048]{1,0:T(8,128)(2,1)} %constant_dynamic-slice_fusion.1), channel_id=1, source_target_pairs={{0,8},{4,12},{8,0},{12,4},{1,9},{5,13},{9,1},{13,5},{2,10},{6,14},... | collective-permute-start | bytes 3145736 | tf_op jit(solution)/shard_map/ppermute | solution.py:1056
  286.4 36.1 %collective-permute-start.4 = (bf16[688,256]{1,0:T(8,128)(2,1)}, bf16[688,256]{1,0:T(8,128)(2,1)}, u32[]{:S(2)}, u32[]{:S(2)}) collective-permute-start(bf16[688,256]{1,0:T(8,128)(2,1)} %get-tuple-element.146), channel_id=1, source_target_pairs={{16,2},{17,6},{18,16},{19,20},{20,3},{21,7},{22,17},{23,21},{24,10... | collective-permute-start | bytes 1056776 | tf_op jit(solution)/shard_map/ppermute | solution.py:1064
  288.4 34.1 %collective-permute-start.5 = (bf16[688,256]{1,0:T(8,128)(2,1)}, bf16[688,256]{1,0:T(8,128)(2,1)}, u32[]{:S(2)}, u32[]{:S(2)}) collective-permute-start(bf16[688,256]{1,0:T(8,128)(2,1)} %get-tuple-element.147), channel_id=1, source_target_pairs={{16,6},{17,16},{18,20},{19,0},{20,7},{21,17},{22,21},{23,1},{24,14... | collective-permute-start | bytes 1056776 | tf_op jit(solution)/shard_map/ppermute | solution.py:1064
  319.2 3.3 copy-start.8
  322.5 3.5 copy-start.13
  326.0 14.5 %copy-start.15 = (bf16[688,256]{1,0:T(8,128)(2,1)S(1)}, bf16[688,256]{1,0:T(8,128)(2,1)}, u32[]{:S(2)}) copy-start(bf16[688,256]{1,0:T(8,128)(2,1)} %get-tuple-element.159) | copy-start | bytes 1056772
  337.2 7.1 collective-permute-start.10
  337.4 48.2 %collective-permute-start.11 = (bf16[256,4096]{1,0:T(8,128)(2,1)}, bf16[256,4096]{1,0:T(8,128)(2,1)}, u32[]{:S(2)}, u32[]{:S(2)}) collective-permute-start(bf16[256,4096]{1,0:T(8,128)(2,1)} %constant_dynamic-slice_fusion), channel_id=1, source_target_pairs={{0,8},{4,12},{8,0},{12,4},{1,9},{5,13},{9,1},{13,5},{2,10},{6,14},... | collective-permute-start | bytes 6291464 | tf_op jit(solution)/shard_map/ppermute | solution.py:1056
  339.2 50.7 %collective-permute-start.12 = (bf16[256,2048]{1,0:T(8,128)(2,1)}, bf16[256,2048]{1,0:T(8,128)(2,1)}, u32[]{:S(2)}, u32[]{:S(2)}) collective-permute-start(bf16[256,2048]{1,0:T(8,128)(2,1)} %copy-done.13), channel_id=1, source_target_pairs={{0,4},{4,0},{8,12},{12,8},{1,5},{5,1},{9,13},{13,9},{2,6},{6,2},{1... | collective-permute-start | bytes 3145736 | tf_op jit(solution)/shard_map/ppermute | solution.py:1053
  339.2 43.5 %collective-permute-start.8 = (bf16[688,256]{1,0:T(8,128)(2,1)}, bf16[688,256]{1,0:T(8,128)(2,1)S(1)}, u32[]{:S(2)}, u32[]{:S(2)}) collective-permute-start(bf16[688,256]{1,0:T(8,128)(2,1)} %get-tuple-element.158), channel_id=1, source_target_pairs={{16,16},{17,20},{18,0},{19,4},{20,17},{21,21},{22,1},{23,5},{24,24... | collective-permute-start | bytes 1056776 | tf_op jit(solution)/shard_map/ppermute | solution.py:1064
  340.5 42.2 %collective-permute-start.9 = (bf16[688,256]{1,0:T(8,128)(2,1)S(1)}, bf16[688,256]{1,0:T(8,128)(2,1)S(1)}, u32[]{:S(2)}, u32[]{:S(2)}) collective-permute-start(bf16[688,256]{1,0:T(8,128)(2,1)S(1)} %copy-done.15), channel_id=1, source_target_pairs={{16,20},{17,0},{18,4},{19,2},{20,21},{21,1},{22,5},{23,3},{24,28},... | collective-permute-start | bytes 1056776 | tf_op jit(solution)/shard_map/ppermute | solution.py:1064
  344.3 1.6 copy-start.2
  385.6 12.1 %collective-permute-start.13 = (bf16[256,4096]{1,0:T(8,128)(2,1)}, bf16[256,4096]{1,0:T(8,128)(2,1)S(1)}, u32[]{:S(2)}, u32[]{:S(2)}) collective-permute-start(bf16[256,4096]{1,0:T(8,128)(2,1)} %collective-permute-done.11), channel_id=1, source_target_pairs={{0,4},{4,0},{8,12},{12,8},{1,5},{5,1},{9,13},{13,9},{2,6},{6,2},{1... | collective-permute-start | bytes 6291464 | tf_op jit(solution)/shard_map/ppermute | solution.py:1053
  474.8 52.4 %collective-permute-start.14 = (bf16[2,256,4096]{2,1,0:T(8,128)(2,1)}, bf16[2,256,4096]{2,1,0:T(8,128)(2,1)}, u32[]{:S(2)}, u32[]{:S(2)}) collective-permute-start(bf16[2,256,4096]{2,1,0:T(8,128)(2,1)} %get-tuple-element.176), channel_id=1, source_target_pairs={{0,4},{4,0},{8,12},{12,8},{1,5},{5,1},{9,13},{13,9},{2,6},{6,2},{1... | collective-permute-start | bytes 12582920 | tf_op jit(solution)/shard_map/ppermute | solution.py:1053
  475.4 56.3 %collective-permute-start.15 = (bf16[2,256,4096]{2,1,0:T(8,128)(2,1)}, bf16[2,256,4096]{2,1,0:T(8,128)(2,1)}, u32[]{:S(2)}, u32[]{:S(2)}) collective-permute-start(bf16[2,256,4096]{2,1,0:T(8,128)(2,1)} %get-tuple-element.178), channel_id=1, source_target_pairs={{0,4},{4,0},{8,12},{12,8},{1,5},{5,1},{9,13},{13,9},{2,6},{6,2},{1... | collective-permute-start | bytes 12582920 | tf_op jit(solution)/shard_map/ppermute | solution.py:1053
  517.9 17.5 %collective-permute-start.17 = (bf16[2,688,1024]{2,1,0:T(8,128)(2,1)}, bf16[2,688,1024]{2,1,0:T(8,128)(2,1)S(1)}, u32[]{:S(2)}, u32[]{:S(2)}) collective-permute-start(bf16[2,688,1024]{2,1,0:T(8,128)(2,1)} %get-tuple-element.186), channel_id=1, source_target_pairs={{0,4},{4,0},{8,12},{12,8},{1,5},{5,1},{9,13},{13,9},{2,6},{6,2},{1... | collective-permute-start | bytes 8454152 | tf_op jit(solution)/shard_map/ppermute | solution.py:1053
  518.4 6.6 collective-permute-start.16
  527.2 4.5 copy-start.3
  535.4 1.6 copy-start.7
  558.3 8.4 copy-start.4
  560.9 7.9 copy-start.9
  560.9 5.7 collective-permute-start.18
  566.7 4.0 copy-start.5
  570.6 49.4 %collective-permute-start.19 = (bf16[256,4096]{1,0:T(8,128)(2,1)}, bf16[256,4096]{1,0:T(8,128)(2,1)S(1)}, u32[]{:S(2)}, u32[]{:S(2)}) collective-permute-start(bf16[256,4096]{1,0:T(8,128)(2,1)} %fusion.4), channel_id=1, source_target_pairs={{0,8},{4,12},{8,0},{12,4},{1,9},{5,13},{9,1},{13,5},{2,10},{6,14},... | collective-permute-start | bytes 6291464 | tf_op jit(solution)/shard_map/ppermute | solution.py:1056
  620.0 43.7 %copy-start.11 = (bf16[256,4096]{1,0:T(8,128)(2,1)}, bf16[256,4096]{1,0:T(8,128)(2,1)S(1)}, u32[]{:S(2)}) copy-start(bf16[256,4096]{1,0:T(8,128)(2,1)S(1)} %collective-permute-done.19) | copy-start | bytes 6291460
  620.0 50.2 %collective-permute-start.20 = (bf16[256,4096]{1,0:T(8,128)(2,1)}, bf16[256,4096]{1,0:T(8,128)(2,1)}, u32[]{:S(2)}, u32[]{:S(2)}) collective-permute-start(bf16[256,4096]{1,0:T(8,128)(2,1)} %fusion.3), channel_id=1, source_target_pairs={{0,8},{4,12},{8,0},{12,4},{1,9},{5,13},{9,1},{13,5},{2,10},{6,14},... | collective-permute-start | bytes 6291464 | tf_op jit(solution)/shard_map/ppermute | solution.py:1056
  621.3 43.5 %copy-start.19 = (f32[8,1024]{1,0:T(8,128)S(1)}, f32[8,1024]{1,0:T(8,128)}, u32[]{:S(2)}) copy-start(f32[8,1024]{1,0:T(8,128)} %get-tuple-element.214) | copy-start | bytes 98308
  663.7 18.0 %collective-permute-start.21 = (bf16[2,688,1024]{2,1,0:T(8,128)(2,1)}, bf16[2,688,1024]{2,1,0:T(8,128)(2,1)}, u32[]{:S(2)}, u32[]{:S(2)}) collective-permute-start(bf16[2,688,1024]{2,1,0:T(8,128)(2,1)} %get-tuple-element.207), channel_id=1, source_target_pairs={{0,4},{4,0},{8,12},{12,8},{1,5},{5,1},{9,13},{13,9},{2,6},{6,2},{1... | collective-permute-start | bytes 8454152 | tf_op jit(solution)/shard_map/ppermute | solution.py:1053
  667.4 1.4 copy-start.21
  670.2 32.9 %collective-permute-start.23 = (bf16[256,1024]{1,0:T(8,128)(2,1)}, bf16[256,1024]{1,0:T(8,128)(2,1)}, u32[]{:S(2)}, u32[]{:S(2)}) collective-permute-start(bf16[256,1024]{1,0:T(8,128)(2,1)} %fusion.7), channel_id=1, source_target_pairs={{0,8},{4,12},{8,0},{12,4},{1,9},{5,13},{9,1},{13,5},{2,10},{6,14},... | collective-permute-start | bytes 1572872 | tf_op jit(solution)/shard_map/ppermute | solution.py:1056
  671.1 47.5 %collective-permute-start.22 = (bf16[3,256,1024]{2,1,0:T(8,128)(2,1)}, bf16[3,256,1024]{2,1,0:T(8,128)(2,1)}, u32[]{:S(2)}, u32[]{:S(2)}) collective-permute-start(bf16[3,256,1024]{2,1,0:T(8,128)(2,1)} %fusion.5), channel_id=1, source_target_pairs={{0,8},{4,12},{8,0},{12,4},{1,9},{5,13},{9,1},{13,5},{2,10},{6,14},... | collective-permute-start | bytes 4718600 | tf_op jit(solution)/shard_map/ppermute | solution.py:1056
  681.7 21.4 %copy-start.20 = (f32[8,1024]{1,0:T(8,128)S(1)}, f32[8,1024]{1,0:T(8,128)}, u32[]{:S(2)}) copy-start(f32[8,1024]{1,0:T(8,128)} %get-tuple-element.211) | copy-start | bytes 98308
  720.6 2.4 copy-start.6
  938.7 9.4 copy-start.10
  948.5 11.1 %copy-start.14 = (f32[256,1024]{1,0:T(8,128)S(1)}, f32[256,1024]{1,0:T(8,128)}, u32[]{:S(2)}) copy-start(f32[256,1024]{1,0:T(8,128)} %get-tuple-element.238) | copy-start | bytes 3145732

commit v3 on v2

--- a/solution.py
+++ b/solution.py
@@ -11,7 +11,7 @@
 HD = 64
 LOW = jnp.bfloat16
 WIDE = jnp.float32
-HBM = pl.BlockSpec(memory_space=pl.ANY)
+HBM = pl.BlockSpec(memory_space=pltpu.HBM)
 
 epsilon = 1e-06
 inv_root_two = 0.7071067811865476
@@ -102,19 +102,22 @@
     return lax.div(image, place.MP), piece % 2, lax.rem(image, place.MP)
 
 
-def gather_counts(S, Y, MP, groups=3):
-    return dict(rows=MP, vectors=S * MP, piece=groups * S * Y * MP, pair=groups * S * Y * MP)
-
-
-def gather_kernel(pieces, sent_ref, vec_ref, a_ref, b_ref, c_ref, rows_ref, vecs_ref, *refs):
+def gather_counts(S, Y, MP, groups=4):
+    return dict(rows=MP, vectors=S * MP, biases=S * MP, piece=groups * S * Y * MP, pair=groups * S * Y * MP)
+
+
+def gather_kernel(pieces, tokens_ref, vec_ref, bias_ref, *refs):
     place = Place()
     s, y, c, z, d = place.s, place.y, place.c, place.z, place.d
     S, Y, MP, H = place.S, place.Y, place.MP, place.H
-    shards = (a_ref, b_ref, c_ref)
-    wholes = (refs[0:S], refs[S : 2 * S], refs[2 * S : 3 * S])
-    send_sems, recv_sems, own_sems = refs[3 * S :]
+    shards, refs = refs[:4], refs[4:]
+    rows_ref, sent_ref, vecs_ref, biases_ref = refs[:4]
+    wholes = [refs[4 + g * S : 4 + (g + 1) * S] for g in range(4)]
+    later, refs = refs[4 + 4 * S : 8 + 4 * S], refs[8 + 4 * S :]
+    send_sems, recv_sems, own_sems, wide, load_sems = refs
     moves = Moves(send_sems, recv_sems, gather_counts(S, Y, MP))
     columns = sent_ref.shape[2]
+    groups = range(4)
 
     def spot(g, l, yy, cc, zz):
         dd = yy * 2 + cc
@@ -154,7 +157,7 @@
         hand(g, True, y, zz, "piece", when, src, section=s, dp=d, mp=jnp.clip(z + step, 0, MP - 1))
 
     def rows_if(g, mine, zz, first_layer, there, src=None):
-        when = first_layer | (zz < H) if g == 1 else first_layer
+        when = first_layer | (zz < H) if g == 2 else first_layer
         for r in range(1, Y):
             hand(g, mine, y, zz, "piece", when & there, src, section=s, dp=place.other_y(r) * 2 + c, mp=z)
 
@@ -201,19 +204,39 @@
     def rows_in(g):
         for r in range(1, Y):
             yy = place.other_y(r)
-            for layer, zz in [(0, zz) for zz in range(MP)] + ([(1, zz) for zz in range(H)] if g == 1 else []):
+            for layer, zz in [(0, zz) for zz in range(MP)] + ([(1, zz) for zz in range(H)] if g == 2 else []):
                 landed(g, layer, yy, zz)
                 there = spot(g, layer, yy, c, zz)
                 moves.send(there, there, "pair", mark(g, layer, yy, zz), section=s, dp=y * 2 + 1 - c, mp=z)
 
-    for q in range(1, S * MP):
-        at = lax.rem(s * MP + z + q, S * MP)
-        moves.send(vec_ref, vecs_ref.at[s * MP + z], "vectors", s * MP + z, section=lax.div(at, MP), dp=d, mp=lax.rem(at, MP))
-    own_vec = pltpu.make_async_copy(vec_ref, vecs_ref.at[s * MP + z], own_sems.at[3])
-    own_vec.start()
-
-    for g in range(3):
+    rows = rows_ref.shape[0]
+    spare = 2 * rows - tokens_ref.shape[1]
+    loads = []
+    for piece in range(pieces):
+        start = (rows - spare) * (piece % 2)
+        copy = pltpu.make_async_copy(
+            tokens_ref.at[piece // 2, pl.ds(start, rows), 0], wide.at[piece], load_sems.at[piece]
+        )
+        copy.start()
+        loads.append(copy)
+
+    own_vectors = []
+    for i, (ref, whole, name) in enumerate(((vec_ref, vecs_ref, "vectors"), (bias_ref, biases_ref, "biases"))):
+        there = whole.at[s, :, tile(z, ref.shape[1])]
+        for q in range(1, S * MP):
+            at = lax.rem(s * MP + z + q, S * MP)
+            moves.send(ref, there, name, s * MP + z, section=lax.div(at, MP), dp=d, mp=lax.rem(at, MP))
+        own_vectors.append(pltpu.make_async_copy(ref, there, own_sems.at[4 + i]))
+        own_vectors[-1].start()
+
+    for g in groups:
         columns_out(g)
+    for piece in range(pieces):
+        loads[piece].wait()
+        low = wide[piece]
+        if piece % 2 and spare:
+            low = jnp.where(lax.broadcasted_iota(jnp.int32, (rows, 1), 0) < spare, 0.0, low)
+        sent_ref[piece] = low.astype(LOW)
     for piece in range(pieces):
         to_s, to_c, to_z = holder(place, c, piece)
         here = (to_s == s) & (to_c == c) & (to_z == z)
@@ -228,12 +251,26 @@
             pltpu.make_async_copy(sent_ref.at[piece], there, moves.arrival("rows", z)).start()
 
     for far in range(1, MP):
-        for g in range(3):
+        for g in groups:
             columns_in(g, far)
             section_in(g, far - 1)
-    for g in range(3):
+    for g in groups:
         section_in(g, MP - 1)
-    for g in range(3):
+    for copy in own_copies:
+        copy.wait()
+    later_copies = []
+    for g in groups:
+        shard, there = shards[g], later[g]
+        at = (tile(d, shard.shape[-2]),)
+        if g < 2:
+            at = at + (slice(None),)
+        else:
+            at = at + (tile(1 if g == 2 else s, there.shape[-1]),)
+        src = wholes[g][1].at[(slice(None),) + at] if len(shard.shape) == 3 else wholes[g][1].at[at]
+        copy = pltpu.make_async_copy(src, there, own_sems.at[6 + g])
+        copy.start()
+        later_copies.append(copy)
+    for g in groups:
         rows_in(g)
 
     @pl.when(s * MP + z < pieces)
@@ -243,48 +280,63 @@
 
     for q in range(1, S * MP):
         at = lax.rem(s * MP + z + q, S * MP)
-        moves.wait(vecs_ref.at[at], "vectors", at)
-    for g in range(3):
+        for ref, whole, name in ((vec_ref, vecs_ref, "vectors"), (bias_ref, biases_ref, "biases")):
+            moves.wait(whole.at[lax.div(at, MP), :, tile(lax.rem(at, MP), ref.shape[1])], name, at)
+    for g in groups:
         for zz in range(MP):
             for r in range(Y):
                 yy = place.other_y(r)
                 moves.wait(spot(g, 0, yy, 1 - c, zz), "pair", mark(g, 0, yy, zz))
-                if g == 1 and zz < H and r:
+                if g == 2 and zz < H and r:
                     moves.wait(spot(g, 1, yy, 1 - c, zz), "pair", mark(g, 1, yy, zz))
             for layer in range(1, S):
                 moves.wait(spot(g, 0, y, 1 - c, zz), "pair", mark(g, layer, y, zz))
-    own_vec.wait()
-    for copy in own_copies:
+    for copy in own_vectors + later_copies:
         copy.wait()
     moves.finish()
 
 
-def gather(sent, vec, a, b, c):
+def gather(tokens, vec, bias, *shards):
     S, DP, MP = (lax.axis_size(name) for name in ("section", "dp", "mp"))
     Y = DP // 2
-    pieces, rows, columns = sent.shape
+    micros, seq_len, _, columns = tokens.shape
+    pieces, rows = 2 * micros, half_rows(seq_len)
     counts = gather_counts(S, Y, MP)
-    sends = pieces + S * MP - 1 + 3 * (2 * MP + (2 * MP - 1) * (1 + 2 * Y) + (Y - 1) * MP) + (Y - 1) * (MP // 2)
+    sends = pieces + 2 * (S * MP - 1) + 4 * (2 * MP + (2 * MP - 1) * (1 + 2 * Y) + (Y - 1) * MP) + (Y - 1) * (MP // 2)
     whole = [
-        jax.ShapeDtypeStruct(shard.shape[:-2] + (shard.shape[-2] * DP, shard.shape[-1] * MP), LOW) for shard in (a, b, c)
+        jax.ShapeDtypeStruct(shard.shape[:-2] + (shard.shape[-2] * DP, shard.shape[-1] * MP), LOW) for shard in shards
     ]
+    later = [
+        jax.ShapeDtypeStruct(shard.shape[:-1] + (shard.shape[-1] * MP // (1 if g < 2 else 2),), LOW)
+        for g, shard in enumerate(shards)
+    ]
+    vmem = pl.BlockSpec(memory_space=pltpu.VMEM)
     got = pl.pallas_call(
         functools.partial(gather_kernel, pieces),
-        in_specs=[HBM] * 5,
-        out_specs=[HBM] * (2 + 3 * S),
+        in_specs=[vmem] * 7,
+        out_specs=[HBM, vmem] + [HBM] * (2 + 4 * S) + [vmem] * 4,
         out_shape=[
             jax.ShapeDtypeStruct((rows, columns * MP), LOW),
-            jax.ShapeDtypeStruct((S * MP,) + vec.shape, WIDE),
+            jax.ShapeDtypeStruct((pieces, rows, columns), LOW),
+            jax.ShapeDtypeStruct((S, vec.shape[0], vec.shape[1] * MP), WIDE),
+            jax.ShapeDtypeStruct((S, bias.shape[0], bias.shape[1] * MP), WIDE),
         ]
-        + [shape for shape in whole for _ in range(S)],
+        + [shape for shape in whole for _ in range(S)]
+        + later,
         scratch_shapes=[
             pltpu.SemaphoreType.DMA((sends,)),
             pltpu.SemaphoreType.DMA((sum(counts.values()),)),
-            pltpu.SemaphoreType.DMA((4,)),
+            pltpu.SemaphoreType.DMA((10,)),
+            pltpu.VMEM((pieces, rows, columns), WIDE),
+            pltpu.SemaphoreType.DMA((pieces,)),
         ],
-        compiler_params=pltpu.CompilerParams(has_side_effects=True),
-    )(sent, vec, a, b, c)
-    return got[0], got[1], [[got[2 + g * S + layer] for g in range(3)] for layer in range(S)]
+        compiler_params=pltpu.CompilerParams(has_side_effects=True, vmem_limit_bytes=63 << 20),
+    )(tokens, vec, bias, *shards)
+    return got[:4], [[got[4 + g * S + layer] for g in range(4)] for layer in range(S)], got[4 + 4 * S :]
+
+
+def half_rows(seq_len):
+    return -(-seq_len // 32) * 16
 
 
 def scatter_counts(S, Y, MP, pieces, groups=4):
@@ -311,7 +363,7 @@
     own, there, above = refs[0:4], refs[4:8], refs[8:12]
     ends_ref, sums_ref, outs = refs[12], refs[13], refs[14:18]
     held, paired, mine, from_x, from_y, from_z = (refs[18 + 4 * i : 22 + 4 * i] for i in range(6))
-    send_sems, recv_sems, load_sems, vec_here, vec_pair, vec_x, vec_y, vec_z, landing = refs[42:]
+    send_sems, recv_sems, load_sems, vec_here, vec_pair, vec_x, vec_y, vec_z = refs[42:]
     moves = Moves(send_sems, recv_sems, scatter_counts(S, Y, MP, pieces))
 
     def part(ref, g, zz, yy=None):
@@ -370,7 +422,7 @@
         for zz in range(MP):
             to_c = lax.rem(number, 2)
             here = (s == section) & (to_c == c) & (z == zz)
-            dst = landing.at[piece]
+            dst = ends_ref.at[piece]
             moves.send(
                 ref.at[zz], dst, "back", piece, active & jnp.logical_not(here), section=section, dp=y * 2 + to_c, mp=zz
             )
@@ -459,21 +511,14 @@
                 total = total + vec_z[place.other_z(r)]
             sums_ref[...] = total
 
-    rows = landing.shape[1]
-    rest = ends_ref.shape[1] - rows
-    for p in range(pieces):
-        moves.wait(landing.at[p], "back", p)
-        if p % 2 == 0:
-            ends_ref[p // 2, 0:rows] = landing[p]
-        else:
-            ends_ref[p // 2, rows:] = landing[p][:rest]
-
     for g in ORDER:
         columns_step(g)
+    for p in range(pieces):
+        moves.wait(ends_ref.at[p], "back", p)
     moves.finish()
 
 
-def scatter(table, first, last, grads, shapes, ends_shape):
+def scatter(table, first, last, grads, shapes):
     S, DP, MP = (lax.axis_size(name) for name in ("section", "dp", "mp"))
     Y = DP // 2
     _, rows, block = first.shape
@@ -490,8 +535,8 @@
     return pl.pallas_call(
         functools.partial(scatter_kernel, pieces),
         in_specs=[vmem] + [HBM] * (2 + len(flat)),
-        out_specs=[vmem] * 6,
-        out_shape=[jax.ShapeDtypeStruct(ends_shape, LOW), jax.ShapeDtypeStruct(table.shape[4:], WIDE)]
+        out_specs=[HBM] + [vmem] * 5,
+        out_shape=[jax.ShapeDtypeStruct((pieces, rows, block), LOW), jax.ShapeDtypeStruct(table.shape[4:], WIDE)]
         + [jax.ShapeDtypeStruct(shape, WIDE) for shape in shapes],
         scratch_shapes=room(Y * MP)
         + room(Y * MP)
@@ -508,10 +553,61 @@
             pltpu.VMEM(table.shape[2:], WIDE),
             pltpu.VMEM((Y - 1,) + table.shape[3:], WIDE),
             pltpu.VMEM(table.shape[3:], WIDE),
-            pltpu.VMEM((pieces, rows, block), LOW),
         ],
         compiler_params=pltpu.CompilerParams(has_side_effects=True, vmem_limit_bytes=63 << 20),
     )(table, first, last, *flat)
+
+
+def finish_kernel(small, landing_ref, sums_ref, qkv_ref, out_ref, fc1_ref, fc2_ref, ends_ref, *refs):
+    projections, (g_out, g_fc1, g_fc2), vectors = refs[0:3], refs[3:6], refs[6:-2]
+    wide, sems = refs[-2:]
+    pieces, rows, _ = landing_ref.shape
+    seq_len = ends_ref.shape[1]
+
+    def end_copy(p):
+        start = (seq_len - rows) * (p % 2)
+        return pltpu.make_async_copy(wide.at[p], ends_ref.at[p // 2, pl.ds(start, rows), 0], sems.at[p])
+
+    for p in list(range(1, pieces, 2)) + list(range(0, pieces, 2)):
+        wide[p] = landing_ref[p].astype(WIDE)
+        if p % 2:
+            end_copy(p).start()
+    for p in range(1, pieces, 2):
+        end_copy(p).wait()
+        end_copy(p - 1).start()
+    for kind, ref in enumerate(projections):
+        ref[...] = qkv_ref[kind]
+    g_out[...] = out_ref[...].T
+    g_fc1[...] = fc1_ref[...]
+    g_fc2[...] = fc2_ref[...].T
+    start = 0
+    for ref in vectors:
+        size = ref.shape[1]
+        done = 0
+        while done < size:
+            row, lane = divmod(start + done, 128)
+            count = min(128 - lane, size - done)
+            ref[0:1, done : done + count] = sums_ref[row : row + 1, lane : lane + count]
+            done += count
+        start += size
+    for p in range(0, pieces, 2):
+        end_copy(p).wait()
+
+
+def finish(ends, sums, grads, seq_len, sizes):
+    pieces, rows, columns = ends.shape
+    vmem = pl.BlockSpec(memory_space=pltpu.VMEM)
+    qkv, out, fc1, fc2 = grads
+    shapes = [qkv.shape[1:]] * 3 + [out.shape[::-1], fc1.shape, fc2.shape[::-1]] + [(1, size) for size in sizes]
+    return pl.pallas_call(
+        functools.partial(finish_kernel, sizes[0]),
+        in_specs=[vmem] * 6,
+        out_specs=[HBM] + [vmem] * len(shapes),
+        out_shape=[jax.ShapeDtypeStruct((pieces // 2, seq_len, 1, columns), WIDE)]
+        + [jax.ShapeDtypeStruct(shape, WIDE) for shape in shapes],
+        scratch_shapes=[pltpu.VMEM((pieces, rows, columns), WIDE), pltpu.SemaphoreType.DMA((pieces,))],
+        compiler_params=pltpu.CompilerParams(vmem_limit_bytes=32 << 20),
+    )(ends, sums, qkv, out, fc1, fc2)
 
 
 def nn(left, right):
@@ -567,29 +663,22 @@
 LN1_GAIN, LN1_BIAS, B_QUERY, B_VALUE, B_OUT, SCALE_ATTN, LN2_GAIN, LN2_BIAS, B_FC2, SCALE_MLP = range(10)
 
 
-def project_kernel(x_ref, vec_ref, w_ref, n_ref, kv_ref, q_ref, held):
+def project_kernel(x_ref, vec_ref, w_ref, n_ref, kv_ref, q_ref):
     step = pl.program_id(0)
 
     @pl.when(step == 0)
     def _():
         xhat, _ = centre(x_ref[...])
-        low = (xhat * vec_ref[LN1_GAIN][None] + vec_ref[LN1_BIAS][None]).astype(LOW)
-        held[...] = low
-        n_ref[...] = low
-
-    value = nn(held[...], w_ref[...])
-
-    @pl.when(step == 0)
-    def _():
-        kv_ref[0] = value.astype(LOW)
+        n_ref[...] = (xhat * vec_ref[LN1_GAIN][None] + vec_ref[LN1_BIAS][None]).astype(LOW)
+        kv_ref[0] = nn(n_ref[...], w_ref[...]).astype(LOW)
 
     @pl.when(step == 1)
     def _():
-        kv_ref[1] = (value + vec_ref[B_VALUE][None]).astype(LOW)
+        kv_ref[1] = (nn(n_ref[...], w_ref[...]) + vec_ref[B_VALUE][None]).astype(LOW)
 
     @pl.when(step == 2)
     def _():
-        q_ref[...] = (value + vec_ref[B_QUERY][None]).astype(LOW)
+        q_ref[...] = (nn(n_ref[...], w_ref[...]) + vec_ref[B_QUERY][None]).astype(LOW)
 
 
 def project(rows_in, vec, attn):
@@ -608,53 +697,82 @@
             (full((2, rows, width)), jax.ShapeDtypeStruct((2, rows, width), LOW)),
             (full(rows_in.shape), low),
         ],
-        [pltpu.VMEM((rows, width), LOW)],
+        [],
         6 * rows * width * width,
         (rows_in, vec, attn),
     )
 
 
-def attend_kernel(q_ref, k0, k1, v0, v1, mask_ref, o_ref, wide_ref, p_ref):
-    bias0, bias1 = mask_ref[:, 0:1], mask_ref[:, 1:2]
-    outs = []
-    for head in range(q_ref.shape[1] // HD):
-        at = slice(head * HD, head * HD + HD)
-        q = (q_ref[:, at].astype(WIDE) * (HD**-0.5)).astype(LOW)
-        s0 = nt(k0[:, at], q) + bias0
-        s1 = nt(k1[:, at], q) + bias1
-        top = jnp.maximum(jnp.max(s0, 0, keepdims=True), jnp.max(s1, 0, keepdims=True))
-        e0 = jnp.exp(s0 - top)
-        e1 = jnp.exp(s1 - top)
-        scale = 1.0 / (jnp.sum(e0, 0, keepdims=True) + jnp.sum(e1, 0, keepdims=True))
-        p0 = (e0 * scale).astype(LOW)
-        p1 = (e1 * scale).astype(LOW)
-        p_ref[head, 0] = p0
-        p_ref[head, 1] = p1
-        outs.append(tn(v0[:, at], p0) + tn(v1[:, at], p1))
+PAD = 32
+GROUP = 4
+
+
+def of_head(value, head):
+    lane = lax.broadcasted_iota(jnp.int32, (1, value.shape[1]), 1)
+    return jnp.where((lane >= head * HD) & (lane < (head + 1) * HD), value, jnp.zeros_like(value))
+
+
+def attend_kernel(q_ref, k0, k1, v0, v1, mask_ref, o_ref, wide_ref, scale_ref, p_ref, score_ref):
+    rows = q_ref.shape[0]
+    heads = q_ref.shape[1] // HD
+    q = (q_ref[...].astype(WIDE) * (HD**-0.5)).astype(LOW)
+    tops, totals, sums, outs, scales = {}, {}, {}, [], []
+
+    def put(store, head, value, join):
+        store[head] = join(store[head], value) if head in store else value
+
+    for turn in range(heads + 2):
+        for half, (k, v) in enumerate(((k0, v0), (k1, v1))):
+            head = turn
+            if head < heads:
+                lanes = slice(head // 2 * 128, head // 2 * 128 + 128)
+                score = nt(k[:, lanes], of_head(q[:, lanes], head % 2))
+                first = score[:PAD] + mask_ref[:PAD, half : half + 1]
+                score_ref[head % 2, half, :PAD] = first
+                score_ref[head % 2, half, PAD:] = score[PAD:]
+                put(tops, head, jnp.max(first, 0, keepdims=True), jnp.maximum)
+                put(tops, head, jnp.max(score[PAD:], 0, keepdims=True), jnp.maximum)
+            head = turn - 1
+            if 0 <= head < heads:
+                power = jnp.exp(score_ref[head % 2, half] - tops[head])
+                put(totals, head, jnp.sum(power, 0, keepdims=True), jnp.add)
+                p_ref[head, half] = power.astype(LOW)
+            head = turn - 2
+            if 0 <= head < heads:
+                lanes = slice(head // 2 * 128, head // 2 * 128 + 128)
+                put(sums, head, tn(v[:, lanes], p_ref[head, half]), jnp.add)
+        head = turn - 2
+        if 0 <= head < heads:
+            scale = 1.0 / totals[head]
+            outs.append(sums[head][head % 2 * HD : (head % 2 + 1) * HD] * scale)
+            scales.append(jnp.broadcast_to(scale, (HD, rows)))
     out = jnp.concatenate(outs, 0).T
     wide_ref[...] = out
     o_ref[...] = out.astype(LOW)
+    scale_ref[...] = jnp.concatenate(scales, 0).T
 
 
 def attend(q, kv0, kv1, mask):
     rows, width = q.shape
-    steps, heads = width // 128, width // HD
-    one = pl.BlockSpec((rows, 128), lambda i: (0, i))
-    key = pl.BlockSpec((None, rows, 128), lambda i: (0, 0, i))
-    value = pl.BlockSpec((None, rows, 128), lambda i: (1, 0, i))
+    heads = width // HD
+    lanes = GROUP * HD
+    one = pl.BlockSpec((rows, lanes), lambda i: (0, i))
+    key = pl.BlockSpec((None, rows, lanes), lambda i: (0, 0, i))
+    value = pl.BlockSpec((None, rows, lanes), lambda i: (1, 0, i))
     return compute_call(
         attend_kernel,
-        steps,
+        heads // GROUP,
         [one, key, key, value, value, full(mask.shape)],
         [
             (one, jax.ShapeDtypeStruct((rows, width), LOW)),
             (one, jax.ShapeDtypeStruct((rows, width), WIDE)),
+            (one, jax.ShapeDtypeStruct((rows, width), WIDE)),
             (
-                pl.BlockSpec((2, 2, rows, rows), lambda i: (i, 0, 0, 0)),
+                pl.BlockSpec((GROUP, 2, rows, rows), lambda i: (i, 0, 0, 0)),
                 jax.ShapeDtypeStruct((heads, 2, rows, rows), LOW),
             ),
         ],
-        [],
+        [pltpu.VMEM((2, 2, rows, rows), WIDE)],
         32 * heads * rows * rows * HD,
         (q, kv0, kv1, kv0, kv1, mask),
     )
@@ -691,7 +809,7 @@
 
 
 def mlp(rows_in, out, vec, bias, weights):
-    attn, fc1, fc2 = weights
+    _, w_out, fc1, fc2 = weights
     rows, width = rows_in.shape
     hidden = fc1.shape[1]
     low = (full(rows_in.shape), jax.ShapeDtypeStruct((rows, width), LOW))
@@ -706,32 +824,29 @@
             full(rows_in.shape),
             full(vec.shape),
             pl.BlockSpec((8, CHUNK), lambda i: (0, i)),
-            pl.BlockSpec((None, width, width), lambda i: (3, 0, 0)),
+            full((width, width)),
             weight,
             weight,
         ],
         [wide, low, wide, low, units, units, low],
         [pltpu.VMEM((rows, width), WIDE)],
         4 * rows * width * hidden,
-        (rows_in, out, vec, bias, attn, fc1, fc2),
-    )
-
-
-def store_halves(value, even_first, own_ref, there_ref, lead=()):
-    count = own_ref.shape[len(lead)]
-    size = own_ref.shape[len(lead) + 1]
+        (rows_in, out, vec, bias, w_out, fc1, fc2),
+    )
+
+
+def own_rows_first(dst, value, c, count):
+    size = value.shape[0] // (2 * count)
     for d in range(2 * count):
-        part = value[d * size : (d + 1) * size].astype(LOW)
-
-        def put(ref, part=part, d=d):
-            ref[lead + (d // 2,)] = part
-
-        if d % 2 == 0:
-            pl.when(even_first)(lambda: put(own_ref))
-            pl.when(jnp.logical_not(even_first))(lambda: put(there_ref))
-        else:
-            pl.when(even_first)(lambda: put(there_ref))
-            pl.when(jnp.logical_not(even_first))(lambda: put(own_ref))
+        at = lax.rem(c + d, 2) * count + d // 2
+        dst[pl.ds(pl.multiple_of(at * size, size), size)] = value[d * size : (d + 1) * size]
+
+
+def store_halves(value, own_ref, there_ref):
+    count, size, _ = own_ref.shape
+    for i in range(count):
+        own_ref[i] = value[i * size : (i + 1) * size].astype(LOW)
+        there_ref[i] = value[(count + i) * size : (count + i + 1) * size].astype(LOW)
 
 
 def mlp_back_kernel(
@@ -739,22 +854,22 @@
     grad_ref, do_ref, own1, there1, own2, there2, own_o, there_o, sums_ref, units_ref, dm, dm_t, n_t, total,
 ):
     step = pl.program_id(0)
-    even = c_ref[0] == 0
+    c, count = c_ref[0], own1.shape[0]
 
     @pl.when(step == 0)
     def _():
         low = (dy_ref[...] * vec_ref[SCALE_MLP][None]).astype(LOW)
         dm[...] = low
-        dm_t[...] = low.T
-        n_t[...] = n_ref[...].T
+        own_rows_first(dm_t, low.T, c, count)
+        own_rows_first(n_t, n_ref[...].T, c, count)
         sums_ref[0:1] = column_sum(dy_ref[...] * two_ref[...].astype(WIDE))
         sums_ref[1:2] = column_sum(low)
         total[...] = jnp.zeros_like(total)
 
     df = (nn(dm[...], w2_ref[...]) * slope_ref[...].astype(WIDE)).astype(LOW)
     units_ref[...] = jnp.broadcast_to(column_sum(df), units_ref.shape)
-    store_halves(nn(dm_t[...], act_ref[...]), even, own2, there2)
-    store_halves(nn(n_t[...], df), even, own1, there1)
+    store_halves(nn(dm_t[...], act_ref[...]), own2, there2)
+    store_halves(nn(n_t[...], df), own1, there1)
     total[...] += nt(df, w1_ref[...])
 
     @pl.when(step == pl.num_programs(0) - 1)
@@ -769,11 +884,12 @@
         sums_ref[5:6] = column_sum(da)
         sums_ref[6:8] = jnp.zeros((2, sums_ref.shape[1]), WIDE)
         do_ref[...] = nn(da, wo_ref[...]).astype(LOW)
-        store_halves(tn(da, o_ref[...]), even, own_o, there_o)
+        own_rows_first(dm_t, da.T, c, count)
+        store_halves(nn(dm_t[...], o_ref[...]), own_o, there_o)
 
 
 def mlp_back(half, dy, vec, saved, weights, count):
-    attn, fc1, fc2 = weights
+    _, w_out, fc1, fc2 = weights
     rows, width = dy.shape
     hidden = fc1.shape[1]
     block = width // (2 * count)
@@ -801,7 +917,7 @@
             whole,
             whole,
             whole,
-            pl.BlockSpec((None, width, width), lambda i: (3, 0, 0)),
+            full((width, width)),
             weight,
             weight,
         ],
@@ -835,34 +951,38 @@
             saved["middle"],
             saved["branch"],
             saved["out"],
-            attn,
+            w_out,
             fc1,
             fc2,
         ),
     )
 
 
-def attend_back_kernel(q_ref, k0, k1, v0, v1, p_ref, g_ref, o_ref, d0_ref, d1_ref):
-    outs = []
+def attend_back_kernel(q_ref, k0, k1, v0, v1, p_ref, g_ref, o_ref, scale_ref, d0_ref, d1_ref):
+    q = q_ref[...]
+    scaled = (g_ref[...].astype(WIDE) * scale_ref[...]).astype(LOW)
+    dots = (scaled.astype(WIDE) * o_ref[...]).T
+    sums = {}
+    dqs = []
     for head in range(q_ref.shape[1] // HD):
-        at = slice(head * HD, head * HD + HD)
-        q = q_ref[:, at]
-        g = g_ref[:, at]
-        prod = g.astype(WIDE) * o_ref[:, at]
-        dot = jnp.sum(prod.T, 0, keepdims=True)
+        g, here = of_head(scaled, head), of_head(q, head)
+        dot = jnp.sum(dots[head * HD : (head + 1) * HD], 0, keepdims=True)
         dq = None
-        for half, (k, v, out, first) in enumerate(((k0, v0, d0_ref, 1), (k1, v1, d1_ref, 0))):
+        for half, (k, v) in enumerate(((k0, v0), (k1, v1))):
             p = p_ref[head, half]
-            out[first + 1, :, at] = nn(p, g).astype(LOW)
-            ds = (p.astype(WIDE) * (nt(v[:, at], g) - dot)).astype(LOW)
-            part = tn(k[:, at], ds)
+            ds = (p.astype(WIDE) * (nt(v[...], g) - dot)).astype(LOW)
+            part = tn(k[...], ds)
             dq = part if dq is None else dq + part
-            out[first, :, at] = (nn(ds, q) * (HD**-0.5)).astype(LOW)
-        outs.append(dq * (HD**-0.5))
-    d0_ref[0] = jnp.concatenate(outs, 0).T.astype(LOW)
-
-
-def attend_back(q, kv0, kv1, probs, grad, out):
+            for name, value in (("v", nn(p, g)), ("k", nn(ds, here))):
+                sums[name, half] = value if head == 0 else sums[name, half] + value
+        dqs.append(dq[head * HD : (head + 1) * HD])
+    d0_ref[0] = (jnp.concatenate(dqs, 0).T * (HD**-0.5)).astype(LOW)
+    for half, (out, first) in enumerate(((d0_ref, 1), (d1_ref, 0))):
+        out[first] = (sums["k", half] * (HD**-0.5)).astype(LOW)
+        out[first + 1] = sums["v", half].astype(LOW)
+
+
+def attend_back(q, kv0, kv1, probs, grad, out, scales):
     rows, width = q.shape
     steps, heads = width // 128, width // HD
     one = pl.BlockSpec((rows, 128), lambda i: (0, i))
@@ -878,11 +998,11 @@
     return compute_call(
         attend_back_kernel,
         steps,
-        [one, key, key, value, value, pl.BlockSpec((2, 2, rows, rows), lambda i: (i, 0, 0, 0)), one, one],
+        [one, key, key, value, value, pl.BlockSpec((2, 2, rows, rows), lambda i: (i, 0, 0, 0)), one, one, one],
         [several(3), several(2)],
         [],
         40 * heads * rows * rows * HD,
-        (q, kv0, kv1, kv0, kv1, probs, grad, out),
+        (q, kv0, kv1, kv0, kv1, probs, grad, out, scales),
     )
 
 
@@ -890,16 +1010,16 @@
     c_ref, d0_ref, d1_ref, n_ref, x_ref, grad_ref, vec_ref, w_ref, dx_ref, own, there, sums_ref, n_t, total
 ):
     step = pl.program_id(0)
-    even = c_ref[0] == 0
+    c, count = c_ref[0], own.shape[0]
 
     @pl.when(step == 0)
     def _():
         total[...] = jnp.zeros_like(total)
-        n_t[...] = n_ref[...].T
+        own_rows_first(n_t, n_ref[...].T, c, count)
 
     theirs = jnp.where(step == 0, 0.0, d1_ref[...].astype(WIDE))
     grad = (d0_ref[...].astype(WIDE) + theirs).astype(LOW)
-    store_halves(nn(n_t[...], grad), even, own, there)
+    store_halves(nn(n_t[...], grad), own, there)
     total[...] += nt(grad, w_ref[...])
     sums = column_sum(grad)
 
@@ -961,7 +1081,7 @@
 def layer_forward(rows_in, vec, bias, weights, mask, from_pair, meanwhile):
     n_one, kv0, q = project(rows_in, vec, weights[0])
     kv1 = from_pair(kv0)
-    out, out_wide, probs = attend(q, kv0, kv1, mask)
+    out, out_wide, scales, probs = attend(q, kv0, kv1, mask)
     out = meanwhile(0, q, out)
     leaving, branch, middle, n_two, active, slope, two = mlp(rows_in, out, vec, bias, weights)
     leaving = meanwhile(1, out, leaving)
@@ -973,6 +1093,7 @@
         kv1=kv1,
         out=out,
         out_wide=out_wide,
+        scales=scales,
         probs=probs,
         branch=branch,
         middle=middle,
@@ -990,7 +1111,7 @@
         half, grad_rows, vec, saved, weights, count
     )
     d_out = meanwhile("fc2", grad_rows, d_out)
-    d0, d1 = attend_back(saved["q"], saved["kv0"], saved["kv1"], saved["probs"], d_out, saved["out_wide"])
+    d0, d1 = attend_back(saved["q"], saved["kv0"], saved["kv1"], saved["probs"], d_out, saved["out_wide"], saved["scales"])
     own, there = dict(out=own_o, fc1=own1, fc2=own2), dict(out=there_o, fc1=there1, fc2=there2)
     d0 = meanwhile("fc1", d_out, d0)
     d1 = from_pair(d1)
@@ -998,7 +1119,6 @@
     grad_in, own["qkv"], there["qkv"], sums_one = project_back(
         half, d0, d1, saved, grad_middle, vec, weights[0], count
     )
-    grad_in = sums_over(dict(qkv=own["qkv"]), dict(qkv=there["qkv"]), grad_in)
     grad_in = meanwhile("out", d0, grad_in)
     grad_in = meanwhile("qkv", d0, grad_in)
     vectors = dict(
@@ -1044,7 +1164,7 @@
     _, micros, images, seq_len, columns = boundary.shape
     S, DP, MP = place.S, place.DP, place.MP
     width = columns * MP
-    rows = -(-seq_len // 32) * 16
+    rows = half_rows(seq_len)
     pieces = 2 * micros
     number = place.s * MP + place.z
     active = number < pieces
@@ -1086,28 +1206,36 @@
     def by_column(value):
         return jnp.stack([value[:, i * columns : (i + 1) * columns].astype(LOW) for i in range(MP)])
 
-    waiting, above = {}, {}
+    waiting, above, projections = {}, {}, []
+
+    def join(name, own, got):
+        axis = own.ndim - 3
+
+        def row(r):
+            at = lax.rem(place.y + r, DP // 2)
+            return pick(own, at, axis).astype(WIDE) + pick(got, at, axis).astype(WIDE)
+
+        others = [row(r).astype(LOW) for r in range(1, DP // 2)]
+        waiting[name] = (row, others)
+        return others
 
     def sums_over(own, there, before):
         parts = []
         for name in own:
-            axis = own[name].ndim - 3
-            got = from_pair(there[name])
-
-            def row(r, value=own[name], got=got, axis=axis):
-                at = lax.rem(place.y + r, DP // 2)
-                return pick(value, at, axis).astype(WIDE) + pick(got, at, axis).astype(WIDE)
-
-            others = [row(r).astype(LOW) for r in range(1, DP // 2)]
-            parts += others
-            waiting[name] = (row, others)
+            parts += join(name, own[name], from_pair(there[name]))
         return after(before, *parts)
 
     def rows_meanwhile(name, before, done):
+        if name == "fc2":
+            own, there = projections
+            got, done = lax.optimization_barrier((from_pair(after(there, before)), done))
+            projections[:] = [own, got]
         row, others = waiting[name]
         got = [from_row(after(part, before), DP // 2 - r) for r, part in enumerate(others, 1)]
         got, done = lax.optimization_barrier((got, done))
         above[name] = (row, got)
+        if name == "fc1":
+            done = after(done, *join("qkv", *projections))
         return done
 
     def sums_done(name):
@@ -1117,52 +1245,39 @@
             total = total + other.astype(WIDE)
         return total.astype(LOW)
 
-    def first_unit(at, weight):
-        return weight.shape[-1] // 2 if at == 1 else 0
-
-    def own_block(at, weight):
+    def from_rows(value, began):
+        return [from_row(after(value, began), r) for r in range(1, DP // 2)]
+
+    def from_section(value):
+        return lax.ppermute(value, "section", [(i, S - 1 - i) for i in range(S)])
+
+    def put_rows(weight, got, first=0):
         axis, block = weight.ndim - 2, weight.shape[-2] // DP
-        weight = weight[..., first_unit(at, weight) :]
-        return lax.dynamic_slice_in_dim(weight, place.d * block, block, axis)
-
-    def fill_rows(layer, at, weight, began, done):
-        axis, block = weight.ndim - 2, weight.shape[-2] // DP
-        value = after(sliced[layer][at], began)
-        for r in range(1, DP // 2):
-            got, done = lax.optimization_barrier((from_row(value, r), done))
+        for r, value in enumerate(got, 1):
             row = lax.rem(place.y + r, DP // 2) * 2
-            for rows_of, part in ((row + place.c, got), (row + 1 - place.c, from_pair(got))):
+            for rows_of, part in ((row + place.c, value), (row + 1 - place.c, from_pair(value))):
                 start = [jnp.int32(0)] * weight.ndim
-                start[axis], start[-1] = rows_of * block, jnp.int32(first_unit(at, weight))
+                start[axis], start[-1] = rows_of * block, jnp.int32(first)
                 weight = lax.dynamic_update_slice(weight, part, start)
-        return weight, done
-
-    images_low = boundary.reshape(micros, seq_len, columns).astype(LOW)
-    sent = jnp.pad(images_low, ((0, 0), (0, 2 * rows - seq_len), (0, 0))).reshape(pieces, rows, columns)
-    keys = jnp.arange(rows)[:, None] + rows * jnp.stack([place.c, 1 - place.c])[None]
-    mask = jnp.where(keys < seq_len, 0.0, -1e30).astype(WIDE)
+        return weight
+
+    spare = jnp.arange(rows)[:, None] < 2 * rows - seq_len
+    mask = jnp.where(spare & (jnp.stack([place.c, 1 - place.c]) == 1)[None], -1e30, 0.0).astype(WIDE)
     mask = jnp.pad(mask, ((0, 0), (0, 126)))
     half = place.c.reshape(1)
     narrow = (ln1_gain, ln1_bias, b_query, b_value, b_out, scale_attn, ln2_gain, ln2_bias, b_fc2, scale_mlp)
-    packed = jnp.concatenate([v[0] for v in narrow] + [b_fc1[0]])
-    lines = -(-packed.shape[0] // 1024) * 8
-    packed = jnp.pad(packed, (0, lines * 128 - packed.shape[0])).reshape(lines, 128)
-    attn_shard = jnp.stack([w_query[0], w_key[0], w_value[0], w_out[0].T])
-    arrived, vecs, weights = gather(sent, packed, attn_shard, w_fc1[0], w_fc2[0].T)
-    sliced = {layer: [own_block(at, w) for at, w in enumerate(weights[layer])] for layer in range(1, S)}
-    arrived = after(arrived, *(w for layer in sliced for w in sliced[layer]))
+    table = jnp.concatenate(list(narrow) + [jnp.zeros((16 - len(narrow), columns), WIDE)], 0)
+    bias = jnp.broadcast_to(b_fc1, (8, b_fc1.shape[1]))
+    qkv_shard = jnp.stack([w_query[0], w_key[0], w_value[0]])
+    tokens = boundary.reshape(micros, seq_len, 1, columns)
+    (arrived, sent, tables, all_biases), weights, later = gather(
+        tokens, table, bias, qkv_shard, w_out[0].T, w_fc1[0], w_fc2[0].T
+    )
     arrived = jnp.where(active, arrived.astype(WIDE), 0.0)
-    vecs = vecs.reshape(S, MP, -1)
-    vectors, biases = [], []
-    for layer in range(S):
-        start = len(NARROW) * columns
-        table = vecs[layer, :, :start].reshape(MP, len(NARROW), columns)
-        table = jnp.moveaxis(table, 0, 1).reshape(len(NARROW), width)
-        vectors.append(jnp.pad(table, ((0, 16 - len(NARROW)), (0, 0))))
-        bias = vecs[layer, :, start : start + b_fc1.shape[1]].reshape(1, -1)
-        biases.append(jnp.pad(bias, ((0, 7), (0, 0))))
-
-    saved, cotangent = [], []
+    vectors = [tables[layer] for layer in range(S)]
+    biases = [all_biases[layer] for layer in range(S)]
+
+    saved, cotangent, halves = [], [], []
     split = [range(turns)[i * turns // 3 : (i + 1) * turns // 3] for i in range(3)]
     rows_now = arrived
     for layer in range(S):
@@ -1170,9 +1285,25 @@
             at = 2 * layer + stage
             if at > 2:
                 return done
-            few, done = lax.optimization_barrier((bring(sent, split[at], before), done))
-            cotangent.extend(few)
-            weights[1][at], done = fill_rows(1, at, weights[1][at], before, done)
+            got = bring(sent, split[at], before)
+            if at == 0:
+                got, new, done = lax.optimization_barrier((got, from_rows(later[0], before), done))
+                weights[1][0] = put_rows(weights[1][0], new)
+            elif at == 1:
+                got, new, done = lax.optimization_barrier((got, from_rows(later[3], before), done))
+                halves.extend(new)
+            else:
+                new = ([from_section(after(h, before)) for h in halves], from_rows(later[2], before), from_rows(later[1], before))
+                got, new, done = lax.optimization_barrier((got, new, done))
+                first = place.s == 0
+                fc2 = [
+                    jnp.where(first, jnp.concatenate([h, o], -1), jnp.concatenate([o, h], -1))
+                    for h, o in zip(halves, new[0])
+                ]
+                weights[1][3] = put_rows(weights[1][3], fc2)
+                weights[1][2] = put_rows(weights[1][2], new[1], weights[1][2].shape[-1] // 2)
+                weights[1][1] = put_rows(weights[1][1], new[2])
+            cotangent.extend(got)
             return done
 
         rows_now, kept = layer_forward(
@@ -1193,11 +1324,12 @@
             (lambda name, before, done: done) if layer else rows_meanwhile,
         )
         if layer:
+            projections[:] = [own["qkv"], there["qkv"]]
             grad_now = grad_now.astype(LOW).astype(WIDE)
 
     above = {name: sums_done(name) for name in ("fc2", "fc1", "out", "qkv")}
     grads = dict(own=own, there=there, above=above, pieces=pieces)
-    shapes = [(3,) + w_query.shape[1:], w_query.shape[1:], w_fc1.shape[1:], (w_fc2.shape[2], w_fc2.shape[1])]
+    shapes = [qkv_shard.shape, w_query.shape[1:], w_fc1.shape[1:], (w_fc2.shape[2], w_fc2.shape[1])]
     names = NARROW + ("b_fc1",)
     table = jnp.stack(
         [
@@ -1208,34 +1340,27 @@
     lines = -(-table.shape[3] // 1024) * 8
     table = jnp.pad(table, ((0, 0), (0, 0), (0, 0), (0, lines * 128 - table.shape[3])))
     table = table.reshape(S, MP, DP // 2, 2, lines, 128).transpose(3, 0, 2, 1, 4, 5)
-    ends, summed, g_qkv, g_out, g_fc1, g_fc2 = scatter(
-        table, by_column(grad_now), by_column(end_rows), grads, shapes, (micros, seq_len, columns)
-    )
-    ends_out = ends.astype(WIDE).reshape(boundary.shape)
-    summed = summed.reshape(-1)
-    v, start = {}, 0
-    for name in names:
-        size = (b_fc1.shape[1] if name == "b_fc1" else columns) // DP
-        v[name] = summed[start : start + size][None]
-        start += size
-
+    ends, summed, *sums = scatter(table, by_column(grad_now), by_column(end_rows), grads, shapes)
+    sizes = [columns // DP] * len(NARROW) + [b_fc1.shape[1] // DP]
+    ends, g_query, g_key, g_value, g_out, g_fc1, g_fc2, *vector_sums = finish(ends, summed, sums, seq_len, sizes)
+    v = dict(zip(names, vector_sums))
     return (
-        ends_out,
+        ends.reshape(boundary.shape),
         v["ln1_gain"],
         v["ln1_bias"],
-        g_qkv[0][None],
-        g_qkv[1][None],
-        g_qkv[2][None],
+        g_query[None],
+        g_key[None],
+        g_value[None],
         v["b_query"],
         v["b_value"],
-        g_out.T[None],
+        g_out[None],
         v["b_out"],
         v["scale_attn"],
         v["ln2_gain"],
         v["ln2_bias"],
         g_fc1[None],
         v["b_fc1"],
-        g_fc2.T[None],
+        g_fc2[None],
         v["b_fc2"],
         v["scale_mlp"],
     )

time: 975 us -> 922 us (0.946)
  local copies, waits for them, and re-layouts: 83.6 us -> 48.6 us
  Pallas kernels: 774 us -> 757 us
    pallas_call x12, Pallas kernels: 375 us -> 342 us  [compute_call(): pl.pallas_call(kernel, grid=(steps,), in_specs=ins, out_specs=[spec for s...]
    unnamed x73 -> x61, local copies, waits for them, and re-layouts: 37.3 us -> 18.8 us
    pallas_call x1 -> x2, Pallas kernels: 187 us -> 204 us  [the longest x1 200 us: gather(): pl.pallas_call(functools.partial(gather_kernel, pieces), in_specs=[vmem]...]
  transfers between devices with their start and end apart: 24 -> 27, of which waited for: 4 -> 4; matrix products, arithmetic and copies ran while one was open for 6% -> 6% of each run, Pallas kernels for 27% -> 25%
where the time goes in v3:
time: 922 us; the launch traced here: 909 us
  Pallas kernels  757 us (82%)
  other arithmetic  48.7 us (5%)
  local copies, waits for them, and re-layouts  48.6 us (5%)
  starting transfers between devices  27.3 us (3%)
  waiting for transfers between devices  25 us (3%)
    pallas_call x12, Pallas kernels, compute_call(): pl.pallas_call(kernel, grid=(steps,), in_specs=ins, out_specs=[spec for s...  342 us
    pallas_call x1, Pallas kernels, scatter(): pl.pallas_call(functools.partial(scatter_kernel, pieces), in_specs=[vmem]...  211 us
    pallas_call x1, Pallas kernels, gather(): pl.pallas_call(functools.partial(gather_kernel, pieces), in_specs=[vmem]...  200 us
    unnamed x61, local copies, waits for them, and re-layouts  18.8 us
  transfers between devices with their start and end apart: 27, of which 4 were waited for; matrix products, arithmetic and copies ran while one was open for 6% of the time, Pallas kernels for 25%

profile of v3, /device:TPU:26, one launch (start us, length us, event | category | flops | bytes accessed | tf_op | source)
XLA Modules:
  0.0 908.5 jit_solution(100838798999204329)
XLA Ops:
  0.7 1.7 copy.42
  2.3 2.0 copy.43
  4.4 1.8 pad_maximum_fusion.2.refs_0_
  6.2 2.7 concatenate.22.vec_ref
  8.9 1.3 broadcast_in_dim.45.bias_ref
  10.2 200.2 %shard_map.313 = (bf16[688,1024]{1,0:T(8,128)(2,1)}, bf16[6,688,256]{2,1,0:T(8,128)(2,1)}, f32[2,16,1024]{2,1,0:T(8,128)}, f32[2,8,4096]{2,1,0:T(8,128)}, bf16[3...) custom-call(f32[3,1370,1,256]{3,2,1,0:T(1,128)} %bitcast.105, ...), custom_call_target="tpu_custom_call" | custom-call | tf_op jit(solution)/shard_map/pallas_call | solution.py:314
  210.4 1.5 slice_bitcast_fusion.10
  211.9 3.3 convert_select_fusion.1.x_ref
  215.2 10.5 %shard_map.314 = (bf16[688,1024]{1,0:T(8,128)(2,1)}, bf16[2,688,1024]{2,1,0:T(8,128)(2,1)}, bf16[688,1024]{1,0:T(8,128)(2,1)}) custom-call(f32[688,1024]{1,0:T(8,128)} %convert_select_fusion.1.x_ref, f32[16,1024]{1,0:T(8,128)} %get-tuple-element.381.vec_ref, bf16[3,1024,1024]{2,1,0:T(8,128)(2,1)} %get-tuple-element.163.w_ref), custom_call_target="tpu_custom_call" | custom-call | flops 1000 | bytes 1000 | tf_op jit(solution)/shard_map/pallas_call | solution.py:651
  227.0 2.8 dynamic-slice_bitcast_fusion.4
  229.9 1.3 collective-permute-start
  231.2 6.1 collective-permute-start.1
  238.3 1.6 copy-done.6
  239.9 31.2 %shard_map.315 = (bf16[688,1024]{1,0:T(8,128)(2,1)}, f32[688,1024]{1,0:T(8,128)}, f32[688,1024]{1,0:T(8,128)}, bf16[16,2,688,688]{3,2,1,0:T(8,128)(2,1)}) custom-call(bf16[688,1024]{1,0:T(8,128)(2,1)} %get-tuple-element.164.q_ref, bf16[2,688,1024]{2,1,0:T(8,128)(2,1)} %get-tuple-element.169.k0.v0, bf16[2,688,1024]{2,1,0:T(8,128)(2,1)} %copy-done.6, ...), custom_call_target="tpu_custom_call" | custom-call | flops 1000 | bytes 1000 | tf_op jit(solution)/shard_map/pallas_call | solution.py:651
  271.2 2.8 collective-permute-start.4
  274.0 2.0 collective-permute-start.5
  276.0 1.7 collective-permute-start.6
  278.4 27.9 %shard_map.316 = (f32[688,1024]{1,0:T(8,128)}, bf16[688,1024]{1,0:T(8,128)(2,1)}, f32[688,1024]{1,0:T(8,128)}, bf16[688,1024]{1,0:T(8,128)(2,1)}, bf16[688,4096]...) custom-call(f32[688,1024]{1,0:T(8,128)} %convert_select_fusion.1.x_ref, ...), custom_call_target="tpu_custom_call" | custom-call | flops 1000 | bytes 1000 | tf_op jit(solution)/shard_map/pallas_call | solution.py:651
  306.3 2.8 constant_dynamic-update-slice_fusion.5
  309.2 1.8 convert_convert_fusion.1.x_ref
  311.0 1.3 constant_dynamic-update-slice_fusion.4.w_ref
  312.3 10.3 %shard_map.317 = (bf16[688,1024]{1,0:T(8,128)(2,1)}, bf16[2,688,1024]{2,1,0:T(8,128)(2,1)}, bf16[688,1024]{1,0:T(8,128)(2,1)}) custom-call(f32[688,1024]{1,0:T(8,128)} %convert_convert_fusion.1.x_ref, f32[16,1024]{1,0:T(8,128)} %get-tuple-element.380.vec_ref, bf16[3,1024,1024]{2,1,0:T(8,128)(2,1)} %constant_dynamic-update-slice_fusion.4.w_ref), custom_call_target="tpu_custom_call" | custom-call | flops 1000 | bytes 1000 | tf_op jit(solution)/shard_map/pallas_call | solution.py:651
  323.1 1.7 collective-permute-start.12
  324.7 2.3 collective-permute-start.8
  328.0 2.7 collective-permute-start.9
  331.7 31.4 %shard_map.318 = (bf16[688,1024]{1,0:T(8,128)(2,1)}, f32[688,1024]{1,0:T(8,128)}, f32[688,1024]{1,0:T(8,128)}, bf16[16,2,688,688]{3,2,1,0:T(8,128)(2,1)}) custom-call(bf16[688,1024]{1,0:T(8,128)(2,1)} %get-tuple-element.188.q_ref, bf16[2,688,1024]{2,1,0:T(8,128)(2,1)} %get-tuple-element.197.k0.v0, bf16[2,688,1024]{2,1,0:T(8,128)(2,1)} %copy-done.7, ...), custom_call_target="tpu_custom_call" | custom-call | flops 1000 | bytes 1000 | tf_op jit(solution)/shard_map/pallas_call | solution.py:651
  363.2 3.7 constant_dynamic-update-slice_fusion.1
  367.1 1.0 bitcast_dynamic-update-slice_fusion.3
  368.1 1.0 bitcast_dynamic-update-slice_fusion.2
  370.7 1.0 bitcast_dynamic-update-slice_fusion
  372.7 2.0 convert_select_fusion.dy_ref
  374.7 2.4 constant_dynamic-update-slice_fusion.7
  377.9 1.2 constant_dynamic-update-slice_fusion.6.w1_ref
  379.1 1.5 constant_dynamic-update-slice_fusion.w2_ref
  380.6 27.3 %shard_map.319 = (f32[688,1024]{1,0:T(8,128)}, bf16[688,1024]{1,0:T(8,128)(2,1)}, f32[688,1024]{1,0:T(8,128)}, bf16[688,1024]{1,0:T(8,128)(2,1)}, bf16[688,4096]...) custom-call(f32[688,1024]{1,0:T(8,128)} %convert_convert_fusion.1.x_ref, ...), custom_call_target="tpu_custom_call" | custom-call | flops 1000 | bytes 1000 | tf_op jit(solution)/shard_map/pallas_call | solution.py:651
  407.9 43.5 %shard_map.320 = (f32[688,1024]{1,0:T(8,128)}, bf16[688,1024]{1,0:T(8,128)(2,1)}, bf16[2,256,4096]{2,1,0:T(8,128)(2,1)}, bf16[2,256,4096]{2,1,0:T(8,128)(2,1)}, ...) custom-call(s32[1]{0:T(128)} %bitcast.c_ref, ...), custom_call_target="tpu_custom_call" | custom-call | flops 1000 | bytes 1000 | tf_op jit(solution)/shard_map/pallas_call | solution.py:651
  451.9 38.9 %shard_map.321 = (bf16[3,688,1024]{2,1,0:T(8,128)(2,1)}, bf16[2,688,1024]{2,1,0:T(8,128)(2,1)}) custom-call(bf16[688,1024]{1,0:T(8,128)(2,1)} %get-tuple-element.188.q_ref, bf16[2,688,1024]{2,1,0:T(8,128)(2,1)} %get-tuple-element.197.k0.v0, bf16[2,688,1024]{2,1,0:T(8,128)(2,1)} %copy-done.7, bf16[2,688,1024]{2,1,0:T(8,128)(2,1)} %get-tuple-element.197.k0.v0, ...), custom_call_target="tpu_custom_call" | custom-call | flops 1000 | bytes 1000 | tf_op jit(solution)/shard_map/pallas_call | solution.py:651
  491.4 6.5 collective-permute-done.19
  497.9 2.2 fusion.7
  500.1 4.5 fusion.3
  504.6 3.7 fusion.4
  508.3 1.6 copy-done.16
  509.8 19.3 %shard_map.322 = (f32[688,1024]{1,0:T(8,128)}, bf16[3,2,256,1024]{3,2,1,0:T(8,128)(2,1)}, bf16[3,2,256,1024]{3,2,1,0:T(8,128)(2,1)}, f32[8,1024]{1,0:T(8,128)}) custom-call(s32[1]{0:T(128)} %bitcast.c_ref, bf16[3,688,1024]{2,1,0:T(8,128)(2,1)} %get-tuple-element.225.d0_ref, bf16[2,688,1024]{2,1,0:T(8,128)(2,1)} %copy-done.16, ...), custom_call_target="tpu_custom_call" | custom-call | flops 1000 | bytes 1000 | tf_op jit(solution)/shard_map/pallas_call | solution.py:651
  529.2 3.9 convert_convert_fusion.dy_ref
  533.1 2.2 copy.44
  535.8 43.4 %shard_map.323 = (f32[688,1024]{1,0:T(8,128)}, bf16[688,1024]{1,0:T(8,128)(2,1)}, bf16[2,256,4096]{2,1,0:T(8,128)(2,1)}, bf16[2,256,4096]{2,1,0:T(8,128)(2,1)}, ...) custom-call(s32[1]{0:T(128)} %bitcast.c_ref, ...), custom_call_target="tpu_custom_call" | custom-call | flops 1000 | bytes 1000 | tf_op jit(solution)/shard_map/pallas_call | solution.py:651
  579.2 4.3 collective-permute-done.21
  583.8 1.1 copy-done.17
  584.9 38.8 %shard_map.324 = (bf16[3,688,1024]{2,1,0:T(8,128)(2,1)}, bf16[2,688,1024]{2,1,0:T(8,128)(2,1)}) custom-call(bf16[688,1024]{1,0:T(8,128)(2,1)} %get-tuple-element.164.q_ref, bf16[2,688,1024]{2,1,0:T(8,128)(2,1)} %get-tuple-element.169.k0.v0, bf16[2,688,1024]{2,1,0:T(8,128)(2,1)} %copy-done.6, bf16[2,688,1024]{2,1,0:T(8,128)(2,1)} %get-tuple-element.169.k0.v0, ...), custom_call_target="tpu_custom_call" | custom-call | flops 1000 | bytes 1000 | tf_op jit(solution)/shard_map/pallas_call | solution.py:651
  625.7 1.3 pad_maximum_fusion.1.last_ref
  628.9 3.4 fusion.5
  633.0 1.3 collective-permute-start.25
  634.4 8.7 fusion
  643.1 19.7 %shard_map.325 = (f32[688,1024]{1,0:T(8,128)}, bf16[3,2,256,1024]{3,2,1,0:T(8,128)(2,1)}, bf16[3,2,256,1024]{3,2,1,0:T(8,128)(2,1)}, f32[8,1024]{1,0:T(8,128)}) custom-call(s32[1]{0:T(128)} %bitcast.c_ref, bf16[3,688,1024]{2,1,0:T(8,128)(2,1)} %get-tuple-element.250.d0_ref, bf16[2,688,1024]{2,1,0:T(8,128)(2,1)} %collective-permute-done.24.d1_ref, ...), custom_call_target="tpu_custom_call" | custom-call | flops 1000 | bytes 1000 | tf_op jit(solution)/shard_map/pallas_call | solution.py:651
  664.9 2.4 fusion.6.refs_9_
  667.3 13.2 %collective-permute-done.25 = bf16[3,256,1024]{2,1,0:T(8,128)(2,1)} collective-permute-done((bf16[3,256,1024]{2,1,0:T(8,128)(2,1)}, bf16[3,256,1024]{2,1,0:T(8,128)(2,1)}, u32[]{:S(2)}, u32[]{:S(2)}) %collective-permute-start.25) | collective-permute-done | bytes 1572896 | tf_op jit(solution)/shard_map/ppermute | solution.py:1176
  680.5 4.1 fusion.2.refs_8_
  684.9 1.3 pad_maximum_fusion.first_ref
  686.1 211.1 %shard_map.326 = (bf16[6,688,256]{2,1,0:T(8,128)(2,1)}, f32[8,128]{1,0:T(8,128)}, f32[3,256,256]{2,1,0:T(8,128)}, f32[256,256]{1,0:T(8,128)}, f32[256,1024]{1,0:T(8,128)}, /*index=5*/f32[256,1024]{1,0:T(8,128)}) custom-call(f32[2,2,2,4,8,128]{5,4,3,2,1,0:T(8,128)} %bitcast.107, bf16[4,688,256]{2,1,0:T(8,128)(2,1)} %pad_maximum_fusion.first_ref, ...), custom_call_target="tpu_custom_call" | custom-call | tf_op jit(solution)/shard_map/pallas_call | solution.py:535
  897.3 1.6 copy-done
  898.8 1.2 copy-done.1
  900.1 1.2 copy-done.2
  901.3 1.1 copy-done.3
  904.1 4.0 shard_map.327
  (137 shorter events, 19.8 us)
Async XLA Ops:
  225.7 12.6 %collective-permute-start.3 = (bf16[2,688,1024]{2,1,0:T(8,128)(2,1)}, bf16[2,688,1024]{2,1,0:T(8,128)(2,1)S(1)}, u32[]{:S(2)}, u32[]{:S(2)}) collective-permute-start(bf16[2,688,1024]{2,1,0:T(8,128)(2,1)} %get-tuple-element.169.k0.v0), channel_id=1, source_target_pairs={{0,4},{4,0},{8,12},{12,8},{1,5},{5,1},{9,13},{13,9},{2,6},{6,2},{1... | collective-permute-start | bytes 8454152 | tf_op jit(solution)/shard_map/ppermute | solution.py:1173
  226.5 44.7 %collective-permute-start.2 = (bf16[3,256,1024]{2,1,0:T(8,128)(2,1)}, bf16[3,256,1024]{2,1,0:T(8,128)(2,1)}, u32[]{:S(2)}, u32[]{:S(2)}) collective-permute-start(bf16[3,256,1024]{2,1,0:T(8,128)(2,1)} %get-tuple-element.168), channel_id=1, source_target_pairs={{0,8},{4,12},{8,0},{12,4},{1,9},{5,13},{9,1},{13,5},{2,10},{6,14},... | collective-permute-start | bytes 4718600 | tf_op jit(solution)/shard_map/ppermute | solution.py:1176
  229.9 41.2 %collective-permute-start = (bf16[688,256]{1,0:T(8,128)(2,1)}, bf16[688,256]{1,0:T(8,128)(2,1)S(1)}, u32[]{:S(2)}, u32[]{:S(2)}) collective-permute-start(bf16[688,256]{1,0:T(8,128)(2,1)} %get-tuple-element.165), channel_id=1, source_target_pairs={{16,0},{17,4},{18,2},{19,6},{20,1},{21,5},{22,3},{23,7},{24,8},{25... | collective-permute-start | bytes 1056776 | tf_op jit(solution)/shard_map/ppermute | solution.py:1184
  231.2 39.9 %collective-permute-start.1 = (bf16[688,256]{1,0:T(8,128)(2,1)}, bf16[688,256]{1,0:T(8,128)(2,1)S(1)}, u32[]{:S(2)}, u32[]{:S(2)}) collective-permute-start(bf16[688,256]{1,0:T(8,128)(2,1)} %get-tuple-element.166), channel_id=1, source_target_pairs={{16,4},{17,2},{18,6},{19,16},{20,5},{21,3},{22,7},{23,17},{24,12},... | collective-permute-start | bytes 1056776 | tf_op jit(solution)/shard_map/ppermute | solution.py:1184
  238.3 39.4 %copy-start.23 = (f32[2,8,4096]{2,1,0:T(8,128)S(1)}, f32[2,8,4096]{2,1,0:T(8,128)}, u32[]{:S(2)}) copy-start(f32[2,8,4096]{2,1,0:T(8,128)} %get-tuple-element.178) | copy-start | bytes 786436
  238.3 1.6 copy-start.6
  271.1 35.2 %copy-start.22 = (bf16[688,256]{1,0:T(8,128)(2,1)}, bf16[688,256]{1,0:T(8,128)(2,1)S(1)}, u32[]{:S(2)}) copy-start(bf16[688,256]{1,0:T(8,128)(2,1)S(1)} %collective-permute-done) | copy-start | bytes 1056772
  271.1 35.2 %copy-start.20 = (bf16[688,256]{1,0:T(8,128)(2,1)}, bf16[688,256]{1,0:T(8,128)(2,1)S(1)}, u32[]{:S(2)}) copy-start(bf16[688,256]{1,0:T(8,128)(2,1)S(1)} %collective-permute-done.1) | copy-start | bytes 1056772
  271.1 39.9 %collective-permute-start.7 = (bf16[3,256,1024]{2,1,0:T(8,128)(2,1)}, bf16[3,256,1024]{2,1,0:T(8,128)(2,1)S(1)}, u32[]{:S(2)}, u32[]{:S(2)}) collective-permute-start(bf16[3,256,1024]{2,1,0:T(8,128)(2,1)} %collective-permute-done.2), channel_id=1, source_target_pairs={{0,4},{4,0},{8,12},{12,8},{1,5},{5,1},{9,13},{13,9},{2,6},{6,2},{1... | collective-permute-start | bytes 4718600 | tf_op jit(solution)/shard_map/ppermute | solution.py:1173
  271.2 38.0 %collective-permute-start.4 = (bf16[688,256]{1,0:T(8,128)(2,1)}, bf16[688,256]{1,0:T(8,128)(2,1)}, u32[]{:S(2)}, u32[]{:S(2)}) collective-permute-start(bf16[688,256]{1,0:T(8,128)(2,1)} %get-tuple-element.174), channel_id=1, source_target_pairs={{16,2},{17,6},{18,16},{19,20},{20,3},{21,7},{22,17},{23,21},{24,10... | collective-permute-start | bytes 1056776 | tf_op jit(solution)/shard_map/ppermute | solution.py:1184
  274.0 35.2 %collective-permute-start.5 = (bf16[688,256]{1,0:T(8,128)(2,1)}, bf16[688,256]{1,0:T(8,128)(2,1)}, u32[]{:S(2)}, u32[]{:S(2)}) collective-permute-start(bf16[688,256]{1,0:T(8,128)(2,1)} %get-tuple-element.175), channel_id=1, source_target_pairs={{16,6},{17,16},{18,20},{19,0},{20,7},{21,17},{22,21},{23,1},{24,14... | collective-permute-start | bytes 1056776 | tf_op jit(solution)/shard_map/ppermute | solution.py:1184
  276.0 33.2 %collective-permute-start.6 = (bf16[256,2048]{1,0:T(8,128)(2,1)}, bf16[256,2048]{1,0:T(8,128)(2,1)S(1)}, u32[]{:S(2)}, u32[]{:S(2)}) collective-permute-start(bf16[256,2048]{1,0:T(8,128)(2,1)} %get-tuple-element.177), channel_id=1, source_target_pairs={{0,8},{4,12},{8,0},{12,4},{1,9},{5,13},{9,1},{13,5},{2,10},{6,14},... | collective-permute-start | bytes 3145736 | tf_op jit(solution)/shard_map/ppermute | solution.py:1176
  306.3 2.9 copy-start.15
  309.2 13.4 %copy-start.18 = (bf16[256,2048]{1,0:T(8,128)(2,1)}, bf16[256,2048]{1,0:T(8,128)(2,1)S(1)}, u32[]{:S(2)}) copy-start(bf16[256,2048]{1,0:T(8,128)(2,1)S(1)} %collective-permute-done.6) | copy-start | bytes 3145732
  322.6 5.4 collective-permute-start.13
  322.6 40.6 %collective-permute-start.10 = (bf16[256,2048]{1,0:T(8,128)(2,1)}, bf16[256,2048]{1,0:T(8,128)(2,1)}, u32[]{:S(2)}, u32[]{:S(2)}) collective-permute-start(bf16[256,2048]{1,0:T(8,128)(2,1)} %copy-done.18), channel_id=1, source_target_pairs={{0,16},{16,0},{1,17},{17,1},{2,18},{18,2},{3,19},{19,3},{4,20},{20... | collective-permute-start | bytes 3145736 | tf_op jit(solution)/shard_map/ppermute | solution.py:1252
  322.6 40.5 %collective-permute-start.11 = (bf16[256,2048]{1,0:T(8,128)(2,1)}, bf16[256,2048]{1,0:T(8,128)(2,1)}, u32[]{:S(2)}, u32[]{:S(2)}) collective-permute-start(bf16[256,2048]{1,0:T(8,128)(2,1)} %get-tuple-element.194), channel_id=1, source_target_pairs={{0,8},{4,12},{8,0},{12,4},{1,9},{5,13},{9,1},{13,5},{2,10},{6,14},... | collective-permute-start | bytes 3145736 | tf_op jit(solution)/shard_map/ppermute | solution.py:1176
  323.1 40.1 %collective-permute-start.12 = (bf16[256,1024]{1,0:T(8,128)(2,1)}, bf16[256,1024]{1,0:T(8,128)(2,1)S(1)}, u32[]{:S(2)}, u32[]{:S(2)}) collective-permute-start(bf16[256,1024]{1,0:T(8,128)(2,1)} %get-tuple-element.196), channel_id=1, source_target_pairs={{0,8},{4,12},{8,0},{12,4},{1,9},{5,13},{9,1},{13,5},{2,10},{6,14},... | collective-permute-start | bytes 1572872 | tf_op jit(solution)/shard_map/ppermute | solution.py:1176
  324.7 38.4 %collective-permute-start.8 = (bf16[688,256]{1,0:T(8,128)(2,1)}, bf16[688,256]{1,0:T(8,128)(2,1)}, u32[]{:S(2)}, u32[]{:S(2)}) collective-permute-start(bf16[688,256]{1,0:T(8,128)(2,1)} %get-tuple-element.189), channel_id=1, source_target_pairs={{16,16},{17,20},{18,0},{19,4},{20,17},{21,21},{22,1},{23,5},{24,24... | collective-permute-start | bytes 1056776 | tf_op jit(solution)/shard_map/ppermute | solution.py:1184
  328.0 3.7 copy-start.7
  328.0 35.1 %collective-permute-start.9 = (bf16[688,256]{1,0:T(8,128)(2,1)}, bf16[688,256]{1,0:T(8,128)(2,1)}, u32[]{:S(2)}, u32[]{:S(2)}) collective-permute-start(bf16[688,256]{1,0:T(8,128)(2,1)} %get-tuple-element.190), channel_id=1, source_target_pairs={{16,20},{17,0},{18,4},{19,2},{20,21},{21,1},{22,5},{23,3},{24,28},... | collective-permute-start | bytes 1056776 | tf_op jit(solution)/shard_map/ppermute | solution.py:1184
  363.1 4.0 copy-start.21
  366.9 12.2 %collective-permute-start.16 = (bf16[256,4096]{1,0:T(8,128)(2,1)S(1)}, bf16[256,4096]{1,0:T(8,128)(2,1)S(1)}, u32[]{:S(2)}, u32[]{:S(2)}) collective-permute-start(bf16[256,4096]{1,0:T(8,128)(2,1)S(1)} %get-tuple-element.359), channel_id=1, source_target_pairs={{0,4},{4,0},{8,12},{12,8},{1,5},{5,1},{9,13},{13,9},{2,6},{6,2},{1... | collective-permute-start | bytes 6291464 | tf_op jit(solution)/shard_map/ppermute | solution.py:1173
  369.2 7.9 collective-permute-start.14
  369.5 8.4 collective-permute-start.15
  451.3 48.7 %collective-permute-start.17 = (bf16[2,256,4096]{2,1,0:T(8,128)(2,1)}, bf16[2,256,4096]{2,1,0:T(8,128)(2,1)}, u32[]{:S(2)}, u32[]{:S(2)}) collective-permute-start(bf16[2,256,4096]{2,1,0:T(8,128)(2,1)} %get-tuple-element.215), channel_id=1, source_target_pairs={{0,4},{4,0},{8,12},{12,8},{1,5},{5,1},{9,13},{13,9},{2,6},{6,2},{1... | collective-permute-start | bytes 12582920 | tf_op jit(solution)/shard_map/ppermute | solution.py:1173
  451.7 52.9 %collective-permute-start.18 = (bf16[2,256,4096]{2,1,0:T(8,128)(2,1)}, bf16[2,256,4096]{2,1,0:T(8,128)(2,1)}, u32[]{:S(2)}, u32[]{:S(2)}) collective-permute-start(bf16[2,256,4096]{2,1,0:T(8,128)(2,1)} %get-tuple-element.217), channel_id=1, source_target_pairs={{0,4},{4,0},{8,12},{12,8},{1,5},{5,1},{9,13},{13,9},{2,6},{6,2},{1... | collective-permute-start | bytes 12582920 | tf_op jit(solution)/shard_map/ppermute | solution.py:1173
  490.8 17.5 %collective-permute-start.20 = (bf16[2,688,1024]{2,1,0:T(8,128)(2,1)}, bf16[2,688,1024]{2,1,0:T(8,128)(2,1)S(1)}, u32[]{:S(2)}, u32[]{:S(2)}) collective-permute-start(bf16[2,688,1024]{2,1,0:T(8,128)(2,1)} %get-tuple-element.226), channel_id=1, source_target_pairs={{0,4},{4,0},{8,12},{12,8},{1,5},{5,1},{9,13},{13,9},{2,6},{6,2},{1... | collective-permute-start | bytes 8454152 | tf_op jit(solution)/shard_map/ppermute | solution.py:1173
  491.1 6.8 collective-permute-start.19
  500.1 4.5 copy-start.9
  508.3 1.6 copy-start.16
  529.2 3.9 copy-start.12
  535.3 43.9 %collective-permute-start.22 = (bf16[3,2,256,1024]{3,2,0,1:T(8,128)(2,1)}, bf16[3,2,256,1024]{3,2,0,1:T(8,128)(2,1)S(1)}, u32[]{:S(2)}, u32[]{:S(2)}) collective-permute-start(bf16[3,2,256,1024]{3,2,0,1:T(8,128)(2,1)} %copy.44), channel_id=1, source_target_pairs={{0,4},{4,0},{8,12},{12,8},{1,5},{5,1},{9,13},{13,9},{2,6},{6,2},{1... | collective-permute-start | bytes 9437192 | tf_op jit(solution)/shard_map/ppermute | solution.py:1173
  535.4 48.1 %collective-permute-start.21 = (bf16[256,4096]{1,0:T(8,128)(2,1)}, bf16[256,4096]{1,0:T(8,128)(2,1)S(1)}, u32[]{:S(2)}, u32[]{:S(2)}) collective-permute-start(bf16[256,4096]{1,0:T(8,128)(2,1)} %fusion.4), channel_id=1, source_target_pairs={{0,8},{4,12},{8,0},{12,4},{1,9},{5,13},{9,1},{13,5},{2,10},{6,14},... | collective-permute-start | bytes 6291464 | tf_op jit(solution)/shard_map/ppermute | solution.py:1176
  579.2 44.5 %copy-start.11 = (bf16[3,2,256,1024]{3,2,0,1:T(8,128)(2,1)}, bf16[3,2,256,1024]{3,2,0,1:T(8,128)(2,1)S(1)}, u32[]{:S(2)}) copy-start(bf16[3,2,256,1024]{3,2,0,1:T(8,128)(2,1)S(1)} %collective-permute-done.22) | copy-start | bytes 9437188
  583.6 1.3 copy-start.17
  583.6 48.8 %collective-permute-start.23 = (bf16[256,4096]{1,0:T(8,128)(2,1)}, bf16[256,4096]{1,0:T(8,128)(2,1)}, u32[]{:S(2)}, u32[]{:S(2)}) collective-permute-start(bf16[256,4096]{1,0:T(8,128)(2,1)} %fusion.3), channel_id=1, source_target_pairs={{0,8},{4,12},{8,0},{12,4},{1,9},{5,13},{9,1},{13,5},{2,10},{6,14},... | collective-permute-start | bytes 6291464 | tf_op jit(solution)/shard_map/ppermute | solution.py:1176
  584.9 39.8 %copy-start.24 = (f32[8,1024]{1,0:T(8,128)S(1)}, f32[8,1024]{1,0:T(8,128)}, u32[]{:S(2)}) copy-start(f32[8,1024]{1,0:T(8,128)} %get-tuple-element.258) | copy-start | bytes 98308
  584.9 40.4 %copy-start.13 = (f32[688,1024]{1,0:T(8,128)S(1)}, f32[688,1024]{1,0:T(8,128)}, u32[]{:S(2)}) copy-start(f32[688,1024]{1,0:T(8,128)} %get-tuple-element.265) | copy-start | bytes 8454148
  623.7 19.4 %collective-permute-start.24 = (bf16[2,688,1024]{2,1,0:T(8,128)(2,1)}, bf16[2,688,1024]{2,1,0:T(8,128)(2,1)}, u32[]{:S(2)}, u32[]{:S(2)}) collective-permute-start(bf16[2,688,1024]{2,1,0:T(8,128)(2,1)} %get-tuple-element.251), channel_id=1, source_target_pairs={{0,4},{4,0},{8,12},{12,8},{1,5},{5,1},{9,13},{13,9},{2,6},{6,2},{1... | collective-permute-start | bytes 8454152 | tf_op jit(solution)/shard_map/ppermute | solution.py:1173
  625.5 1.4 copy-start.25
  625.5 1.4 copy-start.26
  625.5 3.4 copy-start.10
  628.9 3.4 copy-start.19
  628.9 5.5 copy-start.8
  632.3 30.4 %collective-permute-start.26 = (bf16[256,1024]{1,0:T(8,128)(2,1)S(1)}, bf16[256,1024]{1,0:T(8,128)(2,1)}, u32[]{:S(2)}, u32[]{:S(2)}) collective-permute-start(bf16[256,1024]{1,0:T(8,128)(2,1)S(1)} %copy-done.19), channel_id=1, source_target_pairs={{0,8},{4,12},{8,0},{12,4},{1,9},{5,13},{9,1},{13,5},{2,10},{6,14},... | collective-permute-start | bytes 1572872 | tf_op jit(solution)/shard_map/ppermute | solution.py:1176
  633.0 47.4 %collective-permute-start.25 = (bf16[3,256,1024]{2,1,0:T(8,128)(2,1)}, bf16[3,256,1024]{2,1,0:T(8,128)(2,1)}, u32[]{:S(2)}, u32[]{:S(2)}) collective-permute-start(bf16[3,256,1024]{2,1,0:T(8,128)(2,1)} %fusion.5), channel_id=1, source_target_pairs={{0,8},{4,12},{8,0},{12,4},{1,9},{5,13},{9,1},{13,5},{2,10},{6,14},... | collective-permute-start | bytes 4718600 | tf_op jit(solution)/shard_map/ppermute | solution.py:1176
  667.3 17.2 %copy-start.14 = (f32[688,1024]{1,0:T(8,128)S(1)}, f32[688,1024]{1,0:T(8,128)}, u32[]{:S(2)}) copy-start(f32[688,1024]{1,0:T(8,128)} %get-tuple-element.264) | copy-start | bytes 8454148
  897.2 1.6 copy-start
  898.8 1.2 copy-start.1
  900.1 1.2 copy-start.2
  901.3 1.1 copy-start.3
  902.4 0.9 copy-start.4
  903.4 0.7 copy-start.5

commit v4 on v3

--- a/solution.py
+++ b/solution.py
@@ -424,12 +424,12 @@
             here = (s == section) & (to_c == c) & (z == zz)
             dst = ends_ref.at[piece]
             moves.send(
-                ref.at[zz], dst, "back", piece, active & jnp.logical_not(here), section=section, dp=y * 2 + to_c, mp=zz
+                ref.at[:, tile(zz, dst.shape[1])], dst, "back", piece, active & jnp.logical_not(here), section=section, dp=y * 2 + to_c, mp=zz
             )
 
             @pl.when(active & here)
             def _():
-                pltpu.make_async_copy(ref.at[zz], dst, moves.arrival("back", piece)).start()
+                pltpu.make_async_copy(ref.at[:, tile(zz, dst.shape[1])], dst, moves.arrival("back", piece)).start()
 
     for g, k in steps:
         zz = place.other_z(k)
@@ -521,7 +521,7 @@
 def scatter(table, first, last, grads, shapes):
     S, DP, MP = (lax.axis_size(name) for name in ("section", "dp", "mp"))
     Y = DP // 2
-    _, rows, block = first.shape
+    rows, block = first.shape[0], first.shape[1] // MP
     pieces = grads["pieces"]
     names = ("qkv", "out", "fc1", "fc2")
     flat = [grads["own"][n] for n in names] + [grads["there"][n] for n in names] + [grads["above"][n] for n in names]
@@ -778,7 +778,7 @@
     )
 
 
-def mlp_kernel(x_ref, o_ref, vec_ref, bias_ref, wo_ref, w1_ref, w2_ref, y_ref, branch_ref, middle_ref, n_ref, act_ref, slope_ref, two_ref, total):
+def mlp_kernel(x_ref, o_ref, vec_ref, bias_ref, wo_ref, w1_ref, w2_ref, y_ref, low_ref, branch_ref, middle_ref, n_ref, act_ref, slope_ref, two_ref, total):
     step = pl.program_id(0)
 
     @pl.when(step == 0)
@@ -802,7 +802,9 @@
     def _():
         two = total[...] + vec_ref[B_FC2][None]
         two_ref[...] = two.astype(LOW)
-        y_ref[...] = middle_ref[...] + vec_ref[SCALE_MLP][None] * two
+        low = (middle_ref[...] + vec_ref[SCALE_MLP][None] * two).astype(LOW)
+        low_ref[...] = low
+        y_ref[...] = low.astype(WIDE)
 
 
 CHUNK = 512
@@ -828,7 +830,7 @@
             weight,
             weight,
         ],
-        [wide, low, wide, low, units, units, low],
+        [wide, low, low, wide, low, units, units, low],
         [pltpu.VMEM((rows, width), WIDE)],
         4 * rows * width * hidden,
         (rows_in, out, vec, bias, w_out, fc1, fc2),
@@ -1007,7 +1009,7 @@
 
 
 def project_back_kernel(
-    c_ref, d0_ref, d1_ref, n_ref, x_ref, grad_ref, vec_ref, w_ref, dx_ref, own, there, sums_ref, n_t, total
+    c_ref, d0_ref, d1_ref, n_ref, x_ref, grad_ref, vec_ref, w_ref, dx_ref, low_ref, own, there, sums_ref, n_t, total
 ):
     step = pl.program_id(0)
     c, count = c_ref[0], own.shape[0]
@@ -1034,7 +1036,9 @@
         sums_ref[2:3] = d_gain
         sums_ref[3:4] = d_bias
         sums_ref[4:8] = jnp.zeros((4, sums_ref.shape[1]), WIDE)
-        dx_ref[...] = grad_ref[...] + d_rows
+        low = (grad_ref[...] + d_rows).astype(LOW)
+        low_ref[...] = low
+        dx_ref[...] = low.astype(WIDE)
 
 
 def project_back(half, d0, d1, saved, grad, vec, attn, count):
@@ -1060,6 +1064,7 @@
         ],
         [
             (whole, jax.ShapeDtypeStruct((rows, width), WIDE)),
+            (whole, jax.ShapeDtypeStruct((rows, width), LOW)),
             out,
             out,
             (full((8, width)), jax.ShapeDtypeStruct((8, width), WIDE)),
@@ -1083,7 +1088,7 @@
     kv1 = from_pair(kv0)
     out, out_wide, scales, probs = attend(q, kv0, kv1, mask)
     out = meanwhile(0, q, out)
-    leaving, branch, middle, n_two, active, slope, two = mlp(rows_in, out, vec, bias, weights)
+    leaving, leaving_low, branch, middle, n_two, active, slope, two = mlp(rows_in, out, vec, bias, weights)
     leaving = meanwhile(1, out, leaving)
     saved = dict(
         rows_in=rows_in,
@@ -1102,7 +1107,7 @@
         slope=slope,
         two=two,
     )
-    return (leaving, saved)
+    return (leaving, leaving_low, saved)
 
 
 def layer_backward(grad_rows, saved, vec, weights, half, from_pair, sums_over, meanwhile):
@@ -1116,27 +1121,16 @@
     d0 = meanwhile("fc1", d_out, d0)
     d1 = from_pair(d1)
     d0 = sums_over(own, there, d0)
-    grad_in, own["qkv"], there["qkv"], sums_one = project_back(
+    grad_in, grad_low, own["qkv"], there["qkv"], sums_one = project_back(
         half, d0, d1, saved, grad_middle, vec, weights[0], count
     )
     grad_in = meanwhile("out", d0, grad_in)
     grad_in = meanwhile("qkv", d0, grad_in)
-    vectors = dict(
-        ln1_gain=sums_one[2],
-        ln1_bias=sums_one[3],
-        b_query=sums_one[0],
-        b_value=sums_one[1],
-        b_out=sums[5],
-        scale_attn=sums[4],
-        ln2_gain=sums[2],
-        ln2_bias=sums[3],
-        b_fc1=units[0],
-        b_fc2=sums[1],
-        scale_mlp=sums[0],
-    )
-    return (grad_in, own, there, vectors)
-
-
+    vectors = jnp.concatenate([sums[:6], sums_one[:4]], 0), units[0]
+    return (grad_in, grad_low, own, there, vectors)
+
+
+SUMS = ("scale_mlp", "b_fc2", "ln2_gain", "ln2_bias", "scale_attn", "b_out", "b_query", "b_value", "ln1_gain", "ln1_bias")
 NARROW = ("ln1_gain", "ln1_bias", "b_query", "b_value", "b_out", "scale_attn", "ln2_gain", "ln2_bias", "b_fc2", "scale_mlp")
 
 
@@ -1203,10 +1197,7 @@
         stack = jnp.stack(got)
         return jnp.concatenate([pick(stack, lax.rem(here + turns - zz % turns, turns)) for zz in range(MP)], 1)
 
-    def by_column(value):
-        return jnp.stack([value[:, i * columns : (i + 1) * columns].astype(LOW) for i in range(MP)])
-
-    waiting, above, projections = {}, {}, []
+    waiting, above, projections = {}, {}, {}
 
     def join(name, own, got):
         axis = own.ndim - 3
@@ -1221,21 +1212,24 @@
 
     def sums_over(own, there, before):
         parts = []
-        for name in own:
+        for name in ("fc2", "fc1"):
             parts += join(name, own[name], from_pair(there[name]))
+        projections["out"] = (own["out"], there["out"])
         return after(before, *parts)
 
     def rows_meanwhile(name, before, done):
         if name == "fc2":
-            own, there = projections
-            got, done = lax.optimization_barrier((from_pair(after(there, before)), done))
-            projections[:] = [own, got]
+            got = {key: from_pair(after(there, before)) for key, (_, there) in projections.items()}
+            got, done = lax.optimization_barrier((got, done))
+            for key in got:
+                projections[key] = (projections[key][0], got[key])
         row, others = waiting[name]
         got = [from_row(after(part, before), DP // 2 - r) for r, part in enumerate(others, 1)]
         got, done = lax.optimization_barrier((got, done))
         above[name] = (row, got)
         if name == "fc1":
-            done = after(done, *join("qkv", *projections))
+            for key in projections:
+                done = after(done, *join(key, *projections[key]))
         return done
 
     def sums_done(name):
@@ -1306,41 +1300,43 @@
             cotangent.extend(got)
             return done
 
-        rows_now, kept = layer_forward(
+        rows_now, end_rows, kept = layer_forward(
             rows_now, vectors[layer], biases[layer], weights[layer], mask, from_pair, meanwhile
         )
         saved.append(kept)
-        if layer + 1 < S:
-            rows_now = rows_now.astype(LOW).astype(WIDE)
-    end_rows = rows_now
 
     grad_now = jnp.where(active, brought(cotangent).astype(WIDE), 0.0)
     vector_grads = [None] * S
 
     for layer in reversed(range(S)):
-        grad_now, own, there, vector_grads[layer] = layer_backward(
+        grad_now, grad_low, own, there, vector_grads[layer] = layer_backward(
             grad_now, saved[layer], vectors[layer], weights[layer], half, from_pair,
             sums_over if layer else (lambda own, there, before: before),
             (lambda name, before, done: done) if layer else rows_meanwhile,
         )
         if layer:
-            projections[:] = [own["qkv"], there["qkv"]]
-            grad_now = grad_now.astype(LOW).astype(WIDE)
+            projections["qkv"] = (own["qkv"], there["qkv"])
 
     above = {name: sums_done(name) for name in ("fc2", "fc1", "out", "qkv")}
     grads = dict(own=own, there=there, above=above, pieces=pieces)
     shapes = [qkv_shard.shape, w_query.shape[1:], w_fc1.shape[1:], (w_fc2.shape[2], w_fc2.shape[1])]
-    names = NARROW + ("b_fc1",)
+    names = SUMS + ("b_fc1",)
     table = jnp.stack(
         [
-            jnp.concatenate([vector_grads[layer][name].reshape(MP, DP, -1) for name in names], 2)
-            for layer in range(S)
+            jnp.concatenate(
+                [
+                    table.reshape(len(SUMS), MP, DP, -1).transpose(1, 2, 0, 3).reshape(MP, DP, -1),
+                    units.reshape(MP, DP, -1),
+                ],
+                2,
+            )
+            for table, units in vector_grads
         ]
     )
     lines = -(-table.shape[3] // 1024) * 8
     table = jnp.pad(table, ((0, 0), (0, 0), (0, 0), (0, lines * 128 - table.shape[3])))
     table = table.reshape(S, MP, DP // 2, 2, lines, 128).transpose(3, 0, 2, 1, 4, 5)
-    ends, summed, *sums = scatter(table, by_column(grad_now), by_column(end_rows), grads, shapes)
+    ends, summed, *sums = scatter(table, grad_low, end_rows, grads, shapes)
     sizes = [columns // DP] * len(NARROW) + [b_fc1.shape[1] // DP]
     ends, g_query, g_key, g_value, g_out, g_fc1, g_fc2, *vector_sums = finish(ends, summed, sums, seq_len, sizes)
     v = dict(zip(names, vector_sums))
@@ -1367,48 +1363,38 @@
 
 
 def solution(mesh):
+    images = P("section", None, "dp", None, "mp")
+    vector = P("section", "mp")
+    small = P("section", ("mp", "dp"))
+    rows = P("section", "dp", "mp")
+    columns = P("section", "mp", "dp")
+
+    def specs(ends, line):
+        return (
+            ends,
+            line,
+            line,
+            rows,
+            rows,
+            rows,
+            line,
+            line,
+            columns,
+            line,
+            line,
+            line,
+            line,
+            rows,
+            line,
+            columns,
+            line,
+            line,
+        )
+
     return jax.shard_map(
         local,
         mesh=mesh,
-        in_specs=(
-            P("section", None, "dp", None, "mp"),
-            P("section", "mp"),
-            P("section", "mp"),
-            P("section", "dp", "mp"),
-            P("section", "dp", "mp"),
-            P("section", "dp", "mp"),
-            P("section", "mp"),
-            P("section", "mp"),
-            P("section", "mp", "dp"),
-            P("section", "mp"),
-            P("section", "mp"),
-            P("section", "mp"),
-            P("section", "mp"),
-            P("section", "dp", "mp"),
-            P("section", "mp"),
-            P("section", "mp", "dp"),
-            P("section", "mp"),
-            P("section", "mp"),
-        ),
-        out_specs=(
-            P("section", None, "dp", None, "mp"),
-            P("section", ("mp", "dp")),
-            P("section", ("mp", "dp")),
-            P("section", "dp", "mp"),
-            P("section", "dp", "mp"),
-            P("section", "dp", "mp"),
-            P("section", ("mp", "dp")),
-            P("section", ("mp", "dp")),
-            P("section", "mp", "dp"),
-            P("section", ("mp", "dp")),
-            P("section", ("mp", "dp")),
-            P("section", ("mp", "dp")),
-            P("section", ("mp", "dp")),
-            P("section", "dp", "mp"),
-            P("section", ("mp", "dp")),
-            P("section", "mp", "dp"),
-            P("section", ("mp", "dp")),
-            P("section", ("mp", "dp")),
-        ),
+        in_specs=specs(images, vector),
+        out_specs=specs(images, small),
         check_vma=False,
     )

time: 922 us -> 908 us (0.985)
  other arithmetic: 48.7 us -> 38.6 us
    unnamed x61 -> x55, local copies, waits for them, and re-layouts: 18.8 us -> 18.7 us
  transfers between devices with their start and end apart: 27 -> 27, of which waited for: 4 -> 4; matrix products, arithmetic and copies ran while one was open for 6% -> 5% of each run, Pallas kernels for 25% -> 26%
where the time goes in v4:
time: 908 us; the launch traced here: 895 us
  Pallas kernels  760 us (84%)
  local copies, waits for them, and re-layouts  48.4 us (5%)
  other arithmetic  38.6 us (4%)
  starting transfers between devices  27.4 us (3%)
  waiting for transfers between devices  18.9 us (2%)
    pallas_call x12, Pallas kernels, compute_call(): pl.pallas_call(kernel, grid=(steps,), in_specs=ins, out_specs=[spec for s...  345 us
    pallas_call x1, Pallas kernels, scatter(): pl.pallas_call(functools.partial(scatter_kernel, pieces), in_specs=[vmem]...  211 us
    pallas_call x1, Pallas kernels, gather(): pl.pallas_call(functools.partial(gather_kernel, pieces), in_specs=[vmem]...  200 us
    unnamed x55, local copies, waits for them, and re-layouts  18.7 us
  transfers between devices with their start and end apart: 27, of which 4 were waited for; matrix products, arithmetic and copies ran while one was open for 5% of the time, Pallas kernels for 26%

profile of v4, /device:TPU:26, one launch (start us, length us, event | category | flops | bytes accessed | tf_op | source)
XLA Modules:
  0.0 894.8 jit_solution(15280747465594614673)
XLA Ops:
  0.7 1.7 copy.42
  2.3 2.0 copy.43
  4.4 1.8 pad_maximum_fusion.refs_0_
  6.2 2.7 concatenate.28.vec_ref
  8.9 1.3 broadcast_in_dim.45.bias_ref
  10.2 200.2 %shard_map.313 = (bf16[688,1024]{1,0:T(8,128)(2,1)}, bf16[6,688,256]{2,1,0:T(8,128)(2,1)}, f32[2,16,1024]{2,1,0:T(8,128)}, f32[2,8,4096]{2,1,0:T(8,128)}, bf16[3...) custom-call(f32[3,1370,1,256]{3,2,1,0:T(1,128)} %bitcast.99, ...), custom_call_target="tpu_custom_call" | custom-call | tf_op jit(solution)/shard_map/pallas_call | solution.py:314
  210.4 1.5 slice_bitcast_fusion.2
  211.9 3.3 convert_select_fusion.1.x_ref
  215.2 10.5 %shard_map.314 = (bf16[688,1024]{1,0:T(8,128)(2,1)}, bf16[2,688,1024]{2,1,0:T(8,128)(2,1)}, bf16[688,1024]{1,0:T(8,128)(2,1)}) custom-call(f32[688,1024]{1,0:T(8,128)} %convert_select_fusion.1.x_ref, f32[16,1024]{1,0:T(8,128)} %get-tuple-element.351.vec_ref, bf16[3,1024,1024]{2,1,0:T(8,128)(2,1)} %get-tuple-element.162.w_ref), custom_call_target="tpu_custom_call" | custom-call | flops 1000 | bytes 1000 | tf_op jit(solution)/shard_map/pallas_call | solution.py:651
  227.0 2.9 dynamic-slice_bitcast_fusion.4
  229.8 1.3 collective-permute-start
  231.2 6.1 collective-permute-start.1
  238.3 1.6 copy-done.6
  239.9 31.2 %shard_map.315 = (bf16[688,1024]{1,0:T(8,128)(2,1)}, f32[688,1024]{1,0:T(8,128)}, f32[688,1024]{1,0:T(8,128)}, bf16[16,2,688,688]{3,2,1,0:T(8,128)(2,1)}) custom-call(bf16[688,1024]{1,0:T(8,128)(2,1)} %get-tuple-element.163.q_ref, bf16[2,688,1024]{2,1,0:T(8,128)(2,1)} %get-tuple-element.168.k0.v0, bf16[2,688,1024]{2,1,0:T(8,128)(2,1)} %copy-done.6, ...), custom_call_target="tpu_custom_call" | custom-call | flops 1000 | bytes 1000 | tf_op jit(solution)/shard_map/pallas_call | solution.py:651
  271.2 2.7 collective-permute-start.4
  274.0 2.0 collective-permute-start.5
  276.0 1.7 collective-permute-start.6
  278.4 28.4 %shard_map.316 = (f32[688,1024]{1,0:T(8,128)}, bf16[688,1024]{1,0:T(8,128)(2,1)}, bf16[688,1024]{1,0:T(8,128)(2,1)}, f32[688,1024]{1,0:T(8,128)}, bf16[688,1024]...) custom-call(f32[688,1024]{1,0:T(8,128)} %convert_select_fusion.1.x_ref, ...), custom_call_target="tpu_custom_call" | custom-call | flops 1000 | bytes 1000 | tf_op jit(solution)/shard_map/pallas_call | solution.py:651
  306.9 2.7 constant_dynamic-update-slice_fusion.5
  309.6 1.4 constant_dynamic-update-slice_fusion.4.w_ref
  311.0 10.2 %shard_map.317 = (bf16[688,1024]{1,0:T(8,128)(2,1)}, bf16[2,688,1024]{2,1,0:T(8,128)(2,1)}, bf16[688,1024]{1,0:T(8,128)(2,1)}) custom-call(f32[688,1024]{1,0:T(8,128)} %get-tuple-element.180.x_ref, f32[16,1024]{1,0:T(8,128)} %get-tuple-element.350.vec_ref, bf16[3,1024,1024]{2,1,0:T(8,128)(2,1)} %constant_dynamic-update-slice_fusion.4.w_ref), custom_call_target="tpu_custom_call" | custom-call | flops 1000 | bytes 1000 | tf_op jit(solution)/shard_map/pallas_call | solution.py:651
  321.6 1.8 collective-permute-start.13
  323.4 2.4 collective-permute-start.9
  326.6 2.7 collective-permute-start.10
  329.3 1.0 bitcast_dynamic-update-slice_fusion.5
  330.3 31.3 %shard_map.318 = (bf16[688,1024]{1,0:T(8,128)(2,1)}, f32[688,1024]{1,0:T(8,128)}, f32[688,1024]{1,0:T(8,128)}, bf16[16,2,688,688]{3,2,1,0:T(8,128)(2,1)}) custom-call(bf16[688,1024]{1,0:T(8,128)(2,1)} %get-tuple-element.183.q_ref, bf16[2,688,1024]{2,1,0:T(8,128)(2,1)} %get-tuple-element.184.k0.v0, bf16[2,688,1024]{2,1,0:T(8,128)(2,1)} %copy-done.7, ...), custom_call_target="tpu_custom_call" | custom-call | flops 1000 | bytes 1000 | tf_op jit(solution)/shard_map/pallas_call | solution.py:651
  361.7 3.7 constant_dynamic-update-slice_fusion.1
  365.6 1.0 bitcast_dynamic-update-slice_fusion.3
  366.6 1.0 bitcast_dynamic-update-slice_fusion.2
  368.2 1.0 bitcast_dynamic-update-slice_fusion.1
  369.2 1.0 bitcast_dynamic-update-slice_fusion
  371.2 1.9 convert_select_fusion.dy_ref
  373.1 2.3 constant_dynamic-update-slice_fusion.7
  376.2 1.1 constant_dynamic-update-slice_fusion.6.w1_ref
  377.3 1.4 constant_dynamic-update-slice_fusion.w2_ref
  378.7 28.0 %shard_map.319 = (f32[688,1024]{1,0:T(8,128)}, bf16[688,1024]{1,0:T(8,128)(2,1)}, bf16[688,1024]{1,0:T(8,128)(2,1)}, f32[688,1024]{1,0:T(8,128)}, bf16[688,1024]...) custom-call(f32[688,1024]{1,0:T(8,128)} %get-tuple-element.180.x_ref, ...), custom_call_target="tpu_custom_call" | custom-call | flops 1000 | bytes 1000 | tf_op jit(solution)/shard_map/pallas_call | solution.py:651
  406.8 43.5 %shard_map.320 = (f32[688,1024]{1,0:T(8,128)}, bf16[688,1024]{1,0:T(8,128)(2,1)}, bf16[2,256,4096]{2,1,0:T(8,128)(2,1)}, bf16[2,256,4096]{2,1,0:T(8,128)(2,1)}, ...) custom-call(s32[1]{0:T(128)} %bitcast.c_ref, ...), custom_call_target="tpu_custom_call" | custom-call | flops 1000 | bytes 1000 | tf_op jit(solution)/shard_map/pallas_call | solution.py:651
  450.8 38.8 %shard_map.321 = (bf16[3,688,1024]{2,1,0:T(8,128)(2,1)}, bf16[2,688,1024]{2,1,0:T(8,128)(2,1)}) custom-call(bf16[688,1024]{1,0:T(8,128)(2,1)} %get-tuple-element.183.q_ref, bf16[2,688,1024]{2,1,0:T(8,128)(2,1)} %get-tuple-element.184.k0.v0, bf16[2,688,1024]{2,1,0:T(8,128)(2,1)} %copy-done.7, bf16[2,688,1024]{2,1,0:T(8,128)(2,1)} %get-tuple-element.184.k0.v0, ...), custom_call_target="tpu_custom_call" | custom-call | flops 1000 | bytes 1000 | tf_op jit(solution)/shard_map/pallas_call | solution.py:651
  490.0 4.5 fusion.3
  494.5 3.7 fusion.4
  498.2 1.6 copy-done.12
  499.8 20.1 %shard_map.322 = (f32[688,1024]{1,0:T(8,128)}, bf16[688,1024]{1,0:T(8,128)(2,1)}, bf16[3,2,256,1024]{3,2,1,0:T(8,128)(2,1)}, bf16[3,2,256,1024]{3,2,1,0:T(8,128)(2,1)}, f32[8,1024]{1,0:T(8,128)}) custom-call(s32[1]{0:T(128)} %bitcast.c_ref, bf16[3,688,1024]{2,1,0:T(8,128)(2,1)} %get-tuple-element.222.d0_ref, bf16[2,688,1024]{2,1,0:T(8,128)(2,1)} %copy-done.12, ...), custom_call_target="tpu_custom_call" | custom-call | flops 1000 | bytes 1000 | tf_op jit(solution)/shard_map/pallas_call | solution.py:651
  519.8 4.2 copy.44
  524.8 43.4 %shard_map.323 = (f32[688,1024]{1,0:T(8,128)}, bf16[688,1024]{1,0:T(8,128)(2,1)}, bf16[2,256,4096]{2,1,0:T(8,128)(2,1)}, bf16[2,256,4096]{2,1,0:T(8,128)(2,1)}, ...) custom-call(s32[1]{0:T(128)} %bitcast.c_ref, ...), custom_call_target="tpu_custom_call" | custom-call | flops 1000 | bytes 1000 | tf_op jit(solution)/shard_map/pallas_call | solution.py:651
  568.2 4.1 collective-permute-done.20
  572.6 1.0 copy-done.13
  573.6 38.8 %shard_map.324 = (bf16[3,688,1024]{2,1,0:T(8,128)(2,1)}, bf16[2,688,1024]{2,1,0:T(8,128)(2,1)}) custom-call(bf16[688,1024]{1,0:T(8,128)(2,1)} %get-tuple-element.163.q_ref, bf16[2,688,1024]{2,1,0:T(8,128)(2,1)} %get-tuple-element.168.k0.v0, bf16[2,688,1024]{2,1,0:T(8,128)(2,1)} %copy-done.6, bf16[2,688,1024]{2,1,0:T(8,128)(2,1)} %get-tuple-element.168.k0.v0, ...), custom_call_target="tpu_custom_call" | custom-call | flops 1000 | bytes 1000 | tf_op jit(solution)/shard_map/pallas_call | solution.py:651
  612.5 0.9 slice_reduce_fusion
  614.8 1.5 fusion.7
  616.3 3.8 fusion.5
  620.9 1.3 collective-permute-start.25
  622.2 7.9 fusion
  630.1 4.8 collective-permute-done.26
  634.9 2.1 fusion.6.refs_9_
  637.0 20.3 %shard_map.325 = (f32[688,1024]{1,0:T(8,128)}, bf16[688,1024]{1,0:T(8,128)(2,1)}, bf16[3,2,256,1024]{3,2,1,0:T(8,128)(2,1)}, bf16[3,2,256,1024]{3,2,1,0:T(8,128)(2,1)}, f32[8,1024]{1,0:T(8,128)}) custom-call(s32[1]{0:T(128)} %bitcast.c_ref, bf16[3,688,1024]{2,1,0:T(8,128)(2,1)} %get-tuple-element.253.d0_ref, ...), custom_call_target="tpu_custom_call" | custom-call | flops 1000 | bytes 1000 | tf_op jit(solution)/shard_map/pallas_call | solution.py:651
  659.1 9.2 %collective-permute-done.25 = bf16[3,256,1024]{2,1,0:T(8,128)(2,1)} collective-permute-done((bf16[3,256,1024]{2,1,0:T(8,128)(2,1)}, bf16[3,256,1024]{2,1,0:T(8,128)(2,1)}, u32[]{:S(2)}, u32[]{:S(2)}) %collective-permute-start.25) | collective-permute-done | bytes 1572896 | tf_op jit(solution)/shard_map/ppermute | solution.py:1170
  668.3 4.1 fusion.2.refs_8_
  672.4 211.1 %shard_map.326 = (bf16[6,688,256]{2,1,0:T(8,128)(2,1)}, f32[8,128]{1,0:T(8,128)}, f32[3,256,256]{2,1,0:T(8,128)}, f32[256,256]{1,0:T(8,128)}, f32[256,1024]{1,0:T(8,128)}, /*index=5*/f32[256,1024]{1,0:T(8,128)}) custom-call(f32[2,2,2,4,8,128]{5,4,3,2,1,0:T(8,128)} %bitcast.101, bf16[688,1024]{1,0:T(8,128)(2,1)} %get-tuple-element.262.first_ref, ...), custom_call_target="tpu_custom_call" | custom-call | tf_op jit(solution)/shard_map/pallas_call | solution.py:535
  883.5 1.6 copy-done
  885.1 1.2 copy-done.1
  886.3 1.2 copy-done.2
  887.5 1.1 copy-done.3
  888.6 0.9 copy-done.4
  890.3 4.0 shard_map.327
  (109 shorter events, 13.6 us)
Async XLA Ops:
  225.7 12.6 %collective-permute-start.3 = (bf16[2,688,1024]{2,1,0:T(8,128)(2,1)}, bf16[2,688,1024]{2,1,0:T(8,128)(2,1)S(1)}, u32[]{:S(2)}, u32[]{:S(2)}) collective-permute-start(bf16[2,688,1024]{2,1,0:T(8,128)(2,1)} %get-tuple-element.168.k0.v0), channel_id=1, source_target_pairs={{0,4},{4,0},{8,12},{12,8},{1,5},{5,1},{9,13},{13,9},{2,6},{6,2},{1... | collective-permute-start | bytes 8454152 | tf_op jit(solution)/shard_map/ppermute | solution.py:1167
  226.4 44.7 %collective-permute-start.2 = (bf16[3,256,1024]{2,1,0:T(8,128)(2,1)}, bf16[3,256,1024]{2,1,0:T(8,128)(2,1)}, u32[]{:S(2)}, u32[]{:S(2)}) collective-permute-start(bf16[3,256,1024]{2,1,0:T(8,128)(2,1)} %get-tuple-element.167), channel_id=1, source_target_pairs={{0,8},{4,12},{8,0},{12,4},{1,9},{5,13},{9,1},{13,5},{2,10},{6,14},... | collective-permute-start | bytes 4718600 | tf_op jit(solution)/shard_map/ppermute | solution.py:1170
  229.8 41.3 %collective-permute-start = (bf16[688,256]{1,0:T(8,128)(2,1)}, bf16[688,256]{1,0:T(8,128)(2,1)S(1)}, u32[]{:S(2)}, u32[]{:S(2)}) collective-permute-start(bf16[688,256]{1,0:T(8,128)(2,1)} %get-tuple-element.164), channel_id=1, source_target_pairs={{16,0},{17,4},{18,2},{19,6},{20,1},{21,5},{22,3},{23,7},{24,8},{25... | collective-permute-start | bytes 1056776 | tf_op jit(solution)/shard_map/ppermute | solution.py:1178
  231.2 40.0 %collective-permute-start.1 = (bf16[688,256]{1,0:T(8,128)(2,1)}, bf16[688,256]{1,0:T(8,128)(2,1)S(1)}, u32[]{:S(2)}, u32[]{:S(2)}) collective-permute-start(bf16[688,256]{1,0:T(8,128)(2,1)} %get-tuple-element.165), channel_id=1, source_target_pairs={{16,4},{17,2},{18,6},{19,16},{20,5},{21,3},{22,7},{23,17},{24,12},... | collective-permute-start | bytes 1056776 | tf_op jit(solution)/shard_map/ppermute | solution.py:1178
  238.3 39.4 %copy-start.20 = (f32[2,8,4096]{2,1,0:T(8,128)S(1)}, f32[2,8,4096]{2,1,0:T(8,128)}, u32[]{:S(2)}) copy-start(f32[2,8,4096]{2,1,0:T(8,128)} %get-tuple-element.175) | copy-start | bytes 786436
  238.3 1.6 copy-start.6
  271.1 35.7 %copy-start.19 = (bf16[688,256]{1,0:T(8,128)(2,1)}, bf16[688,256]{1,0:T(8,128)(2,1)S(1)}, u32[]{:S(2)}) copy-start(bf16[688,256]{1,0:T(8,128)(2,1)S(1)} %collective-permute-done) | copy-start | bytes 1056772
  271.1 35.7 %copy-start.17 = (bf16[688,256]{1,0:T(8,128)(2,1)}, bf16[688,256]{1,0:T(8,128)(2,1)S(1)}, u32[]{:S(2)}) copy-start(bf16[688,256]{1,0:T(8,128)(2,1)S(1)} %collective-permute-done.1) | copy-start | bytes 1056772
  271.2 38.4 %collective-permute-start.7 = (bf16[3,256,1024]{2,1,0:T(8,128)(2,1)}, bf16[3,256,1024]{2,1,0:T(8,128)(2,1)S(1)}, u32[]{:S(2)}, u32[]{:S(2)}) collective-permute-start(bf16[3,256,1024]{2,1,0:T(8,128)(2,1)} %collective-permute-done.2), channel_id=1, source_target_pairs={{0,4},{4,0},{8,12},{12,8},{1,5},{5,1},{9,13},{13,9},{2,6},{6,2},{1... | collective-permute-start | bytes 4718600 | tf_op jit(solution)/shard_map/ppermute | solution.py:1167
  271.2 38.3 %collective-permute-start.4 = (bf16[688,256]{1,0:T(8,128)(2,1)}, bf16[688,256]{1,0:T(8,128)(2,1)}, u32[]{:S(2)}, u32[]{:S(2)}) collective-permute-start(bf16[688,256]{1,0:T(8,128)(2,1)} %get-tuple-element.171), channel_id=1, source_target_pairs={{16,2},{17,6},{18,16},{19,20},{20,3},{21,7},{22,17},{23,21},{24,10... | collective-permute-start | bytes 1056776 | tf_op jit(solution)/shard_map/ppermute | solution.py:1178
  274.0 35.6 %collective-permute-start.5 = (bf16[688,256]{1,0:T(8,128)(2,1)}, bf16[688,256]{1,0:T(8,128)(2,1)}, u32[]{:S(2)}, u32[]{:S(2)}) collective-permute-start(bf16[688,256]{1,0:T(8,128)(2,1)} %get-tuple-element.172), channel_id=1, source_target_pairs={{16,6},{17,16},{18,20},{19,0},{20,7},{21,17},{22,21},{23,1},{24,14... | collective-permute-start | bytes 1056776 | tf_op jit(solution)/shard_map/ppermute | solution.py:1178
  276.0 33.6 %collective-permute-start.6 = (bf16[256,2048]{1,0:T(8,128)(2,1)}, bf16[256,2048]{1,0:T(8,128)(2,1)S(1)}, u32[]{:S(2)}, u32[]{:S(2)}) collective-permute-start(bf16[256,2048]{1,0:T(8,128)(2,1)} %get-tuple-element.174), channel_id=1, source_target_pairs={{0,8},{4,12},{8,0},{12,4},{1,9},{5,13},{9,1},{13,5},{2,10},{6,14},... | collective-permute-start | bytes 3145736 | tf_op jit(solution)/shard_map/ppermute | solution.py:1170
  309.6 11.6 %copy-start.16 = (bf16[256,2048]{1,0:T(8,128)(2,1)}, bf16[256,2048]{1,0:T(8,128)(2,1)S(1)}, u32[]{:S(2)}) copy-start(bf16[256,2048]{1,0:T(8,128)(2,1)S(1)} %collective-permute-done.6) | copy-start | bytes 3145732
  321.2 5.4 collective-permute-start.8
  321.2 40.5 %collective-permute-start.11 = (bf16[256,2048]{1,0:T(8,128)(2,1)}, bf16[256,2048]{1,0:T(8,128)(2,1)}, u32[]{:S(2)}, u32[]{:S(2)}) collective-permute-start(bf16[256,2048]{1,0:T(8,128)(2,1)} %copy-done.16), channel_id=1, source_target_pairs={{0,16},{16,0},{1,17},{17,1},{2,18},{18,2},{3,19},{19,3},{4,20},{20... | collective-permute-start | bytes 3145736 | tf_op jit(solution)/shard_map/ppermute | solution.py:1246
  321.3 40.4 %collective-permute-start.12 = (bf16[256,2048]{1,0:T(8,128)(2,1)}, bf16[256,2048]{1,0:T(8,128)(2,1)}, u32[]{:S(2)}, u32[]{:S(2)}) collective-permute-start(bf16[256,2048]{1,0:T(8,128)(2,1)} %get-tuple-element.195), channel_id=1, source_target_pairs={{0,8},{4,12},{8,0},{12,4},{1,9},{5,13},{9,1},{13,5},{2,10},{6,14},... | collective-permute-start | bytes 3145736 | tf_op jit(solution)/shard_map/ppermute | solution.py:1170
  321.6 40.0 %collective-permute-start.13 = (bf16[256,1024]{1,0:T(8,128)(2,1)}, bf16[256,1024]{1,0:T(8,128)(2,1)S(1)}, u32[]{:S(2)}, u32[]{:S(2)}) collective-permute-start(bf16[256,1024]{1,0:T(8,128)(2,1)} %get-tuple-element.197), channel_id=1, source_target_pairs={{0,8},{4,12},{8,0},{12,4},{1,9},{5,13},{9,1},{13,5},{2,10},{6,14},... | collective-permute-start | bytes 1572872 | tf_op jit(solution)/shard_map/ppermute | solution.py:1170
  323.4 38.2 %collective-permute-start.9 = (bf16[688,256]{1,0:T(8,128)(2,1)}, bf16[688,256]{1,0:T(8,128)(2,1)}, u32[]{:S(2)}, u32[]{:S(2)}) collective-permute-start(bf16[688,256]{1,0:T(8,128)(2,1)} %get-tuple-element.190), channel_id=1, source_target_pairs={{16,16},{17,20},{18,0},{19,4},{20,17},{21,21},{22,1},{23,5},{24,24... | collective-permute-start | bytes 1056776 | tf_op jit(solution)/shard_map/ppermute | solution.py:1178
  326.6 3.7 copy-start.7
  326.6 35.0 %collective-permute-start.10 = (bf16[688,256]{1,0:T(8,128)(2,1)}, bf16[688,256]{1,0:T(8,128)(2,1)}, u32[]{:S(2)}, u32[]{:S(2)}) collective-permute-start(bf16[688,256]{1,0:T(8,128)(2,1)} %get-tuple-element.191), channel_id=1, source_target_pairs={{16,20},{17,0},{18,4},{19,2},{20,21},{21,1},{22,5},{23,3},{24,28},... | collective-permute-start | bytes 1056776 | tf_op jit(solution)/shard_map/ppermute | solution.py:1178
  361.7 3.9 copy-start.18
  365.4 12.0 %collective-permute-start.16 = (bf16[256,4096]{1,0:T(8,128)(2,1)S(1)}, bf16[256,4096]{1,0:T(8,128)(2,1)S(1)}, u32[]{:S(2)}, u32[]{:S(2)}) collective-permute-start(bf16[256,4096]{1,0:T(8,128)(2,1)S(1)} %get-tuple-element.337), channel_id=1, source_target_pairs={{0,4},{4,0},{8,12},{12,8},{1,5},{5,1},{9,13},{13,9},{2,6},{6,2},{1... | collective-permute-start | bytes 6291464 | tf_op jit(solution)/shard_map/ppermute | solution.py:1167
  367.6 7.8 collective-permute-start.14
  368.0 8.3 collective-permute-start.15
  450.3 39.8 %collective-permute-start.17 = (bf16[2,256,4096]{2,1,0:T(8,128)(2,1)}, bf16[2,256,4096]{2,1,0:T(8,128)(2,1)}, u32[]{:S(2)}, u32[]{:S(2)}) collective-permute-start(bf16[2,256,4096]{2,1,0:T(8,128)(2,1)} %get-tuple-element.219), channel_id=1, source_target_pairs={{0,4},{4,0},{8,12},{12,8},{1,5},{5,1},{9,13},{13,9},{2,6},{6,2},{1... | collective-permute-start | bytes 12582920 | tf_op jit(solution)/shard_map/ppermute | solution.py:1167
  450.6 43.9 %collective-permute-start.18 = (bf16[2,256,4096]{2,1,0:T(8,128)(2,1)}, bf16[2,256,4096]{2,1,0:T(8,128)(2,1)}, u32[]{:S(2)}, u32[]{:S(2)}) collective-permute-start(bf16[2,256,4096]{2,1,0:T(8,128)(2,1)} %get-tuple-element.221), channel_id=1, source_target_pairs={{0,4},{4,0},{8,12},{12,8},{1,5},{5,1},{9,13},{13,9},{2,6},{6,2},{1... | collective-permute-start | bytes 12582920 | tf_op jit(solution)/shard_map/ppermute | solution.py:1167
  489.7 8.5 collective-permute-start.19
  490.0 4.5 copy-start.8
  498.2 1.6 copy-start.12
  524.0 44.2 %collective-permute-start.22 = (bf16[3,2,256,1024]{3,2,0,1:T(8,128)(2,1)}, bf16[3,2,256,1024]{3,2,0,1:T(8,128)(2,1)S(1)}, u32[]{:S(2)}, u32[]{:S(2)}) collective-permute-start(bf16[3,2,256,1024]{3,2,0,1:T(8,128)(2,1)} %copy.44), channel_id=1, source_target_pairs={{0,4},{4,0},{8,12},{12,8},{1,5},{5,1},{9,13},{13,9},{2,6},{6,2},{1... | collective-permute-start | bytes 9437192 | tf_op jit(solution)/shard_map/ppermute | solution.py:1167
  524.2 48.0 %collective-permute-start.20 = (bf16[256,4096]{1,0:T(8,128)(2,1)}, bf16[256,4096]{1,0:T(8,128)(2,1)S(1)}, u32[]{:S(2)}, u32[]{:S(2)}) collective-permute-start(bf16[256,4096]{1,0:T(8,128)(2,1)} %fusion.3), channel_id=1, source_target_pairs={{0,8},{4,12},{8,0},{12,4},{1,9},{5,13},{9,1},{13,5},{2,10},{6,14},... | collective-permute-start | bytes 6291464 | tf_op jit(solution)/shard_map/ppermute | solution.py:1170
  524.8 43.4 %collective-permute-start.21 = (bf16[2,256,1024]{2,1,0:T(8,128)(2,1)}, bf16[2,256,1024]{2,1,0:T(8,128)(2,1)}, u32[]{:S(2)}, u32[]{:S(2)}) collective-permute-start(bf16[2,256,1024]{2,1,0:T(8,128)(2,1)} %get-tuple-element.236), channel_id=1, source_target_pairs={{0,4},{4,0},{8,12},{12,8},{1,5},{5,1},{9,13},{13,9},{2,6},{6,2},{1... | collective-permute-start | bytes 3145736 | tf_op jit(solution)/shard_map/ppermute | solution.py:1167
  568.2 4.4 copy-start.11
  572.3 1.3 copy-start.13
  572.3 47.9 %collective-permute-start.23 = (bf16[256,4096]{1,0:T(8,128)(2,1)}, bf16[256,4096]{1,0:T(8,128)(2,1)}, u32[]{:S(2)}, u32[]{:S(2)}) collective-permute-start(bf16[256,4096]{1,0:T(8,128)(2,1)} %fusion.4), channel_id=1, source_target_pairs={{0,8},{4,12},{8,0},{12,4},{1,9},{5,13},{9,1},{13,5},{2,10},{6,14},... | collective-permute-start | bytes 6291464 | tf_op jit(solution)/shard_map/ppermute | solution.py:1170
  573.6 39.9 %copy-start.23 = (f32[8,1024]{1,0:T(8,128)S(1)}, f32[8,1024]{1,0:T(8,128)}, u32[]{:S(2)}) copy-start(f32[8,1024]{1,0:T(8,128)} %get-tuple-element.260) | copy-start | bytes 98308
  573.6 39.9 %copy-start.21 = (f32[8,1024]{1,0:T(8,128)S(1)}, f32[8,1024]{1,0:T(8,128)}, u32[]{:S(2)}) copy-start(f32[8,1024]{1,0:T(8,128)} %get-tuple-element.259) | copy-start | bytes 98308
  573.6 42.7 %copy-start.10 = (bf16[3,2,256,1024]{3,2,1,0:T(8,128)(2,1)S(1)}, bf16[3,2,256,1024]{3,2,1,0:T(8,128)(2,1)}, u32[]{:S(2)}) copy-start(bf16[3,2,256,1024]{3,2,1,0:T(8,128)(2,1)} %get-tuple-element.251) | copy-start | bytes 9437188
  612.4 24.6 %collective-permute-start.24 = (bf16[2,688,1024]{2,1,0:T(8,128)(2,1)}, bf16[2,688,1024]{2,1,0:T(8,128)(2,1)}, u32[]{:S(2)}, u32[]{:S(2)}) collective-permute-start(bf16[2,688,1024]{2,1,0:T(8,128)(2,1)} %get-tuple-element.254), channel_id=1, source_target_pairs={{0,4},{4,0},{8,12},{12,8},{1,5},{5,1},{9,13},{13,9},{2,6},{6,2},{1... | collective-permute-start | bytes 8454152 | tf_op jit(solution)/shard_map/ppermute | solution.py:1167
  614.7 7.4 copy-start.9
  614.8 7.4 copy-start.14
  620.2 14.7 %copy-start.15 = (bf16[2,256,1024]{2,1,0:T(8,128)(2,1)S(1)}, bf16[2,256,1024]{2,1,0:T(8,128)(2,1)}, u32[]{:S(2)}) copy-start(bf16[2,256,1024]{2,1,0:T(8,128)(2,1)} %get-tuple-element.248) | copy-start | bytes 3145732
  620.2 14.7 %collective-permute-start.26 = (bf16[256,1024]{1,0:T(8,128)(2,1)S(1)}, bf16[256,1024]{1,0:T(8,128)(2,1)S(1)}, u32[]{:S(2)}, u32[]{:S(2)}) collective-permute-start(bf16[256,1024]{1,0:T(8,128)(2,1)S(1)} %fusion.7), channel_id=1, source_target_pairs={{0,8},{4,12},{8,0},{12,4},{1,9},{5,13},{9,1},{13,5},{2,10},{6,14},... | collective-permute-start | bytes 1572872 | tf_op jit(solution)/shard_map/ppermute | solution.py:1170
  620.9 47.4 %collective-permute-start.25 = (bf16[3,256,1024]{2,1,0:T(8,128)(2,1)}, bf16[3,256,1024]{2,1,0:T(8,128)(2,1)}, u32[]{:S(2)}, u32[]{:S(2)}) collective-permute-start(bf16[3,256,1024]{2,1,0:T(8,128)(2,1)} %fusion.5), channel_id=1, source_target_pairs={{0,8},{4,12},{8,0},{12,4},{1,9},{5,13},{9,1},{13,5},{2,10},{6,14},... | collective-permute-start | bytes 4718600 | tf_op jit(solution)/shard_map/ppermute | solution.py:1170
  637.0 21.1 %copy-start.22 = (f32[8,1024]{1,0:T(8,128)S(1)}, f32[8,1024]{1,0:T(8,128)}, u32[]{:S(2)}) copy-start(f32[8,1024]{1,0:T(8,128)} %get-tuple-element.233) | copy-start | bytes 98308
  883.5 1.6 copy-start
  885.1 1.2 copy-start.1
  886.3 1.2 copy-start.2
  887.5 1.1 copy-start.3
  888.6 0.9 copy-start.4
  889.6 0.7 copy-start.5
